TPU v7x, 32 devices: a whole 2x2x4 slice. The times are simulated.
32 devices in a mesh: rep: 2 (over x), dp: 16 (over z, y, core).
Axes of the slice: x: 2, y: 2, z: 4, core: 2. Of those that a mesh axis runs over, the one named last changes fastest.
Arguments:
- tokens: bfloat16 [32, 256, 2048], P(('rep', 'dp')), may hold values from -6 to 6
- cotangent: bfloat16 [32, 256, 2048], P(('rep', 'dp')), may hold values from -6 to 6
- branch: int32 [32, 2], P(('rep', 'dp')), may hold values from 32 to 128, as said below
- att_master: float32 [2048, 8192], P('dp')
- att_first: float32 [2, 2048, 8192], P('rep', 'dp')
- att_second: float32 [2, 2048, 8192], P('rep', 'dp')
- att_outer: float32 [2048, 8192], P('dp'), may hold values from -0.3125 to 0.3125
- mlp_master: float32 [2048, 24576], P('dp')
- mlp_first: float32 [2, 2048, 24576], P('rep', 'dp')
- mlp_second: float32 [2, 2048, 24576], P('rep', 'dp')
- mlp_outer: float32 [2048, 24576], P('dp'), may hold values from -0.3125 to 0.3125
Outputs:
- out_tokens: bfloat16 [32, 256, 2048], P(('rep', 'dp'))
- grad_tokens: float32 [32, 256, 2048], P(('rep', 'dp'))
- att_new: float32 [2048, 8192], P('dp')
- att_first_new: float32 [2, 2048, 8192], P('rep', 'dp')
- att_second_new: float32 [2, 2048, 8192], P('rep', 'dp')
- att_mean_diff: float32 [2048, 8192], P('dp')
- att_outer_new: float32 [2048, 8192], P('dp')
- mlp_new: float32 [2048, 24576], P('dp')
- mlp_first_new: float32 [2, 2048, 24576], P('rep', 'dp')
- mlp_second_new: float32 [2, 2048, 24576], P('rep', 'dp')
- mlp_mean_diff: float32 [2048, 24576], P('dp')
- mlp_outer_new: float32 [2048, 24576], P('dp')
Inputs may be any that keep to these rules, and one draw needn't show every extreme that they name: Continuation c of a unit follows the first branch[unit, c] prompt tokens; the value 128 occurs in every draw.
All inputs are finite; a program needn't handle non-finite values.
Results may differ from a plain program's by a relative error of at most 0.015.
Values may be sent and summed in bfloat16 or wider, within the bound.
A program may use at most 960 MiB of HBM per device.

v0:
```python
import functools
import math

import jax
import jax.numpy as jnp
from jax import lax
from jax.experimental import pallas as pl
from jax.experimental.pallas import tpu as pltpu
from jax.sharding import PartitionSpec as P

HEAD_DIM = 128
PROMPT = 128
CLEN = 64
CONT = 2
STEP = 10
TEAM = 8


LN_EPS = 1e-05
BETA_ONE = 0.9
BETA_TWO = 0.95
ADAM_EPS = 1e-08
DECAY = 0.1
RATE = 0.05
OUTER_RATE = 0.7
OUTER_MOMENTUM = 0.9
CONTRACT_LAST = (((1,), (1,)), ((), ()))
CONTRACT_FIRST = (((0,), (0,)), ((), ()))
LOW = jnp.bfloat16
FULL = jnp.float32


def normalize(values):
    centre = values - jnp.mean(values, axis=-1, keepdims=True)
    factor = lax.rsqrt(jnp.mean(centre * centre, axis=-1, keepdims=True) + LN_EPS)
    return (centre * factor, factor)


def normalize_back(values, gradient):
    normed, factor = normalize(values)
    projection = jnp.mean(gradient * normed, axis=-1, keepdims=True)
    return factor * (gradient - jnp.mean(gradient, axis=-1, keepdims=True) - normed * projection)


def token_layout(seen, length):
    places = jnp.arange(length, dtype=jnp.int32)
    segment = jnp.where(places < PROMPT, -1, (places - PROMPT) // CLEN)
    within = jnp.where(places < PROMPT, places, (places - PROMPT) % CLEN)
    lookup = jnp.arange(CONT, dtype=jnp.int32)
    reach = jnp.sum(jnp.where(segment[:, None] == lookup[None, :], seen[None, :], 0), axis=1)
    position = jnp.where(segment < 0, places, reach + within)
    allowed = (segment[:, None] == segment[None, :]) & (within[None, :] <= within[:, None]) | (
        segment[None, :] < 0
    ) & (segment[:, None] >= 0) & (places[None, :] < reach[:, None])
    return (position, allowed)


def rotary_tables(position, depth):
    half_depth = depth // 2
    freqs = jnp.exp(jnp.arange(half_depth, dtype=jnp.float32) * (-2.0 * math.log(10000.0) / depth))
    angle = position.astype(jnp.float32)[:, None] * freqs[None, :]
    return (jnp.cos(angle)[:, None, :], jnp.sin(angle)[:, None, :])


def rotate(values, cosine, sine):
    half_depth = values.shape[-1] // 2
    first = values[..., :half_depth]
    second = values[..., half_depth:]
    return jnp.concatenate(
        [first * cosine - second * sine, second * cosine + first * sine], axis=-1
    )


def rotate_back(gradient, cosine, sine):
    half_depth = gradient.shape[-1] // 2
    first = gradient[..., :half_depth]
    second = gradient[..., half_depth:]
    return jnp.concatenate(
        [first * cosine + second * sine, second * cosine - first * sine], axis=-1
    )


def adam_step(master, gradient, first, second):
    first_new = BETA_ONE * first + (1.0 - BETA_ONE) * gradient
    second_new = BETA_TWO * second + (1.0 - BETA_TWO) * gradient * gradient
    ratio = (
        first_new
        / (1.0 - BETA_ONE**STEP)
        / (jnp.sqrt(second_new / (1.0 - BETA_TWO**STEP)) + ADAM_EPS)
    )
    return (master - RATE * (ratio + DECAY * master), first_new, second_new)


def outer_step(master, mean_diff, momentum):
    momentum_new = OUTER_MOMENTUM * momentum + mean_diff
    return (master - OUTER_RATE * (mean_diff + OUTER_MOMENTUM * momentum_new), momentum_new)


def dot(left, right, dims=(((1,), (0,)), ((), ()))):
    return lax.dot_general(left, right, dims, preferred_element_type=FULL)


MESH = pl.DeviceIdType.MESH
ANYWHERE = pl.BlockSpec(memory_space=pl.ANY)
BITS = (1, 2, 4)
PIECES = 4
STRIP = 16
GATHER_COPIES = 6 * PIECES + 1
VMEM_BYTES = 56 * 1024 * 1024


def flip(me, bit):
    return me + bit - 2 * bit * ((me // bit) % 2)


def across(me, other):
    bit = 1
    while bit <= other:
        if other & bit:
            me = flip(me, bit)
        bit *= 2
    return me


def greet(me, others, with_rep):
    barrier = pltpu.get_barrier_semaphore()
    for other in others:
        pl.semaphore_signal(
            barrier, inc=1, device_id={"dp": across(me, other)}, device_id_type=MESH
        )
    if with_rep:
        rep = lax.axis_index("rep")
        pl.semaphore_signal(barrier, inc=1, device_id={"rep": 1 - rep}, device_id_type=MESH)
    pl.semaphore_wait(barrier, len(others) + (1 if with_rep else 0))


class Sender:
    def __init__(self, sent, came):
        self.sent, self.came, self.index = sent, came, 0

    def __call__(self, source, target, where):
        copy = pltpu.make_async_remote_copy(
            src_ref=source,
            dst_ref=target,
            send_sem=self.sent.at[self.index],
            recv_sem=self.came.at[self.index],
            device_id=where,
            device_id_type=MESH,
        )
        copy.start()
        self.index += 1
        return copy


class TeamGather:
    def __init__(self, me, own, out, send):
        self.out, self.send = out, send
        self.piece = own.shape[0] // PIECES
        self.core, self.second, self.third = ({"dp": flip(me, bit)} for bit in BITS)
        self.late = list(range(PIECES // 2, PIECES)) + list(range(PIECES // 2))
        self.early = list(range(PIECES))
        self.own = own
        self.over_second, self.over_third, self.rest = {}, {}, []

    def cut(self, ref, p):
        return ref.at[pl.ds(p * self.piece, self.piece)]

    def begin(self):
        own, out, cut = self.own, self.out, self.cut
        for a, b in zip(self.late, self.early):
            self.over_second[a] = self.send(cut(own, a), cut(out.at[2], a), self.second)
            self.over_third[b] = self.send(cut(own, b), cut(out.at[4], b), self.third)
        self.rest.append(self.send(own, out.at[1], self.core))

    def finish(self):
        out, cut, send = self.out, self.cut, self.send
        half = PIECES // 2
        corner = {}
        for a, b in zip(self.late, self.early):
            self.over_second[a].wait_recv()
            if a >= half:
                corner[a] = send(cut(out.at[2], a), cut(out.at[6], a), self.third)
            self.rest.append(send(cut(out.at[2], a), cut(out.at[3], a), self.core))
            self.over_third[b].wait_recv()
            if b < half:
                corner[b] = send(cut(out.at[4], b), cut(out.at[6], b), self.second)
            self.rest.append(send(cut(out.at[4], b), cut(out.at[5], b), self.core))
        for p in range(half):
            for q in (p, p + half):
                corner[q].wait_recv()
                self.rest.append(send(cut(out.at[6], q), cut(out.at[7], q), self.core))
        for group in (self.over_second, self.over_third, corner):
            for copy in group.values():
                copy.wait_send()
        for copy in self.rest:
            copy.wait()


SUM_COPIES = 6


def sum_scratch(count, width):
    return [
        pltpu.VMEM((4, count, width), LOW),
        pltpu.VMEM((4, count, width), LOW),
        pltpu.VMEM((3, count, width), LOW),
        pltpu.SemaphoreType.DMA((SUM_COPIES + 4,)),
        pltpu.SemaphoreType.DMA((SUM_COPIES + 4,)),
        pltpu.SemaphoreType.DMA((4,)),
    ]


def team_sum(me, parts, own, got, edge, sent, came, loads, total):
    send = Sender(sent, came)
    core = {"dp": flip(me, 1)}
    loading = [pltpu.make_async_copy(parts.at[2 * j], own.at[j], loads.at[j]) for j in range(4)]
    first = {}
    for j in (3, 2, 1, 0):
        loading[j].start()
        first[j] = send(parts.at[2 * j + 1], got.at[j], core)
    for copy in loading:
        copy.wait()
    sum_steps(me, own, got, edge, first, send, total, lambda: None)


def sum_steps(me, own, got, edge, first, send, total, between):
    count = own.shape[1]
    half = count // 2
    _, second, third = ({"dp": flip(me, bit)} for bit in BITS)

    def cut(ref, h):
        return ref.at[pl.ds(h * half, half)]

    def add(j, h, extra=None):
        @pl.loop(0, half // STRIP)
        def _(step):
            at = pl.ds(h * half + step * STRIP, STRIP)
            value = own[j, at].astype(FULL) + got[j, at].astype(FULL)
            if extra is not None:
                value = value + extra[at].astype(FULL)
            own[j, at] = value.astype(LOW)

    first[3].wait_recv()
    add(3, 0)
    corner_second = send(cut(own.at[3], 0), cut(edge.at[0], 0), second)
    add(3, 1)
    corner_third = send(cut(own.at[3], 1), cut(edge.at[0], 1), third)
    first[2].wait_recv()
    add(2, 1)
    third_late = send(cut(own.at[2], 1), cut(edge.at[2], 1), third)
    first[1].wait_recv()
    add(1, 0)
    second_early = send(cut(own.at[1], 0), cut(edge.at[1], 0), second)
    between()
    corner_second.wait_recv()
    add(2, 0, edge.at[0])
    third_early = send(cut(own.at[2], 0), cut(edge.at[2], 0), third)
    corner_third.wait_recv()
    add(1, 1, edge.at[0])
    second_late = send(cut(own.at[1], 1), cut(edge.at[1], 1), second)
    first[0].wait_recv()
    for h, waits in ((0, (second_early, third_early)), (1, (third_late, second_late))):
        for copy in waits:
            copy.wait_recv()

        @pl.loop(0, half // STRIP)
        def _(step, h=h):
            start = h * half + step * STRIP
            at = pl.ds(start, STRIP)
            value = own[0, at].astype(FULL) + got[0, at].astype(FULL)
            total(start, value + edge[1, at].astype(FULL) + edge[2, at].astype(FULL))

    for copy in (
        corner_second, corner_third, third_late, second_early, third_early, second_late
    ):
        copy.wait_send()
    for j in range(4):
        first[j].wait_send()


def params(collective_id):
    return pltpu.CompilerParams(
        collective_id=collective_id, has_side_effects=True, vmem_limit_bytes=VMEM_BYTES
    )


def strip_normalize(value):
    width = value.shape[1]
    centre = value - jnp.sum(value, axis=1, keepdims=True) * (1.0 / width)
    factor = lax.rsqrt(jnp.sum(centre * centre, axis=1, keepdims=True) * (1.0 / width) + LN_EPS)
    return (centre * factor, factor)


class RowGather:
    def __init__(self, ranks, me, rep, weights, send, send_x, local):
        self.me, self.rep, self.weights, self.local = me, rep, weights, local
        self.send, self.send_x = send, send_x
        self.rows = weights.shape[0] // ranks
        self.half = self.rows // 2
        self.order = list(range(TEAM, ranks)) + list(range(1, TEAM))

    def place(self, device):
        return self.weights.at[pl.ds(device * self.rows + self.rep * self.half, self.half)]

    def begin(self, pack):
        me, rep = self.me, self.rep
        at = self.weights.at[pl.ds(me * self.rows, self.rows)]
        self.own = pltpu.make_async_copy(pack.at[me % TEAM], at, self.local)
        self.own.start()
        self.ways = []
        for other in self.order:
            where = across(me, other)
            source = pack.at[where % TEAM, pl.ds(rep * self.half, self.half)]
            self.ways.append(self.send(source, self.place(me), {"dp": where}))

    def forward(self):
        self.swaps = []
        for other, copy in zip(self.order, self.ways):
            copy.wait_recv()
            at = self.place(across(self.me, other))
            self.swaps.append(self.send_x(at, at, {"rep": 1 - self.rep}))

    def finish(self):
        for copy in self.ways:
            copy.wait_send()
        for copy in self.swaps + [self.own]:
            copy.wait()


def attend_unit(values, cosine, sine, bias, share):
    depth = HEAD_DIM
    parts = []
    for p in range(2):
        turned = []
        for at in range(p * share, (p + 1) * share, depth):
            head = values[:, at : at + depth]
            turned.append((head * cosine + pltpu.roll(head, depth // 2, 1) * sine).astype(LOW))
        parts.append(turned)
    query, keys = parts
    value = [
        values[:, at : at + depth].astype(LOW) for at in range(2 * share, 3 * share, depth)
    ]
    mixed = []
    for one, two, three in zip(query, keys, value):
        scores = dot(one, two, CONTRACT_LAST) * depth ** (-0.5) + bias
        powers = jnp.exp(scores - jnp.max(scores, axis=1, keepdims=True))
        prob = powers / jnp.sum(powers, axis=1, keepdims=True)
        mixed.append(dot(prob.astype(LOW), three).astype(LOW))
    return jnp.concatenate(query + keys + value, axis=1), jnp.concatenate(mixed, axis=1)


def forward_kernel(
    ranks,
    flat,
    normed_own,
    cot,
    att_pack,
    mlp_master,
    cosine,
    sine,
    bias,
    normed_all,
    cot_all,
    att_weights,
    gate_weights,
    down_weights,
    gate_pack,
    down_pack,
    projected_all,
    mixed_all,
    resid,
    normed_two_all,
    gate_all,
    up_all,
    hidden_all,
    att,
    gate,
    block,
    odd,
    own,
    got,
    edge,
    normed,
    *sems,
):
    sent_team, came_team, sent_rows, came_rows, sent_x, came_x, first_sent, first_came, local = sems
    me = lax.axis_index("dp")
    rep = lax.axis_index("rep")
    rows, share = att_pack.shape[1], att_pack.shape[2] // 4
    hid = gate_pack.shape[2] // 2
    core = {"dp": flip(me, 1)}
    greet(me, range(1, ranks), True)
    send = Sender(sent_team, came_team)
    send_rows = Sender(sent_rows, came_rows)
    send_x = Sender(sent_x, came_x)
    tokens = TeamGather(me, normed_own, normed_all, send)
    tokens.begin()
    gathers = [
        RowGather(ranks, me, rep, weights, send_rows, send_x, local.at[i])
        for i, weights in enumerate((att_weights, gate_weights, down_weights))
    ]
    gathers[0].begin(att_pack)
    keep = [pltpu.make_async_copy(normed_own, normed_all.at[0], local.at[3])]
    keep.append(pltpu.make_async_copy(cot, cot_all.at[0], local.at[4]))
    for copy in keep:
        copy.start()

    def pack(wide, low):
        def loads(t, slot):
            return [
                pltpu.make_async_copy(
                    mlp_master.at[:, pl.ds((p * TEAM + t) * hid, hid)],
                    wide.at[slot, p],
                    local.at[5 + 3 * slot + p],
                )
                for p in range(3)
            ]

        for copy in loads(0, 0):
            copy.start()

        @pl.loop(0, TEAM)
        def _(t):
            slot = t % 2

            @pl.when(t + 1 < TEAM)
            def _():
                for copy in loads(t + 1, 1 - slot):
                    copy.start()

            for copy in loads(t, slot):
                copy.wait()
            low[:, : 2 * hid] = jnp.concatenate(
                [wide[slot, 0].astype(LOW), wide[slot, 1].astype(LOW)], axis=1
            )
            low[:, 2 * hid :] = wide[slot, 2].astype(LOW)
            out_copies = [
                pltpu.make_async_copy(low.at[:, pl.ds(0, 2 * hid)], gate_pack.at[t], local.at[11]),
                pltpu.make_async_copy(low.at[:, pl.ds(2 * hid, hid)], down_pack.at[t], local.at[12]),
            ]
            for copy in out_copies:
                copy.start()
            for copy in out_copies:
                copy.wait()

    pl.run_scoped(
        pack, pltpu.VMEM((2, 3, rows, hid), FULL), pltpu.VMEM((rows, 3 * hid), LOW)
    )
    tokens.finish()
    gathers[1].begin(gate_pack)
    gathers[0].forward()
    gathers[0].finish()
    for copy in keep:
        copy.wait()
    load = pltpu.make_async_copy(att_weights, att, local.at[0])
    load.start()
    load.wait()

    def unit_of(step):
        return 2 * (TEAM // 2 - 1 - step % (TEAM // 2)) + jnp.where(step < TEAM // 2, 1, 0)

    def fetch(step, slot):
        return pltpu.make_async_copy(
            normed_all.at[unit_of(step)], block.at[slot], local.at[5 + slot]
        )

    fetch(0, 0).start()

    @pl.loop(0, TEAM)
    def _(step):
        slot = step % 2
        unit = unit_of(step)

        @pl.when(step + 1 < TEAM)
        def _():
            fetch(step + 1, 1 - slot).start()

        fetch(step, slot).wait()
        values = dot(block[slot], att[:, : 3 * share])
        projected, mixed = attend_unit(values, cosine[unit], sine[unit], bias[unit], share)
        projected_all[unit] = projected
        mixed_all[unit] = mixed
        term = dot(mixed, att[:, 3 * share :], CONTRACT_LAST).astype(LOW)
        j = unit // 2

        @pl.when(step < TEAM // 2)
        def _():
            odd[j] = term
            pltpu.make_async_remote_copy(
                src_ref=odd.at[j],
                dst_ref=got.at[j],
                send_sem=first_sent.at[j],
                recv_sem=first_came.at[j],
                device_id=core,
                device_id_type=MESH,
            ).start()

        @pl.when(step >= TEAM // 2)
        def _():
            own[j] = term

    first = [
        pltpu.make_async_remote_copy(
            src_ref=odd.at[j],
            dst_ref=got.at[j],
            send_sem=first_sent.at[j],
            recv_sem=first_came.at[j],
            device_id=core,
            device_id_type=MESH,
        )
        for j in range(TEAM // 2)
    ]

    def total(start, value):
        at = pl.ds(start, STRIP)
        value = value + flat[at].astype(FULL)
        resid[at] = value
        normed[at] = strip_normalize(value)[0].astype(LOW)

    sum_steps(me, own, got, edge, first, send, total, gathers[1].forward)
    tokens = TeamGather(me, normed, normed_two_all, send)
    tokens.begin()
    keep = pltpu.make_async_copy(normed, normed_two_all.at[0], local.at[3])
    keep.start()
    tokens.finish()
    cots = TeamGather(me, cot, cot_all, send)
    cots.begin()
    gathers[2].begin(down_pack)
    keep.wait()
    gathers[1].finish()
    load = pltpu.make_async_copy(gate_weights, gate, local.at[1])
    load.start()
    load.wait()

    def feed(low):
        def fetch(unit, slot):
            return pltpu.make_async_copy(
                normed_two_all.at[unit], block.at[slot], local.at[5 + slot]
            )

        def stores(unit, slot):
            return [
                pltpu.make_async_copy(low.at[slot, i], out.at[unit], local.at[7 + 3 * slot + i])
                for i, out in enumerate((gate_all, up_all, hidden_all))
            ]

        fetch(0, 0).start()

        @pl.loop(0, TEAM)
        def _(unit):
            slot = unit % 2

            @pl.when(unit + 1 < TEAM)
            def _():
                fetch(unit + 1, 1 - slot).start()

            fetch(unit, slot).wait()

            @pl.when(unit >= 2)
            def _():
                for copy in stores(unit - 2, slot):
                    copy.wait()

            tile = 256

            @pl.loop(0, hid // tile)
            def _(column):
                at = pl.ds(pl.multiple_of(column * tile, tile), tile)
                later = pl.ds(pl.multiple_of(hid + column * tile, tile), tile)
                gate_value = dot(block[slot], gate[:, at])
                up_value = dot(block[slot], gate[:, later])
                low[slot, 0, :, at] = gate_value.astype(LOW)
                low[slot, 1, :, at] = up_value.astype(LOW)
                hidden = gate_value * jax.nn.sigmoid(gate_value) * up_value
                low[slot, 2, :, at] = hidden.astype(LOW)

            for copy in stores(unit, slot):
                copy.start()

        for unit in (TEAM - 2, TEAM - 1):
            for copy in stores(unit, unit % 2):
                copy.wait()

    pl.run_scoped(feed, pltpu.VMEM((2, 3, normed.shape[0], hid), LOW))
    cots.finish()
    gathers[2].forward()
    gathers[2].finish()


def forward_layer(ranks, flat, normed, cot, att_pack, mlp_master, cosine, sine, bias):
    count, width = normed.shape
    rows, share = att_pack.shape[1], att_pack.shape[2] // 4
    hid = mlp_master.shape[1] // (3 * TEAM)
    gathered = jax.ShapeDtypeStruct((TEAM, count, width), LOW)
    hidden = jax.ShapeDtypeStruct((TEAM, count, hid), LOW)
    vmem = pl.BlockSpec(memory_space=pltpu.VMEM)

    def weights(columns):
        return jax.ShapeDtypeStruct((ranks * rows, columns), LOW)

    def packs(columns):
        return jax.ShapeDtypeStruct((TEAM, rows, columns), LOW)

    out = [
        (gathered, ANYWHERE),
        (gathered, ANYWHERE),
        (weights(4 * share), ANYWHERE),
        (weights(2 * hid), ANYWHERE),
        (weights(hid), ANYWHERE),
        (packs(2 * hid), ANYWHERE),
        (packs(hid), ANYWHERE),
        (jax.ShapeDtypeStruct((TEAM, count, 3 * share), LOW), vmem),
        (jax.ShapeDtypeStruct((TEAM, count, share), LOW), vmem),
        (jax.ShapeDtypeStruct((count, width), FULL), vmem),
        (gathered, ANYWHERE),
        (hidden, ANYWHERE),
        (hidden, ANYWHERE),
        (hidden, ANYWHERE),
    ]
    team_copies = 3 * GATHER_COPIES + SUM_COPIES
    pairs = [team_copies] * 2 + [3 * (ranks - 1)] * 4 + [TEAM // 2] * 2 + [13]
    return pl.pallas_call(
        functools.partial(forward_kernel, ranks),
        out_shape=[shape for shape, _ in out],
        in_specs=[vmem] + [ANYWHERE] * 4 + [vmem] * 3,
        out_specs=[spec for _, spec in out],
        scratch_shapes=[
            pltpu.VMEM((ranks * rows, 4 * share), LOW),
            pltpu.VMEM((ranks * rows, 2 * hid), LOW),
            pltpu.VMEM((2, count, width), LOW),
            pltpu.VMEM((TEAM // 2, count, width), LOW),
            pltpu.VMEM((TEAM // 2, count, width), LOW),
            pltpu.VMEM((TEAM // 2, count, width), LOW),
            pltpu.VMEM((3, count, width), LOW),
            pltpu.VMEM((count, width), LOW),
        ]
        + [pltpu.SemaphoreType.DMA((number,)) for number in pairs],
        compiler_params=params(0),
        name="forward_layer",
    )(flat, normed, cot, att_pack, mlp_master, cosine, sine, bias)


def back_kernel(parts, resid, cot, grad_resid, grad_all, grad_low, *refs):
    sum_refs, (sent, came, local) = refs[:6], refs[6:]
    me = lax.axis_index("dp")
    greet(me, BITS, False)

    def total(start, value):
        at = pl.ds(start, STRIP)
        width = value.shape[1]
        normed, factor = strip_normalize(resid[at])
        along = jnp.sum(value * normed, axis=1, keepdims=True) * (1.0 / width)
        middle = jnp.sum(value, axis=1, keepdims=True) * (1.0 / width)
        value = cot[at].astype(FULL) + factor * (value - middle - normed * along)
        grad_resid[at] = value
        grad_low[at] = value.astype(LOW)

    team_sum(me, parts, *sum_refs, total)
    gather = TeamGather(me, grad_low, grad_all, Sender(sent, came))
    gather.begin()
    keep = pltpu.make_async_copy(grad_low, grad_all.at[0], local)
    keep.start()
    gather.finish()
    keep.wait()


def back_layer(parts, resid, cot):
    team, count, width = parts.shape
    vmem = pl.BlockSpec(memory_space=pltpu.VMEM)
    return pl.pallas_call(
        back_kernel,
        out_shape=[
            jax.ShapeDtypeStruct((count, width), FULL),
            jax.ShapeDtypeStruct((team, count, width), LOW),
        ],
        in_specs=[ANYWHERE, vmem, vmem],
        out_specs=[vmem, ANYWHERE],
        scratch_shapes=[pltpu.VMEM((count, width), LOW)]
        + sum_scratch(count, width)
        + [pltpu.SemaphoreType.DMA((GATHER_COPIES,))] * 2
        + [pltpu.SemaphoreType.DMA],
        compiler_params=params(2),
        name="back_layer",
    )(parts, resid, cot)


def sum_kernel(parts, out, *refs):
    me = lax.axis_index("dp")
    greet(me, BITS, False)

    def total(start, value):
        out[pl.ds(start, STRIP)] = value

    team_sum(me, parts, *refs, total)


def sum_layer(parts, collective_id):
    team, count, width = parts.shape
    return pl.pallas_call(
        sum_kernel,
        out_shape=jax.ShapeDtypeStruct((count, width), FULL),
        in_specs=[ANYWHERE],
        out_specs=pl.BlockSpec(memory_space=pltpu.VMEM),
        scratch_shapes=sum_scratch(count, width),
        compiler_params=params(collective_id),
        name="sum_layer",
    )(parts)


def trade_kernel(blocks, out, sent, came, local):
    me = lax.axis_index("dp")
    greet(me, range(1, TEAM), False)
    send = Sender(sent, came)
    keep = pltpu.make_async_copy(blocks.at[me % TEAM], out.at[me % TEAM], local)
    keep.start()
    copies = []
    for other in (7, 6, 5, 4, 3, 2, 1):
        where = across(me, other)
        copies.append(send(blocks.at[where % TEAM], out.at[me % TEAM], {"dp": where}))
    for copy in copies:
        copy.wait()
    keep.wait()


def trade(blocks, collective_id):
    return pl.pallas_call(
        trade_kernel,
        out_shape=jax.ShapeDtypeStruct(blocks.shape, blocks.dtype),
        in_specs=[ANYWHERE],
        out_specs=ANYWHERE,
        scratch_shapes=[pltpu.SemaphoreType.DMA((TEAM - 1,))] * 2 + [pltpu.SemaphoreType.DMA],
        compiler_params=params(collective_id),
        name="trade",
    )(blocks)


def pack_kernel(*refs):
    share = refs[0].shape[1]
    for p, ref in enumerate(refs[:-1]):
        refs[-1][0, :, p * share : (p + 1) * share] = ref[...].astype(LOW)


def pack_shares(master, bases, share):
    rows = master.shape[0]
    return pl.pallas_call(
        pack_kernel,
        grid=(TEAM,),
        out_shape=jax.ShapeDtypeStruct((TEAM, rows, len(bases) * share), LOW),
        in_specs=[
            pl.BlockSpec((rows, share), lambda i, base=base: (0, base + i)) for base in bases
        ],
        out_specs=pl.BlockSpec((1, rows, len(bases) * share), lambda i: (i, 0, 0)),
        name="pack_shares",
    )(*[master] * len(bases))


def adam_kernel(grad, master, first, second, *refs):
    first_new, second_new, diff = refs[-3:]
    gradient = grad[0].astype(FULL)
    inner, first_new[0], second_new[0] = adam_step(master[...], gradient, first[0], second[0])
    diff[...] = (master[...] - inner).astype(LOW)


def adam_chunk(grads, master, first, second, bases, share, written):
    rows = master.shape[0]
    parts = len(bases)

    def column(t, p):
        place = bases[0]
        for q in range(1, parts):
            place = place + jnp.where(p >= q, bases[q] - bases[q - 1], 0)
        return place + t

    wide = pl.BlockSpec((1, rows, share), lambda t, p: (0, 0, column(t, p)))
    flat = pl.BlockSpec((rows, share), lambda t, p: (0, column(t, p)))
    state = jax.ShapeDtypeStruct(first.shape, FULL)
    extra = [] if written is None else list(written)
    return pl.pallas_call(
        adam_kernel,
        grid=(TEAM, parts),
        out_shape=[state, state, jax.ShapeDtypeStruct((rows, TEAM * parts * share), LOW)],
        in_specs=[pl.BlockSpec((1, rows, share), lambda t, p: (t, 0, p)), flat, wide, wide]
        + [ANYWHERE] * len(extra),
        out_specs=[wide, wide, pl.BlockSpec((rows, share), lambda t, p: (0, p * TEAM + t))],
        input_output_aliases={4 + i: i for i in range(len(extra))},
        name="adam_chunk",
    )(grads, master, first, second, *extra)


def outer_kernel(reps, diff, other, master, momentum, *refs):
    mean_out, new, momentum_new = refs[-3:]
    mean = (diff[...].astype(FULL) + other[...].astype(FULL)) / reps
    mean_out[...] = mean
    new[...], momentum_new[...] = outer_step(master[...], mean, momentum[...])


def outer_chunk(reps, diff, other, master, momentum, bases, share, written):
    rows = master.shape[0]
    parts = len(bases)

    def column(t, p):
        place = bases[0]
        for q in range(1, parts):
            place = place + jnp.where(p >= q, bases[q] - bases[q - 1], 0)
        return place + t

    flat = pl.BlockSpec((rows, share), lambda t, p: (0, column(t, p)))
    packed = pl.BlockSpec((rows, share), lambda t, p: (0, p * TEAM + t))
    extra = [] if written is None else list(written)
    return pl.pallas_call(
        functools.partial(outer_kernel, reps),
        grid=(TEAM, parts),
        out_shape=[jax.ShapeDtypeStruct(master.shape, FULL)] * 3,
        in_specs=[packed, packed, flat, flat] + [ANYWHERE] * len(extra),
        out_specs=[flat] * 3,
        input_output_aliases={4 + i: i for i in range(len(extra))},
        name="outer_chunk",
    )(diff, other, master, momentum, *extra)


def on_device(
    reps,
    ranks,
    tokens,
    cotangent,
    branch,
    att_master,
    att_first,
    att_second,
    att_outer,
    mlp_master,
    mlp_first,
    mlp_second,
    mlp_outer,
):
    units, length, width = tokens.shape
    hidden_width = mlp_master.shape[1] // 3
    depth = HEAD_DIM
    count = units * length
    rows = att_master.shape[0]
    team = TEAM
    tops = ranks // team
    all_tokens = team * count
    att_share = width // team
    hid_share = hidden_width // team
    me = lax.axis_index("dp")
    rep = lax.axis_index("rep")
    top = me // team

    def hop(values, other):
        pairs = [(r * ranks + i, r * ranks + (i ^ other)) for r in range(reps) for i in range(ranks)]
        return lax.ppermute(values, ("rep", "dp"), pairs)

    def swap(values):
        pairs = [(r * ranks + i, (1 - r) * ranks + i) for r in range(reps) for i in range(ranks)]
        return lax.ppermute(values, ("rep", "dp"), pairs)

    def combine(grad):
        span = team * rows
        kept = lax.dynamic_slice_in_dim(grad, top * span, span, 0)
        if tops > 1:
            kept = kept.astype(FULL)
        for other in range(1, tops):
            sent = lax.dynamic_slice_in_dim(grad, (top ^ other) * span, span, 0)
            kept = kept + hop(sent, other * team).astype(FULL)
        return kept.astype(LOW).reshape(team, rows, grad.shape[1])

    flat_low = tokens.reshape(count, width)
    flat = flat_low.astype(FULL)
    cot = cotangent.reshape(count, width)
    seen_all = jnp.stack([branch if k == 0 else hop(branch, k) for k in range(team)])
    seen_all = seen_all.reshape(team * units, CONT)
    heads = att_share // depth
    position, allowed = jax.vmap(lambda seen: token_layout(seen, length))(seen_all)
    cosine, sine = jax.vmap(lambda places: rotary_tables(places, depth))(position)
    scale = depth ** (-0.5)
    bias = jnp.where(allowed, 0.0, -1e30).astype(FULL)
    wide_cosine = jnp.concatenate([cosine, cosine], axis=-1).reshape(team, count, depth)
    wide_sine = jnp.concatenate([-sine, sine], axis=-1).reshape(team, count, depth)
    att_pack = pack_shares(att_master, [0, team, 2 * team, 3 * team], att_share)
    (
        normed_one,
        grad_fed,
        att_low,
        gate_low,
        down_low,
        _,
        _,
        projected,
        mixed,
        resid,
        normed_two,
        gate_value,
        up_value,
        hidden,
    ) = forward_layer(
        ranks,
        flat_low,
        normalize(flat)[0].astype(LOW),
        cot,
        att_pack,
        mlp_master,
        wide_cosine,
        wide_sine,
        bias,
    )
    normed_one = normed_one.reshape(all_tokens, width)
    grad_fed = grad_fed.reshape(all_tokens, width)
    mixed = mixed.reshape(all_tokens, att_share)
    normed_two = normed_two.reshape(all_tokens, width)
    gate_value = gate_value.reshape(all_tokens, hid_share).astype(FULL)
    up_value = up_value.reshape(all_tokens, hid_share).astype(FULL)
    hidden = hidden.reshape(all_tokens, hid_share)
    qkv_low, out_low = att_low[:, : 3 * att_share], att_low[:, 3 * att_share :]
    projected = projected.reshape(team * units, length, 3, heads, depth)
    query, keys, values = projected[:, :, 0], projected[:, :, 1], projected[:, :, 2]

    def ein(spec, left, right):
        return jnp.einsum(spec, left, right, preferred_element_type=FULL)

    scores = ein("uqhd,ukhd->uhqk", query, keys) * scale + bias[:, None]
    powers = jnp.exp(scores - jnp.max(scores, axis=-1, keepdims=True))
    prob = powers / jnp.sum(powers, axis=-1, keepdims=True)
    prob_low = prob.astype(LOW)
    sigmoid_gate = jax.nn.sigmoid(gate_value)
    silu_gate = gate_value * sigmoid_gate
    down_grad = combine(dot(grad_fed, hidden, CONTRACT_FIRST).astype(LOW))
    grad_hidden = dot(grad_fed, down_low)
    grad_gate = grad_hidden * up_value * sigmoid_gate * (1.0 + gate_value * (1.0 - sigmoid_gate))
    grad_up = grad_hidden * silu_gate
    grad_gate_up = jnp.concatenate([grad_gate, grad_up], axis=1).astype(LOW)
    gate_grad = combine(dot(normed_two, grad_gate_up, CONTRACT_FIRST).astype(LOW))
    grad_normed_two = dot(grad_gate_up, gate_low, CONTRACT_LAST).astype(LOW)
    grad_resid, grad_attended = back_layer(
        grad_normed_two.reshape(team, count, width), resid, cot
    )
    grad_attended = grad_attended.reshape(all_tokens, width)
    grad_mixed = dot(grad_attended, out_low).astype(LOW)
    out_grad = dot(grad_attended, mixed, CONTRACT_FIRST)
    grad_mixed = grad_mixed.reshape(team * units, length, heads, depth)
    grad_prob = ein("uqhd,ukhd->uhqk", grad_mixed, values)
    grad_values = ein("uhqk,uqhd->ukhd", prob_low, grad_mixed)
    grad_scores = prob * (grad_prob - jnp.sum(grad_prob * prob, axis=-1, keepdims=True))
    grad_scores = grad_scores.astype(LOW)
    grad_query = rotate_back(ein("uhqk,ukhd->uqhd", grad_scores, keys) * scale, cosine, sine)
    grad_keys = rotate_back(ein("uhqk,uqhd->ukhd", grad_scores, query) * scale, cosine, sine)
    grad_projected = jnp.stack([grad_query, grad_keys, grad_values], axis=2).astype(LOW)
    grad_projected = grad_projected.reshape(all_tokens, 3 * att_share)
    qkv_grad = dot(normed_one, grad_projected, CONTRACT_FIRST)
    att_grad = combine(jnp.concatenate([qkv_grad, out_grad], axis=1).astype(LOW))
    grad_normed_one = dot(grad_projected, qkv_low, CONTRACT_LAST).astype(LOW)
    grad_normed_one = sum_layer(grad_normed_one.reshape(team, count, width), 3)
    grad_tokens = (grad_resid + normalize_back(flat, grad_normed_one)).reshape(units, length, width)
    fed = dot(hidden, down_low, CONTRACT_LAST).astype(LOW)
    fed = sum_layer(fed.reshape(team, count, width), 3)
    out_tokens = (resid + fed).astype(LOW).reshape(units, length, width)

    mlp_state, mlp_out = None, None
    for grads, bases in ((down_grad, [2 * team]), (gate_grad, [0, team])):
        *mlp_state, diff = adam_chunk(
            trade(grads, 4 if len(bases) == 1 else 5),
            mlp_master, mlp_first, mlp_second, bases, hid_share, mlp_state,
        )
        mlp_out = outer_chunk(
            reps, diff, swap(diff), mlp_master, mlp_outer, bases, hid_share, mlp_out
        )
    bases = [0, team, 2 * team, 3 * team]
    *att_state, diff = adam_chunk(
        trade(att_grad, 4), att_master, att_first, att_second, bases, att_share, None
    )
    att_out = outer_chunk(reps, diff, swap(diff), att_master, att_outer, bases, att_share, None)
    return (
        out_tokens,
        grad_tokens,
        *(att_out[1], *att_state, att_out[0], att_out[2]),
        *(mlp_out[1], *mlp_state, mlp_out[0], mlp_out[2]),
    )


def solution(mesh):
    in_specs = (
        P(("rep", "dp"), None, None),
        P(("rep", "dp"), None, None),
        P(("rep", "dp"), None),
        P("dp", None),
        P("rep", "dp", None),
        P("rep", "dp", None),
        P("dp", None),
        P("dp", None),
        P("rep", "dp", None),
        P("rep", "dp", None),
        P("dp", None),
    )
    out_specs = (
        P(("rep", "dp"), None, None),
        P(("rep", "dp"), None, None),
        P("dp", None),
        P("rep", "dp", None),
        P("rep", "dp", None),
        P("dp", None),
        P("dp", None),
        P("dp", None),
        P("rep", "dp", None),
        P("rep", "dp", None),
        P("dp", None),
        P("dp", None),
    )

    def body(*args):
        return on_device(mesh.shape["rep"], mesh.shape["dp"], *args)

    return jax.shard_map(
        body, mesh=mesh, in_specs=in_specs, out_specs=out_specs, check_vma=False
    )
```

profile of v0, /device:TPU:0, one launch (start us, length us, event | category | flops | bytes accessed | tf_op | source)
XLA Modules:
  0.0 1304.5 jit_solution(2444660945451780638)
XLA Ops:
  0.6 2.5 collective-permute-start.4
  3.8 1.3 collective-permute-start.2
  6.5 1.4 convert_reduce_fusion
  7.9 1.6 fusion.14
  10.2 2.5 fusion.8.normed_own
  12.7 6.1 pack_shares.1.att_pack
  19.0 2.7 collective-permute-start.6
  23.1 3.1 collective-permute-done.5
  26.5 2.8 multiply_cosine_fusion.1
  29.3 5.5 fusion.31
  35.3 2.0 copy.111
  37.3 2.9 maximum_bitcast_fusion.2.cosine
  40.2 2.5 maximum_bitcast_fusion.3.sine
  42.7 353.3 %forward_layer.1 = (bf16[8,256,2048]{2,1,0:T(8,128)(2,1)}, bf16[8,256,2048]{2,1,0:T(8,128)(2,1)}, bf16[2048,1024]{1,0:T(8,128)(2,1)}, bf16[2048,2048]{1,0:T(8,12...) custom-call(bf16[256,2048]{1,0:T(8,128)(2,1)} %bitcast.95, ...), custom_call_target="tpu_custom_call" | custom-call | tf_op jit(solution)/shard_map/forward_layer/pallas_call | solution.py:622
  396.0 5.7 reshape.349
  401.7 3.3 fusion.40
  405.1 4.7 bitcast_convert_fusion.1
  409.8 9.1 copy.105
  418.9 6.6 bitcast_convert_fusion.2
  425.5 9.1 copy.106
  434.7 21.3 %multiply_convert_fusion.1 = (bf16[2048,1024]{0,1:T(8,128)(2,1)}, bf16[2048,1024]{0,1:T(8,128)(2,1)}) fusion(f32[2048,1024]{0,1:T(8,128)} %copy.106, f32[2048,1024]{0,1:T(8,128)} %copy.105, bf16[2048,2048]{1,0:T(8,128)(2,1)} %bitcast.112, bf16[2048,1024]{1,0:T(8,128)(2,1)} %get-tuple-element.46), kind=kOutput, calls=%fused_computation.5 | convolution fusion | flops 8617197568 | bytes 37748736 | tf_op jit(solution)/shard_map/dot_general | solution.py:100
  456.0 23.9 %convolution_convert_fusion.2 = bf16[2048,2048]{1,0:T(8,128)(2,1)} fusion(bf16[2048,2048]{1,0:T(8,128)(2,1)} %get-tuple-element.50, bf16[2048,1024]{0,1:T(8,128)(2,1)} %get-tuple-element.79, bf16[2048,1024]{0,1:T(8,128)(2,1)} %get-tuple-element.78), kind=kOutput, calls=%fused_computation.9 | convolution fusion | flops 17200840704 | bytes 25165824 | tf_op jit(solution)/shard_map/dot_general | solution.py:100
  479.8 87.0 %back_layer.1 = (f32[256,2048]{1,0:T(8,128)}, bf16[8,256,2048]{2,1,0:T(8,128)(2,1)}) custom-call(bf16[8,256,2048]{2,1,0:T(8,128)(2,1)} %bitcast.101, f32[256,2048]{1,0:T(8,128)} %get-tuple-element.44.resid, bf16[256,2048]{1,0:T(8,128)(2,1)} %bitcast.104), custom_call_target="tpu_custom_call" | custom-call | tf_op jit(solution)/shard_map/back_layer/pallas_call | solution.py:670
  566.8 6.9 convolution_convert_fusion.5
  573.8 1.5 reshape.351
  575.3 1.9 copy.118
  577.9 0.9 copy-done.5
  578.8 2.0 fusion.41
  584.5 1.2 copy-done.24
  585.6 10.0 bitcast_convert_fusion
  595.6 2.0 copy-done.11
  597.6 1.5 constant_dynamic-slice_fusion.1
  599.6 23.8 %convolution_convert_fusion = bf16[2048,2048]{1,0:T(8,128)(2,1)} fusion(bf16[2048,2048]{1,0:T(8,128)(2,1)} %bitcast.111, bf16[2048,1024]{0,1:T(8,128)(2,1)} %get-tuple-element.79, bf16[2048,1024]{0,1:T(8,128)(2,1)} %get-tuple-element.78), kind=kOutput, calls=%fused_computation.7 | convolution fusion | flops 17200840704 | bytes 25165824 | tf_op jit(solution)/shard_map/dot_general | solution.py:100
  623.4 4.9 constant_dynamic-slice_fusion
  628.3 2.5 collective-permute-start.9
  632.6 1.2 slice-done.4
  633.7 1.3 slice-done.5
  635.3 2.4 fusion.3
  638.0 1.9 copy.120
  639.9 1.1 copy.134
  641.5 6.8 convolution_convert_fusion.4
  648.4 1.6 fusion.15
  650.4 177.3 %collective-permute-done.10 = bf16[1024,1024]{1,0:T(8,128)(2,1)S(1)} collective-permute-done((bf16[1024,1024]{1,0:T(8,128)(2,1)}, bf16[1024,1024]{1,0:T(8,128)(2,1)S(1)}, u32[]{:S(2)}, u32[]{:S(2)}) %collective-permute-start.10) | collective-permute-done | bytes 2097184 | tf_op jit(solution)/shard_map/ppermute | solution.py:852
  827.7 2.3 add_convert_fusion.1
  830.0 155.2 %trade.5.grad = bf16[8,128,1024]{2,1,0:T(8,128)(2,1)} custom-call(bf16[8,128,1024]{2,1,0:T(8,128)(2,1)} %bitcast.100), custom_call_target="tpu_custom_call" | custom-call | tf_op jit(solution)/shard_map/trade/pallas_call | solution.py:726
  985.2 11.7 adam_chunk.4
  996.9 7.8 add_convert_fusion
  1004.7 48.7 %trade.4.grad = bf16[8,128,2048]{2,1,0:T(8,128)(2,1)} custom-call(bf16[8,128,2048]{2,1,0:T(8,128)(2,1)} %bitcast.96), custom_call_target="tpu_custom_call" | custom-call | tf_op jit(solution)/shard_map/trade/pallas_call | solution.py:726
  1053.3 22.2 %adam_chunk.5 = (f32[1,128,24576]{2,1,0:T(8,128)}, f32[1,128,24576]{2,1,0:T(8,128)}, bf16[128,16384]{1,0:T(8,128)(2,1)}) custom-call(bf16[8,128,2048]{2,1,0:T(8,128)(2,1)} %trade.4.grad, f32[128,24576]{1,0:T(8,128)} %master.11, f32[1,128,24576]{2,1,0:T(8,128)} %first.5, f32[1,128,24576]{2,1,0:T(8,128)} %second.5, ...), custom_call_target="tpu_custom_call", output_to_operand_aliasing={{0}: (4, {}), {1}: (5, {})} | custom-call | tf_op jit(solution)/shard_map/adam_chunk/pallas_call | solution.py:778
  1075.5 14.1 %convolution_convert_fusion.3 = bf16[2048,2048]{1,0:T(8,128)(2,1)} fusion(bf16[2048,1024]{1,0:T(8,128)(2,1)} %bitcast.118, bf16[2048,1024]{1,0:T(8,128)(2,1)} %get-tuple-element.46), kind=kOutput, calls=%fused_computation.10 | convolution fusion | flops 8594128896 | bytes 16777216 | tf_op jit(solution)/shard_map/dot_general | solution.py:100
  1089.6 3.9 add_convert_fusion.2
  1093.5 3.9 copy.122
  1097.4 26.7 %trade.3.grad = bf16[8,128,1024]{2,1,0:T(8,128)(2,1)} custom-call(bf16[8,128,1024]{2,1,0:T(8,128)(2,1)} %bitcast.102), custom_call_target="tpu_custom_call" | custom-call | tf_op jit(solution)/shard_map/trade/pallas_call | solution.py:726
  1124.2 21.6 %adam_chunk.3 = (f32[1,128,8192]{2,1,0:T(8,128)}, f32[1,128,8192]{2,1,0:T(8,128)}, bf16[128,8192]{1,0:T(8,128)(2,1)}) custom-call(bf16[8,128,1024]{2,1,0:T(8,128)(2,1)} %trade.3.grad, f32[128,8192]{1,0:T(8,128)} %master.7, f32[1,128,8192]{2,1,0:T(8,128)} %first.3, f32[1,128,8192]{2,1,0:T(8,128)} %second.3), custom_call_target="tpu_custom_call" | custom-call | tf_op jit(solution)/shard_map/adam_chunk/pallas_call | solution.py:778
  1145.8 2.0 collective-permute-start.8
  1147.9 11.1 convolution_convert_fusion.1
  1159.0 41.9 %sum_layer.2 = f32[256,2048]{1,0:T(8,128)} custom-call(bf16[8,256,2048]{2,1,0:T(8,128)(2,1)} %bitcast.98), custom_call_target="tpu_custom_call" | custom-call | tf_op jit(solution)/shard_map/sum_layer/pallas_call | solution.py:699
  1201.0 42.0 %sum_layer.3 = f32[256,2048]{1,0:T(8,128)} custom-call(bf16[8,256,2048]{2,1,0:T(8,128)(2,1)} %bitcast.99), custom_call_target="tpu_custom_call" | custom-call | tf_op jit(solution)/shard_map/sum_layer/pallas_call | solution.py:699
  1243.1 2.3 fusion.39
  1245.4 1.2 fusion.27
  1246.6 2.0 fusion.13
  1248.6 21.1 %outer_chunk.3 = (f32[128,8192]{1,0:T(8,128)}, f32[128,8192]{1,0:T(8,128)}, f32[128,8192]{1,0:T(8,128)}) custom-call(bf16[128,8192]{1,0:T(8,128)(2,1)} %get-tuple-element.57.diff, bf16[128,8192]{1,0:T(8,128)(2,1)} %collective-permute-done.8.other, f32[128,8192]{1,0:T(8,128)} %master.7, f32[128,8192]{1,0:T(8,128)} %momentum.3), custom_call_target="tpu_custom_call" | custom-call | tf_op jit(solution)/shard_map/outer_chunk/pallas_call | solution.py:810
  1269.7 11.6 outer_chunk.4
  1281.3 22.7 %outer_chunk.5 = (f32[128,24576]{1,0:T(8,128)}, f32[128,24576]{1,0:T(8,128)}, f32[128,24576]{1,0:T(8,128)}) custom-call(bf16[128,16384]{1,0:T(8,128)(2,1)} %get-tuple-element.66.diff, bf16[128,16384]{1,0:T(8,128)(2,1)} %collective-permute-done.11.other, f32[128,24576]{1,0:T(8,128)} %master.11, ...), custom_call_target="tpu_custom_call", output_to_operand_aliasing={{0}: (4, {}), {1}: (5, {}), {2}: (6, {})} | custom-call | tf_op jit(solution)/shard_map/outer_chunk/pallas_call | solution.py:810
  (115 shorter events, 12.9 us)
Async XLA Ops:
  0.6 18.3 %collective-permute-start.4 = (s32[1,2]{1,0:T(1,128)}, s32[1,2]{1,0:T(1,128)S(1)}, u32[]{:S(2)}, u32[]{:S(2)}) collective-permute-start(s32[1,2]{1,0:T(1,128)} %param.13), channel_id=1, source_target_pairs={{0,5},{1,4},{2,7},{3,6},{4,1},{5,0},{6,3},{7,2},{8,13},{9,12},{10,... | collective-permute-start | bytes 32 | tf_op jit(solution)/shard_map/ppermute | solution.py:852
  3.2 18.6 %collective-permute-start.3 = (s32[1,2]{1,0:T(1,128)}, s32[1,2]{1,0:T(1,128)S(1)}, u32[]{:S(2)}, u32[]{:S(2)}) collective-permute-start(s32[1,2]{1,0:T(1,128)} %param.13), channel_id=1, source_target_pairs={{0,4},{1,5},{2,6},{3,7},{4,0},{5,1},{6,2},{7,3},{8,12},{9,13},{10,... | collective-permute-start | bytes 32 | tf_op jit(solution)/shard_map/ppermute | solution.py:852
  3.8 18.3 %collective-permute-start.2 = (s32[1,2]{1,0:T(1,128)}, s32[1,2]{1,0:T(1,128)S(1)}, u32[]{:S(2)}, u32[]{:S(2)}) collective-permute-start(s32[1,2]{1,0:T(1,128)} %param.13), channel_id=1, source_target_pairs={{0,3},{1,2},{2,1},{3,0},{4,7},{5,6},{6,5},{7,4},{8,11},{9,10},{10,... | collective-permute-start | bytes 32 | tf_op jit(solution)/shard_map/ppermute | solution.py:852
  5.1 17.0 %collective-permute-start.1 = (s32[1,2]{1,0:T(1,128)}, s32[1,2]{1,0:T(1,128)S(1)}, u32[]{:S(2)}, u32[]{:S(2)}) collective-permute-start(s32[1,2]{1,0:T(1,128)} %param.13), channel_id=1, source_target_pairs={{0,2},{1,3},{2,0},{3,1},{4,6},{5,7},{6,4},{7,5},{8,10},{9,11},{10,... | collective-permute-start | bytes 32 | tf_op jit(solution)/shard_map/ppermute | solution.py:852
  5.5 16.8 %collective-permute-start = (s32[1,2]{1,0:T(1,128)}, s32[1,2]{1,0:T(1,128)S(1)}, u32[]{:S(2)}, u32[]{:S(2)}) collective-permute-start(s32[1,2]{1,0:T(1,128)} %param.13), channel_id=1, source_target_pairs={{0,1},{1,0},{2,3},{3,2},{4,5},{5,4},{6,7},{7,6},{8,9},{9,8},{10,11... | collective-permute-start | bytes 32 | tf_op jit(solution)/shard_map/ppermute | solution.py:852
  7.9 1.8 copy-start.20
  9.6 0.6 copy-start.22
  12.7 6.3 copy-start.26
  19.0 4.0 collective-permute-start.6
  21.8 4.4 collective-permute-start.5
  35.3 7.4 copy-start.2
  401.7 3.3 copy-start.8
  573.8 3.4 copy-start.3
  573.8 3.4 copy-start.4
  577.2 1.6 copy-start.5
  578.8 2.0 copy-start.18
  578.8 2.0 copy-start.19
  580.8 3.0 slice-start.2
  581.6 2.9 slice-start.3
  582.5 3.2 copy-start.24
  595.6 2.0 copy-start.11
  599.1 228.6 %collective-permute-start.10 = (bf16[1024,1024]{1,0:T(8,128)(2,1)}, bf16[1024,1024]{1,0:T(8,128)(2,1)S(1)}, u32[]{:S(2)}, u32[]{:S(2)}) collective-permute-start(bf16[1024,1024]{1,0:T(8,128)(2,1)} %constant_dynamic-slice_fusion.1), channel_id=1, source_target_pairs={{0,8},{1,9},{2,10},{3,11},{4,12},{5,13},{6,14},{7,15},{8,0},{9,1},... | collective-permute-start | bytes 6291464 | tf_op jit(solution)/shard_map/ppermute | solution.py:852
  623.4 7.4 copy-start.15
  623.4 7.4 copy-start.16
  628.3 368.6 %collective-permute-start.9 = (bf16[1024,2048]{1,0:T(8,128)(2,1)}, bf16[1024,2048]{1,0:T(8,128)(2,1)}, u32[]{:S(2)}, u32[]{:S(2)}) collective-permute-start(bf16[1024,2048]{1,0:T(8,128)(2,1)} %constant_dynamic-slice_fusion), channel_id=1, source_target_pairs={{0,8},{1,9},{2,10},{3,11},{4,12},{5,13},{6,14},{7,15},{8,0},{9,1},... | collective-permute-start | bytes 12582920 | tf_op jit(solution)/shard_map/ppermute | solution.py:852
  631.5 2.2 slice-start.4
  631.7 3.3 slice-start.5
  631.7 3.5 copy-start.25
  637.6 10.7 copy-start.9
  637.6 3.4 slice-start
  638.0 3.5 slice-start.1
  641.0 7.3 copy-start.13
  648.4 179.3 %copy-start.12 = (bf16[2048,1024]{1,0:T(8,128)(2,1)S(1)}, bf16[2048,1024]{1,0:T(8,128)(2,1)}, u32[]{:S(2)}) copy-start(bf16[2048,1024]{1,0:T(8,128)(2,1)} %copy-done.11) | copy-start | bytes 12582916
  649.9 439.7 %collective-permute-start.7 = (bf16[1024,1024]{0,1:T(8,128)(2,1)}, bf16[1024,1024]{0,1:T(8,128)(2,1)}, u32[]{:S(2)}, u32[]{:S(2)}) collective-permute-start(bf16[1024,1024]{0,1:T(8,128)(2,1)} %fusion.15), channel_id=1, source_target_pairs={{0,8},{1,9},{2,10},{3,11},{4,12},{5,13},{6,14},{7,15},{8,0},{9,1},... | collective-permute-start | bytes 6291464 | tf_op jit(solution)/shard_map/ppermute | solution.py:852
  1075.5 205.8 %collective-permute-start.11 = (bf16[128,16384]{1,0:T(8,128)(2,1)}, bf16[128,16384]{1,0:T(8,128)(2,1)}, u32[]{:S(2)}, u32[]{:S(2)}) collective-permute-start(bf16[128,16384]{1,0:T(8,128)(2,1)} %get-tuple-element.66.diff), channel_id=1, source_target_pairs={{0,16},{1,17},{2,18},{3,19},{4,20},{5,21},{6,22},{7,23},{8,24},{9,... | collective-permute-start | bytes 12582920 | tf_op jit(solution)/shard_map/ppermute | solution.py:856
  1075.5 14.1 %copy-start.10 = (bf16[2048,256]{0,1:T(8,128)(2,1)S(1)}, bf16[2048,256]{0,1:T(8,128)(2,1)}, u32[]{:S(2)}) copy-start(bf16[2048,256]{0,1:T(8,128)(2,1)} %copy-done.9) | copy-start | bytes 3145732
  1124.2 23.7 %copy-start.14 = (bf16[96,8,8,256]{3,1,2,0:T(8,128)(2,1)S(1)}, bf16[96,8,8,256]{3,1,2,0:T(8,128)(2,1)}, u32[]{:S(2)}) copy-start(bf16[96,8,8,256]{3,1,2,0:T(8,128)(2,1)} %copy-done.13) | copy-start | bytes 9437188
  1145.8 102.8 %collective-permute-start.8 = (bf16[128,8192]{1,0:T(8,128)(2,1)}, bf16[128,8192]{1,0:T(8,128)(2,1)}, u32[]{:S(2)}, u32[]{:S(2)}) collective-permute-start(bf16[128,8192]{1,0:T(8,128)(2,1)} %get-tuple-element.57.diff), channel_id=1, source_target_pairs={{0,16},{1,17},{2,18},{3,19},{4,20},{5,21},{6,22},{7,23},{8,24},{9,... | collective-permute-start | bytes 6291464 | tf_op jit(solution)/shard_map/ppermute | solution.py:856
  1147.8 121.9 %collective-permute-start.12 = (bf16[128,8192]{1,0:T(8,128)(2,1)}, bf16[128,8192]{1,0:T(8,128)(2,1)}, u32[]{:S(2)}, u32[]{:S(2)}) collective-permute-start(bf16[128,8192]{1,0:T(8,128)(2,1)} %get-tuple-element.67.diff), channel_id=1, source_target_pairs={{0,16},{1,17},{2,18},{3,19},{4,20},{5,21},{6,22},{7,23},{8,24},{9,... | collective-permute-start | bytes 6291464 | tf_op jit(solution)/shard_map/ppermute | solution.py:856
  1201.0 42.1 %copy-start = (bf16[1,256,2048]{2,1,0:T(8,128)(2,1)S(1)}, bf16[1,256,2048]{2,1,0:T(8,128)(2,1)}, u32[]{:S(2)}) copy-start(bf16[1,256,2048]{2,1,0:T(8,128)(2,1)} %param.11) | copy-start | bytes 3145732
  1201.0 42.1 %copy-start.21 = (f32[256]{0:T(256)S(1)}, f32[256]{0:T(256)}, u32[]{:S(2)}) copy-start(f32[256]{0:T(256)} %copy-done.20) | copy-start | bytes 3076
  1201.0 42.1 %copy-start.23 = (f32[256]{0:T(256)S(1)}, f32[256]{0:T(256)}, u32[]{:S(2)}) copy-start(f32[256]{0:T(256)} %copy-done.22) | copy-start | bytes 3076
  1201.0 44.4 %copy-start.6 = (f32[256,2048]{1,0:T(8,128)S(1)}, f32[256,2048]{1,0:T(8,128)}, u32[]{:S(2)}) copy-start(f32[256,2048]{1,0:T(8,128)} %sum_layer.2) | copy-start | bytes 6291460
  1201.0 44.4 %copy-start.7 = (f32[256,2048]{1,0:T(8,128)S(1)}, f32[256,2048]{1,0:T(8,128)}, u32[]{:S(2)}) copy-start(f32[256,2048]{1,0:T(8,128)} %get-tuple-element.44.resid) | copy-start | bytes 6291460
  1243.0 3.6 copy-start.1
  1243.0 3.6 copy-start.17
where the time goes:
time: 1320 us; the launch traced here: 1300 us
  Pallas kernels  872 us (66%)
  waiting for transfers between devices  181 us (14%)
  matrix products  124 us (9%)
  other arithmetic  56.7 us (4%)
  local copies, waits for them, and re-layouts  55.9 us (4%)
  starting transfers between devices  13.4 us (1%)
    pallas_call x1, Pallas kernels, forward_layer(): pl.pallas_call(functools.partial(forward_kernel, ranks), out_shape=[shape...  353 us
    pallas_call x3, Pallas kernels, trade(): pl.pallas_call(trade_kernel, out_shape=jax.ShapeDtypeStruct(blocks.shape,...  231 us
    ppermute x10, waiting for transfers between devices, hop(): return lax.ppermute(values, ('rep', 'dp'), pairs)  181 us
    dot_general x9, matrix products, dot(): return lax.dot_general(left, right, dims, preferred_element_type=FULL)  120 us
    pallas_call x1, Pallas kernels, back_layer(): pl.pallas_call(back_kernel, out_shape=[jax.ShapeDtypeStruct((count, width...  87 us
    pallas_call x2, Pallas kernels, sum_layer(): pl.pallas_call(sum_kernel, out_shape=jax.ShapeDtypeStruct((count, width),...  83.9 us
    pallas_call x3, Pallas kernels, adam_chunk(): pl.pallas_call(adam_kernel, grid=(TEAM, parts), out_shape=[state, state,...  55.5 us
    pallas_call x3, Pallas kernels, outer_chunk(): pl.pallas_call(functools.partial(outer_kernel, reps), grid=(TEAM, parts),...  55.4 us
  transfers between devices with their start and end apart: 13, of which 3 were waited for; matrix products, arithmetic and copies ran while one was open for 8% of the time, Pallas kernels for 31%

commit v1 on v0

--- a/solution.py
+++ b/solution.py
@@ -172,7 +172,7 @@
             self.over_third[b] = self.send(cut(own, b), cut(out.at[4], b), self.third)
         self.rest.append(self.send(own, out.at[1], self.core))
 
-    def finish(self):
+    def finish(self, middle=None):
         out, cut, send = self.out, self.cut, self.send
         half = PIECES // 2
         corner = {}
@@ -185,6 +185,8 @@
             if b < half:
                 corner[b] = send(cut(out.at[4], b), cut(out.at[6], b), self.second)
             self.rest.append(send(cut(out.at[4], b), cut(out.at[5], b), self.core))
+        if middle is not None:
+            middle()
         for p in range(half):
             for q in (p, p + half):
                 corner[q].wait_recv()
@@ -201,17 +203,13 @@
 
 def sum_scratch(count, width):
     return [
-        pltpu.VMEM((4, count, width), LOW),
-        pltpu.VMEM((4, count, width), LOW),
+        pltpu.VMEM((TEAM // 2, count, width), LOW),
+        pltpu.VMEM((TEAM // 2, count, width), LOW),
         pltpu.VMEM((3, count, width), LOW),
-        pltpu.SemaphoreType.DMA((SUM_COPIES + 4,)),
-        pltpu.SemaphoreType.DMA((SUM_COPIES + 4,)),
-        pltpu.SemaphoreType.DMA((4,)),
     ]
 
 
-def team_sum(me, parts, own, got, edge, sent, came, loads, total):
-    send = Sender(sent, came)
+def team_sum(me, parts, own, got, edge, send, loads, total, between=None, after=None):
     core = {"dp": flip(me, 1)}
     loading = [pltpu.make_async_copy(parts.at[2 * j], own.at[j], loads.at[j]) for j in range(4)]
     first = {}
@@ -220,10 +218,10 @@
         first[j] = send(parts.at[2 * j + 1], got.at[j], core)
     for copy in loading:
         copy.wait()
-    sum_steps(me, own, got, edge, first, send, total, lambda: None)
-
-
-def sum_steps(me, own, got, edge, first, send, total, between):
+    sum_steps(me, own, got, edge, first, send, total, between, after)
+
+
+def sum_steps(me, own, got, edge, first, send, total, between=None, after=None):
     count = own.shape[1]
     half = count // 2
     _, second, third = ({"dp": flip(me, bit)} for bit in BITS)
@@ -251,13 +249,16 @@
     first[1].wait_recv()
     add(1, 0)
     second_early = send(cut(own.at[1], 0), cut(edge.at[1], 0), second)
-    between()
+    if between is not None:
+        between()
     corner_second.wait_recv()
     add(2, 0, edge.at[0])
     third_early = send(cut(own.at[2], 0), cut(edge.at[2], 0), third)
     corner_third.wait_recv()
     add(1, 1, edge.at[0])
     second_late = send(cut(own.at[1], 1), cut(edge.at[1], 1), second)
+    if after is not None:
+        after()
     first[0].wait_recv()
     for h, waits in ((0, (second_early, third_early)), (1, (third_late, second_late))):
         for copy in waits:
@@ -640,14 +641,348 @@
     )(flat, normed, cot, att_pack, mlp_master, cosine, sine, bias)
 
 
-def back_kernel(parts, resid, cot, grad_resid, grad_all, grad_low, *refs):
-    sum_refs, (sent, came, local) = refs[:6], refs[6:]
+def attend_unit_back(values, given, cosine, sine, bias, share):
+    depth = HEAD_DIM
+    scale = depth ** (-0.5)
+    grads = ([], [], [])
+    for at in range(0, share, depth):
+        query, keys, value = (values[:, p * share + at : p * share + at + depth] for p in range(3))
+        grad = given[:, at : at + depth]
+        scores = dot(query, keys, CONTRACT_LAST) * scale + bias
+        powers = jnp.exp(scores - jnp.max(scores, axis=1, keepdims=True))
+        prob = powers / jnp.sum(powers, axis=1, keepdims=True)
+        grad_prob = dot(grad, value, CONTRACT_LAST)
+        grad_value = dot(prob.astype(LOW), grad, CONTRACT_FIRST)
+        along = jnp.sum(grad_prob * prob, axis=1, keepdims=True)
+        grad_scores = (prob * (grad_prob - along)).astype(LOW)
+        turned = (
+            dot(grad_scores, keys) * scale,
+            dot(grad_scores, query, CONTRACT_FIRST) * scale,
+        )
+        for p in range(2):
+            back = turned[p] * cosine - pltpu.roll(turned[p], depth // 2, 1) * sine
+            grads[p].append(back.astype(LOW))
+        grads[2].append(grad_value.astype(LOW))
+    return jnp.concatenate(grads[0] + grads[1] + grads[2], axis=1)
+
+
+UNIT = 256
+
+
+def unit_of(step):
+    return 2 * (TEAM // 2 - 1 - step % (TEAM // 2)) + jnp.where(step < TEAM // 2, 1, 0)
+
+
+class Terms:
+    def __init__(self, me, odd, own, got, sent, came):
+        self.odd, self.own, self.got, self.sent, self.came = odd, own, got, sent, came
+        self.core = {"dp": flip(me, 1)}
+
+    def copy(self, j):
+        return pltpu.make_async_remote_copy(
+            src_ref=self.odd.at[j],
+            dst_ref=self.got.at[j],
+            send_sem=self.sent.at[j],
+            recv_sem=self.came.at[j],
+            device_id=self.core,
+            device_id_type=MESH,
+        )
+
+    def put(self, step, term):
+        j = unit_of(step) // 2
+
+        @pl.when(step < TEAM // 2)
+        def _():
+            self.odd[j] = term
+            self.copy(j).start()
+
+        @pl.when(step >= TEAM // 2)
+        def _():
+            self.own[j] = term
+
+    def first(self):
+        return [self.copy(j) for j in range(TEAM // 2)]
+
+
+def stream(steps, loads, body):
+    for copy in loads(0, 0):
+        copy.start()
+
+    @pl.loop(0, steps)
+    def _(step):
+        slot = step % 2
+
+        @pl.when(step + 1 < steps)
+        def _():
+            for copy in loads(step + 1, 1 - slot):
+                copy.start()
+
+        for copy in loads(step, slot):
+            copy.wait()
+        body(step, slot)
+
+
+def stream_out(steps, loads, stores, body):
+    def whole(step, slot):
+        @pl.when(step >= 2)
+        def _():
+            for copy in stores(step - 2, slot):
+                copy.wait()
+
+        body(step, slot)
+        for copy in stores(step, slot):
+            copy.start()
+
+    stream(steps, loads, whole)
+    for step in (steps - 2, steps - 1):
+        for copy in stores(step, step % 2):
+            copy.wait()
+
+
+def rows_at(step, size):
+    return pl.ds(pl.multiple_of(step * size, size), size)
+
+
+def backward_kernel(
+    ranks,
+    flat,
+    resid,
+    cot,
+    cosine,
+    sine,
+    bias,
+    cot_all,
+    hidden_all,
+    gate_all,
+    up_all,
+    normed_two_all,
+    normed_one_all,
+    projected_all,
+    mixed_all,
+    att_weights,
+    gate_weights,
+    down_weights,
+    att_master,
+    att_first,
+    att_second,
+    mlp_master,
+    mlp_first,
+    mlp_second,
+    out_tokens,
+    grad_tokens,
+    got_att,
+    got_gate,
+    got_down,
+    att_diff,
+    att_other,
+    mlp_diff,
+    mlp_other,
+    grad_all,
+    att_grad,
+    gate_grad,
+    down_grad,
+    fed_all,
+    own,
+    got,
+    edge,
+    odd,
+    own_two,
+    got_two,
+    edge_two,
+    grad_low,
+    grad_resid,
+    stage,
+    sent,
+    came,
+    sent_rows,
+    came_rows,
+    sent_first,
+    came_first,
+    sent_x,
+    came_x,
+    kept,
+    local,
+):
     me = lax.axis_index("dp")
-    greet(me, BITS, False)
-
-    def total(start, value):
+    rep = lax.axis_index("rep")
+    tops = ranks // TEAM
+    rows = got_att.shape[1]
+    share = mixed_all.shape[1]
+    hid = hidden_all.shape[1]
+    count, width = resid.shape
+    tokens = TEAM * count
+    tiles = width // UNIT
+    greet(me, range(1, ranks), True)
+    send = Sender(sent, came)
+    order = []
+    for low_bits in range(TEAM):
+        order += [top * TEAM + low_bits for top in range(1, tops)]
+        order += [low_bits] if low_bits else []
+
+    chunks = ((down_grad, got_down), (gate_grad, got_gate), (att_grad, got_att))
+
+    def block_copy(chunk, other):
+        grad, target = chunks[chunk]
+        index = chunk * (ranks - 1) + other - 1
+        where = across(me, other)
+        return pltpu.make_async_remote_copy(
+            src_ref=grad.at[pl.ds(where * rows, rows)],
+            dst_ref=target.at[me],
+            send_sem=sent_rows.at[index],
+            recv_sem=came_rows.at[index],
+            device_id={"dp": where},
+            device_id_type=MESH,
+        )
+
+    def keep_own(grad, target, index):
+        copy = pltpu.make_async_copy(
+            grad.at[pl.ds(me * rows, rows)], target.at[me], kept.at[index]
+        )
+        copy.start()
+        return copy
+
+    def down_phase(hidden, tile, low):
+        whole = pltpu.make_async_copy(hidden_all, hidden, local.at[0])
+        whole.start()
+
+        def loads(step, slot):
+            at = rows_at(step, UNIT)
+            return [pltpu.make_async_copy(cot_all.at[:, at], tile.at[slot], local.at[2 + slot])]
+
+        def stores(step, slot):
+            at = rows_at(step, UNIT)
+            return [pltpu.make_async_copy(low.at[slot], down_grad.at[at], local.at[4 + slot])]
+
+        def body(step, slot):
+            low[slot] = dot(tile[slot], hidden[...], CONTRACT_FIRST).astype(LOW)
+
+        whole.wait()
+        stream_out(tiles, loads, stores, body)
+
+    pl.run_scoped(
+        down_phase,
+        pltpu.VMEM((tokens, hid), LOW),
+        pltpu.VMEM((2, tokens, UNIT), LOW),
+        pltpu.VMEM((2, UNIT, hid), LOW),
+    )
+    for other in order:
+        block_copy(0, other).start()
+    own_copies = [keep_own(down_grad, got_down, 0)]
+
+    def fed_phase(hidden, down, term):
+        whole = [
+            pltpu.make_async_copy(hidden_all, hidden, local.at[0]),
+            pltpu.make_async_copy(down_weights, down, local.at[1]),
+        ]
+        for copy in whole:
+            copy.start()
+        for copy in whole:
+            copy.wait()
+
+        def fed_stores(step, slot):
+            return [pltpu.make_async_copy(term.at[slot], fed_all.at[step], local.at[6 + slot])]
+
+        def fed_body(step, slot):
+            term[slot] = dot(hidden[rows_at(step, count)], down[...], CONTRACT_LAST).astype(LOW)
+
+        stream_out(TEAM, lambda step, slot: [], fed_stores, fed_body)
+
+    pl.run_scoped(
+        fed_phase,
+        pltpu.VMEM((tokens, hid), LOW),
+        pltpu.VMEM((width, hid), LOW),
+        pltpu.VMEM((2, count, width), LOW),
+    )
+    gate_order = list(order)
+
+    def more(number):
+        def some():
+            for _ in range(min(number, len(gate_order))):
+                block_copy(1, gate_order.pop(0)).start()
+
+        return some
+
+    terms = Terms(me, odd, own, got, sent_first.at[0], came_first.at[0])
+
+    def gate_phase(grad_gate):
+        def hidden_phase(down, block, gate, up):
+            whole = pltpu.make_async_copy(down_weights, down, local.at[1])
+            whole.start()
+
+            def loads(step, slot):
+                at = rows_at(step, count)
+                return [
+                    pltpu.make_async_copy(cot_all.at[at], block.at[slot], local.at[2 + slot]),
+                    pltpu.make_async_copy(gate_all.at[at], gate.at[slot], local.at[4 + slot]),
+                    pltpu.make_async_copy(up_all.at[at], up.at[slot], local.at[6 + slot]),
+                ]
+
+            def body(step, slot):
+                at = rows_at(step, count)
+
+                @pl.loop(0, hid // UNIT)
+                def _(column):
+                    place = rows_at(column, UNIT)
+                    later = pl.ds(pl.multiple_of(hid + column * UNIT, UNIT), UNIT)
+                    grad = dot(block[slot], down[:, place])
+                    value = gate[slot, :, place].astype(FULL)
+                    sigmoid = jax.nn.sigmoid(value)
+                    slope = sigmoid * (1.0 + value * (1.0 - sigmoid))
+                    up_value = up[slot, :, place].astype(FULL)
+                    grad_gate[at, place] = (grad * up_value * slope).astype(LOW)
+                    grad_gate[at, later] = (grad * value * sigmoid).astype(LOW)
+
+            whole.wait()
+            stream(TEAM, loads, body)
+
+        pl.run_scoped(
+            hidden_phase,
+            pltpu.VMEM((width, hid), LOW),
+            pltpu.VMEM((2, count, width), LOW),
+            pltpu.VMEM((2, count, hid), LOW),
+            pltpu.VMEM((2, count, hid), LOW),
+        )
+
+        def weight_phase(tile, low):
+            def loads(step, slot):
+                at = rows_at(step, UNIT)
+                return [
+                    pltpu.make_async_copy(
+                        normed_two_all.at[:, at], tile.at[slot], local.at[2 + slot]
+                    )
+                ]
+
+            def stores(step, slot):
+                at = rows_at(step, UNIT)
+                return [pltpu.make_async_copy(low.at[slot], gate_grad.at[at], local.at[4 + slot])]
+
+            def body(step, slot):
+                low[slot] = dot(tile[slot], grad_gate[...], CONTRACT_FIRST).astype(LOW)
+
+            stream_out(tiles, loads, stores, body)
+
+        pl.run_scoped(
+            weight_phase, pltpu.VMEM((2, tokens, UNIT), LOW), pltpu.VMEM((2, UNIT, 2 * hid), LOW)
+        )
+        more(GATE_FIRST)()
+
+        def back_phase(gate):
+            whole = pltpu.make_async_copy(gate_weights, gate, local.at[0])
+            whole.start()
+            whole.wait()
+
+            @pl.loop(0, TEAM)
+            def _(step):
+                at = rows_at(unit_of(step), count)
+                terms.put(step, dot(grad_gate[at], gate[...], CONTRACT_LAST).astype(LOW))
+
+        pl.run_scoped(back_phase, pltpu.VMEM((width, 2 * hid), LOW))
+
+    pl.run_scoped(gate_phase, pltpu.VMEM((tokens, 2 * hid), LOW))
+    own_copies.append(keep_own(gate_grad, got_gate, 1))
+
+    def resid_total(start, value):
         at = pl.ds(start, STRIP)
-        width = value.shape[1]
         normed, factor = strip_normalize(resid[at])
         along = jnp.sum(value * normed, axis=1, keepdims=True) * (1.0 / width)
         middle = jnp.sum(value, axis=1, keepdims=True) * (1.0 / width)
@@ -655,83 +990,300 @@
         grad_resid[at] = value
         grad_low[at] = value.astype(LOW)
 
-    team_sum(me, parts, *sum_refs, total)
-    gather = TeamGather(me, grad_low, grad_all, Sender(sent, came))
+    sum_steps(
+        me, own, got, edge, terms.first(), send, resid_total, more(GATE_EARLY), more(GATE_LATE)
+    )
+    gather = TeamGather(me, grad_low, grad_all, send)
     gather.begin()
-    keep = pltpu.make_async_copy(grad_low, grad_all.at[0], local)
+    more(GATE_GATHER)()
+    keep = pltpu.make_async_copy(grad_low, grad_all.at[0], local.at[0])
     keep.start()
-    gather.finish()
+    gather.finish(more(len(gate_order)))
     keep.wait()
 
-
-def back_layer(parts, resid, cot):
-    team, count, width = parts.shape
+    terms = Terms(me, odd, own, got, sent_first.at[1], came_first.at[1])
+
+    def att_phase(att, grad_projected):
+        def unit_phase(block, projected, tables, mask):
+            def loads(step, slot):
+                unit = unit_of(step)
+                return [
+                    pltpu.make_async_copy(grad_all.at[unit], block.at[slot], local.at[slot]),
+                    pltpu.make_async_copy(
+                        projected_all.at[unit], projected.at[slot], local.at[2 + slot]
+                    ),
+                    pltpu.make_async_copy(cosine.at[unit], tables.at[slot, 0], local.at[4 + slot]),
+                    pltpu.make_async_copy(sine.at[unit], tables.at[slot, 1], local.at[6 + slot]),
+                    pltpu.make_async_copy(bias.at[unit], mask.at[slot], local.at[8 + slot]),
+                ]
+
+            def body(step, slot):
+                given = dot(block[slot], att[:, 3 * share :]).astype(LOW)
+                grads = attend_unit_back(
+                    projected[slot], given, tables[slot, 0], tables[slot, 1], mask[slot], share
+                )
+                grad_projected[rows_at(unit_of(step), count)] = grads
+                terms.put(step, dot(grads, att[:, : 3 * share], CONTRACT_LAST).astype(LOW))
+
+            whole = pltpu.make_async_copy(att_weights, att, local.at[10])
+            whole.start()
+            whole.wait()
+            stream(TEAM, loads, body)
+
+        pl.run_scoped(
+            unit_phase,
+            pltpu.VMEM((2, count, width), LOW),
+            pltpu.VMEM((2, count, 3 * share), LOW),
+            pltpu.VMEM((2, 2, count, HEAD_DIM), FULL),
+            pltpu.VMEM((2, count, count), FULL),
+        )
+
+        def weight_phase(normed, grad, mixed, low):
+            def loads(step, slot):
+                at = rows_at(step, UNIT)
+                return [
+                    pltpu.make_async_copy(
+                        normed_one_all.at[:, at], normed.at[slot], local.at[slot]
+                    ),
+                    pltpu.make_async_copy(
+                        grad_all.at[:, :, at], grad.at[slot], local.at[2 + slot]
+                    ),
+                ]
+
+            def stores(step, slot):
+                at = rows_at(step, UNIT)
+                return [pltpu.make_async_copy(low.at[slot], att_grad.at[at], local.at[4 + slot])]
+
+            def body(step, slot):
+                left = normed[slot]
+                low[slot, :, : 3 * share] = dot(left, grad_projected[...], CONTRACT_FIRST).astype(LOW)
+                left = grad[slot].reshape(tokens, UNIT)
+                low[slot, :, 3 * share :] = dot(left, mixed[...], CONTRACT_FIRST).astype(LOW)
+
+            whole = pltpu.make_async_copy(mixed_all, mixed, local.at[10])
+            whole.start()
+            whole.wait()
+            stream_out(tiles, loads, stores, body)
+
+        pl.run_scoped(
+            weight_phase,
+            pltpu.VMEM((2, tokens, UNIT), LOW),
+            pltpu.VMEM((2, TEAM, count, UNIT), LOW),
+            pltpu.VMEM((tokens, share), LOW),
+            pltpu.VMEM((2, UNIT, 4 * share), LOW),
+        )
+
+    pl.run_scoped(
+        att_phase, pltpu.VMEM((width, 4 * share), LOW), pltpu.VMEM((tokens, 3 * share), LOW)
+    )
+    for other in order:
+        block_copy(2, other).start()
+    own_copies.append(keep_own(att_grad, got_att, 2))
+
+    def differ(chunk, pieces, states, diff, other, column, mates):
+        master, first, second = states
+        each = hid // mates
+
+        def near(block):
+            return pltpu.make_async_copy(
+                stage.at[block], diff.at[:, column(block)], kept.at[3 + block]
+            )
+
+        def far(block):
+            index = chunk * TEAM + block
+            return pltpu.make_async_remote_copy(
+                src_ref=stage.at[block],
+                dst_ref=other.at[:, column(block)],
+                send_sem=sent_x.at[index],
+                recv_sem=came_x.at[index],
+                device_id={"rep": 1 - rep},
+                device_id_type=MESH,
+            )
+
+        def run(wide, low):
+            def loads(block, slot):
+                at = column(block)
+                return [
+                    pltpu.make_async_copy(master.at[:, at], wide.at[slot, 0], local.at[slot]),
+                    pltpu.make_async_copy(first.at[0, :, at], wide.at[slot, 1], local.at[2 + slot]),
+                    pltpu.make_async_copy(second.at[0, :, at], wide.at[slot, 2], local.at[4 + slot]),
+                ] + [
+                    pltpu.make_async_copy(
+                        pieces(block, top, i),
+                        low.at[slot, top, i],
+                        local.at[6 + slot + 2 * (top * mates + i)],
+                    )
+                    for top in range(tops)
+                    for i in range(mates)
+                ]
+
+            def body(block, slot):
+                @pl.loop(0, rows // STRIP)
+                def _(step):
+                    at = pl.ds(step * STRIP, STRIP)
+                    for i in range(mates):
+                        span = slice(i * each, (i + 1) * each)
+                        grad = low[slot, 0, i, at].astype(FULL)
+                        for top in range(1, tops):
+                            grad = grad + low[slot, top, i, at].astype(FULL)
+                        value = wide[slot, 0, at, span]
+                        inner, _, _ = adam_step(
+                            value, grad, wide[slot, 1, at, span], wide[slot, 2, at, span]
+                        )
+                        stage[block, at, span] = (value - inner).astype(LOW)
+
+                near(block).start()
+                far(block).start()
+
+            stream(TEAM, loads, body)
+
+            @pl.loop(0, TEAM)
+            def _(block):
+                near(block).wait()
+                far(block).wait_send()
+
+        pl.run_scoped(
+            run,
+            pltpu.VMEM((2, 3, rows, hid), FULL),
+            pltpu.VMEM((2, tops, mates, rows, each), LOW),
+        )
+
+        def finish():
+            @pl.loop(0, TEAM)
+            def _(block):
+                far(block).wait_recv()
+
+        return finish
+
+    def mlp_chunk(chunk, part, source, offset):
+        return differ(
+            chunk,
+            lambda block, top, i: source.at[top * TEAM + block, :, pl.ds(offset, hid)],
+            (mlp_master, mlp_first, mlp_second),
+            mlp_diff,
+            mlp_other,
+            lambda block: pl.ds(pl.multiple_of((part * TEAM + block) * hid, hid), hid),
+            1,
+        )
+
+    def att_chunk(chunk):
+        mates = hid // share
+        steps = TEAM // mates
+
+        def piece(block, top, i):
+            part = block // steps
+            mate = (block % steps) * mates + i
+            at = pl.ds(pl.multiple_of(part * share, share), share)
+            return got_att.at[top * TEAM + mate, :, at]
+
+        return differ(
+            chunk,
+            piece,
+            (att_master, att_first, att_second),
+            att_diff,
+            att_other,
+            lambda block: pl.ds(pl.multiple_of(block * hid, hid), hid),
+            mates,
+        )
+
+    waits = []
+
+    def down_changes():
+        own_copies[0].wait()
+        for other in order:
+            block_copy(0, other).wait_recv()
+        waits.append(mlp_chunk(0, 2, got_down, 0))
+
+    def gate_changes():
+        own_copies[1].wait()
+        for other in order:
+            block_copy(1, other).wait_recv()
+        waits.append(mlp_chunk(1, 0, got_gate, 0))
+        waits.append(mlp_chunk(2, 1, got_gate, hid))
+
+    def tokens_total(start, value):
+        at = pl.ds(start, STRIP)
+        normed, factor = strip_normalize(flat[at].astype(FULL))
+        along = jnp.sum(value * normed, axis=1, keepdims=True) * (1.0 / width)
+        middle = jnp.sum(value, axis=1, keepdims=True) * (1.0 / width)
+        grad_tokens[at] = grad_resid[at] + factor * (value - middle - normed * along)
+
+    def out_total(start, value):
+        at = pl.ds(start, STRIP)
+        out_tokens[at] = (resid[at] + value).astype(LOW)
+
+    def fed_sum():
+        team_sum(
+            me, fed_all, own_two, got_two, edge_two, send, local, out_total, gate_changes
+        )
+
+    down_changes()
+    sum_steps(me, own, got, edge, terms.first(), send, tokens_total, fed_sum)
+    own_copies[2].wait()
+    for other in order:
+        block_copy(2, other).wait_recv()
+    waits.append(att_chunk(3))
+    for chunk in range(3):
+        for other in order:
+            block_copy(chunk, other).wait_send()
+    for wait in waits:
+        wait()
+
+
+GATE_FIRST, GATE_EARLY, GATE_LATE, GATE_GATHER = 2, 2, 2, 2
+
+
+def backward_layer(ranks, tokens, att, mlp, *rest):
+    flat, resid, cot = tokens
+    hidden_all, projected_all, gate_weights = rest[4], rest[9], rest[12]
+    count, width = flat.shape
+    all_tokens, hid = hidden_all.shape
+    share = projected_all.shape[2] // 3
+    rows = width // ranks
     vmem = pl.BlockSpec(memory_space=pltpu.VMEM)
+    low = functools.partial(jax.ShapeDtypeStruct, dtype=LOW)
+    out = [
+        (low((count, width)), vmem),
+        (jax.ShapeDtypeStruct((count, width), FULL), vmem),
+        (low((ranks, rows, 4 * share)), ANYWHERE),
+        (low((ranks, rows, 2 * hid)), ANYWHERE),
+        (low((ranks, rows, hid)), ANYWHERE),
+        (low(att[0].shape), ANYWHERE),
+        (low(att[0].shape), ANYWHERE),
+        (low(mlp[0].shape), ANYWHERE),
+        (low(mlp[0].shape), ANYWHERE),
+        (low((TEAM, count, width)), ANYWHERE),
+        (low((width, 4 * share)), ANYWHERE),
+        (low((width, 2 * hid)), ANYWHERE),
+        (low((width, hid)), ANYWHERE),
+        (low((TEAM, count, width)), ANYWHERE),
+    ]
+    team_copies = GATHER_COPIES + 2 * SUM_COPIES + SUM_COPIES + TEAM // 2
+    locals_needed = 6 + 2 * (ranks // TEAM) * (hid // share) + 2
+    sems = [team_copies] * 2 + [3 * (ranks - 1)] * 2
     return pl.pallas_call(
-        back_kernel,
-        out_shape=[
-            jax.ShapeDtypeStruct((count, width), FULL),
-            jax.ShapeDtypeStruct((team, count, width), LOW),
+        functools.partial(backward_kernel, ranks),
+        out_shape=[shape for shape, _ in out],
+        in_specs=[vmem] * 3 + [ANYWHERE] * (len(rest) + 6),
+        out_specs=[spec for _, spec in out],
+        scratch_shapes=sum_scratch(count, width)
+        + [pltpu.VMEM((TEAM // 2, count, width), LOW)]
+        + sum_scratch(count, width)
+        + [
+            pltpu.VMEM((count, width), LOW),
+            pltpu.VMEM((count, width), FULL),
+            pltpu.VMEM((TEAM, rows, hid), LOW),
+        ]
+        + [pltpu.SemaphoreType.DMA((number,)) for number in sems]
+        + [pltpu.SemaphoreType.DMA((2, TEAM // 2))] * 2
+        + [pltpu.SemaphoreType.DMA((4 * TEAM,))] * 2
+        + [
+            pltpu.SemaphoreType.DMA((3 + TEAM,)),
+            pltpu.SemaphoreType.DMA((max(locals_needed, 12),)),
         ],
-        in_specs=[ANYWHERE, vmem, vmem],
-        out_specs=[vmem, ANYWHERE],
-        scratch_shapes=[pltpu.VMEM((count, width), LOW)]
-        + sum_scratch(count, width)
-        + [pltpu.SemaphoreType.DMA((GATHER_COPIES,))] * 2
-        + [pltpu.SemaphoreType.DMA],
         compiler_params=params(2),
-        name="back_layer",
-    )(parts, resid, cot)
-
-
-def sum_kernel(parts, out, *refs):
-    me = lax.axis_index("dp")
-    greet(me, BITS, False)
-
-    def total(start, value):
-        out[pl.ds(start, STRIP)] = value
-
-    team_sum(me, parts, *refs, total)
-
-
-def sum_layer(parts, collective_id):
-    team, count, width = parts.shape
-    return pl.pallas_call(
-        sum_kernel,
-        out_shape=jax.ShapeDtypeStruct((count, width), FULL),
-        in_specs=[ANYWHERE],
-        out_specs=pl.BlockSpec(memory_space=pltpu.VMEM),
-        scratch_shapes=sum_scratch(count, width),
-        compiler_params=params(collective_id),
-        name="sum_layer",
-    )(parts)
-
-
-def trade_kernel(blocks, out, sent, came, local):
-    me = lax.axis_index("dp")
-    greet(me, range(1, TEAM), False)
-    send = Sender(sent, came)
-    keep = pltpu.make_async_copy(blocks.at[me % TEAM], out.at[me % TEAM], local)
-    keep.start()
-    copies = []
-    for other in (7, 6, 5, 4, 3, 2, 1):
-        where = across(me, other)
-        copies.append(send(blocks.at[where % TEAM], out.at[me % TEAM], {"dp": where}))
-    for copy in copies:
-        copy.wait()
-    keep.wait()
-
-
-def trade(blocks, collective_id):
-    return pl.pallas_call(
-        trade_kernel,
-        out_shape=jax.ShapeDtypeStruct(blocks.shape, blocks.dtype),
-        in_specs=[ANYWHERE],
-        out_specs=ANYWHERE,
-        scratch_shapes=[pltpu.SemaphoreType.DMA((TEAM - 1,))] * 2 + [pltpu.SemaphoreType.DMA],
-        compiler_params=params(collective_id),
-        name="trade",
-    )(blocks)
+        name="backward_layer",
+    )(flat, resid, cot, *rest, *att, *mlp)
 
 
 def pack_kernel(*refs):
@@ -754,68 +1306,56 @@
     )(*[master] * len(bases))
 
 
-def adam_kernel(grad, master, first, second, *refs):
-    first_new, second_new, diff = refs[-3:]
-    gradient = grad[0].astype(FULL)
-    inner, first_new[0], second_new[0] = adam_step(master[...], gradient, first[0], second[0])
-    diff[...] = (master[...] - inner).astype(LOW)
-
-
-def adam_chunk(grads, master, first, second, bases, share, written):
-    rows = master.shape[0]
+LANES = 1024
+
+
+def finish_kernel(reps, share, grads, master, first, second, outer, diff, other, *refs):
+    first_new, second_new, mean_out, new, outer_new = refs[-5:]
+    for t in range(grads.shape[1]):
+        at = slice(t * share, (t + 1) * share)
+        grad = grads[0, t].astype(FULL)
+        for top in range(1, grads.shape[0]):
+            grad = grad + grads[top, t].astype(FULL)
+        first_new[0, :, at] = BETA_ONE * first[0, :, at] + (1.0 - BETA_ONE) * grad
+        second_new[0, :, at] = BETA_TWO * second[0, :, at] + (1.0 - BETA_TWO) * grad * grad
+    mean = (diff[...].astype(FULL) + other[...].astype(FULL)) / reps
+    mean_out[...] = mean
+    new[...], outer_new[...] = outer_step(master[...], mean, outer[...])
+
+
+def finish_chunk(reps, grads, master, first, second, outer, diff, other, bases, written):
+    ranks, rows, columns = grads.shape
     parts = len(bases)
-
-    def column(t, p):
+    share = columns // parts
+    lanes = max(LANES, share)
+    per = lanes // share
+    steps = TEAM // per
+
+    def column(p, t):
         place = bases[0]
         for q in range(1, parts):
             place = place + jnp.where(p >= q, bases[q] - bases[q - 1], 0)
-        return place + t
-
-    wide = pl.BlockSpec((1, rows, share), lambda t, p: (0, 0, column(t, p)))
-    flat = pl.BlockSpec((rows, share), lambda t, p: (0, column(t, p)))
+        return place * steps + t
+
+    grad = pl.BlockSpec((ranks // TEAM, per, rows, share), lambda p, t: (0, t, 0, p))
+    wide = pl.BlockSpec((1, rows, lanes), lambda p, t: (0, 0, column(p, t)))
+    flat = pl.BlockSpec((rows, lanes), lambda p, t: (0, column(p, t)))
+    extra = [] if written is None else list(written)
     state = jax.ShapeDtypeStruct(first.shape, FULL)
-    extra = [] if written is None else list(written)
+    plain = jax.ShapeDtypeStruct(master.shape, FULL)
     return pl.pallas_call(
-        adam_kernel,
-        grid=(TEAM, parts),
-        out_shape=[state, state, jax.ShapeDtypeStruct((rows, TEAM * parts * share), LOW)],
-        in_specs=[pl.BlockSpec((1, rows, share), lambda t, p: (t, 0, p)), flat, wide, wide]
-        + [ANYWHERE] * len(extra),
-        out_specs=[wide, wide, pl.BlockSpec((rows, share), lambda t, p: (0, p * TEAM + t))],
-        input_output_aliases={4 + i: i for i in range(len(extra))},
-        name="adam_chunk",
-    )(grads, master, first, second, *extra)
-
-
-def outer_kernel(reps, diff, other, master, momentum, *refs):
-    mean_out, new, momentum_new = refs[-3:]
-    mean = (diff[...].astype(FULL) + other[...].astype(FULL)) / reps
-    mean_out[...] = mean
-    new[...], momentum_new[...] = outer_step(master[...], mean, momentum[...])
-
-
-def outer_chunk(reps, diff, other, master, momentum, bases, share, written):
-    rows = master.shape[0]
-    parts = len(bases)
-
-    def column(t, p):
-        place = bases[0]
-        for q in range(1, parts):
-            place = place + jnp.where(p >= q, bases[q] - bases[q - 1], 0)
-        return place + t
-
-    flat = pl.BlockSpec((rows, share), lambda t, p: (0, column(t, p)))
-    packed = pl.BlockSpec((rows, share), lambda t, p: (0, p * TEAM + t))
-    extra = [] if written is None else list(written)
-    return pl.pallas_call(
-        functools.partial(outer_kernel, reps),
-        grid=(TEAM, parts),
-        out_shape=[jax.ShapeDtypeStruct(master.shape, FULL)] * 3,
-        in_specs=[packed, packed, flat, flat] + [ANYWHERE] * len(extra),
-        out_specs=[flat] * 3,
-        input_output_aliases={4 + i: i for i in range(len(extra))},
-        name="outer_chunk",
-    )(diff, other, master, momentum, *extra)
+        functools.partial(finish_kernel, reps, share),
+        grid=(parts, steps),
+        out_shape=[state, state, plain, plain, plain],
+        in_specs=[grad, flat, wide, wide, flat, flat, flat] + [ANYWHERE] * len(extra),
+        out_specs=[wide, wide, flat, flat, flat],
+        input_output_aliases={7 + i: i for i in range(len(extra))},
+        compiler_params=pltpu.CompilerParams(vmem_limit_bytes=VMEM_BYTES),
+        name="finish_chunk",
+    )(
+        grads.reshape(ranks // TEAM, TEAM, rows, columns),
+        master, first, second, outer, diff, other, *extra,
+    )
 
 
 def on_device(
@@ -851,29 +1391,13 @@
         pairs = [(r * ranks + i, r * ranks + (i ^ other)) for r in range(reps) for i in range(ranks)]
         return lax.ppermute(values, ("rep", "dp"), pairs)
 
-    def swap(values):
-        pairs = [(r * ranks + i, (1 - r) * ranks + i) for r in range(reps) for i in range(ranks)]
-        return lax.ppermute(values, ("rep", "dp"), pairs)
-
-    def combine(grad):
-        span = team * rows
-        kept = lax.dynamic_slice_in_dim(grad, top * span, span, 0)
-        if tops > 1:
-            kept = kept.astype(FULL)
-        for other in range(1, tops):
-            sent = lax.dynamic_slice_in_dim(grad, (top ^ other) * span, span, 0)
-            kept = kept + hop(sent, other * team).astype(FULL)
-        return kept.astype(LOW).reshape(team, rows, grad.shape[1])
-
     flat_low = tokens.reshape(count, width)
     flat = flat_low.astype(FULL)
     cot = cotangent.reshape(count, width)
     seen_all = jnp.stack([branch if k == 0 else hop(branch, k) for k in range(team)])
     seen_all = seen_all.reshape(team * units, CONT)
-    heads = att_share // depth
     position, allowed = jax.vmap(lambda seen: token_layout(seen, length))(seen_all)
     cosine, sine = jax.vmap(lambda places: rotary_tables(places, depth))(position)
-    scale = depth ** (-0.5)
     bias = jnp.where(allowed, 0.0, -1e30).astype(FULL)
     wide_cosine = jnp.concatenate([cosine, cosine], axis=-1).reshape(team, count, depth)
     wide_sine = jnp.concatenate([-sine, sine], axis=-1).reshape(team, count, depth)
@@ -904,76 +1428,49 @@
         wide_sine,
         bias,
     )
-    normed_one = normed_one.reshape(all_tokens, width)
-    grad_fed = grad_fed.reshape(all_tokens, width)
-    mixed = mixed.reshape(all_tokens, att_share)
-    normed_two = normed_two.reshape(all_tokens, width)
-    gate_value = gate_value.reshape(all_tokens, hid_share).astype(FULL)
-    up_value = up_value.reshape(all_tokens, hid_share).astype(FULL)
-    hidden = hidden.reshape(all_tokens, hid_share)
-    qkv_low, out_low = att_low[:, : 3 * att_share], att_low[:, 3 * att_share :]
-    projected = projected.reshape(team * units, length, 3, heads, depth)
-    query, keys, values = projected[:, :, 0], projected[:, :, 1], projected[:, :, 2]
-
-    def ein(spec, left, right):
-        return jnp.einsum(spec, left, right, preferred_element_type=FULL)
-
-    scores = ein("uqhd,ukhd->uhqk", query, keys) * scale + bias[:, None]
-    powers = jnp.exp(scores - jnp.max(scores, axis=-1, keepdims=True))
-    prob = powers / jnp.sum(powers, axis=-1, keepdims=True)
-    prob_low = prob.astype(LOW)
-    sigmoid_gate = jax.nn.sigmoid(gate_value)
-    silu_gate = gate_value * sigmoid_gate
-    down_grad = combine(dot(grad_fed, hidden, CONTRACT_FIRST).astype(LOW))
-    grad_hidden = dot(grad_fed, down_low)
-    grad_gate = grad_hidden * up_value * sigmoid_gate * (1.0 + gate_value * (1.0 - sigmoid_gate))
-    grad_up = grad_hidden * silu_gate
-    grad_gate_up = jnp.concatenate([grad_gate, grad_up], axis=1).astype(LOW)
-    gate_grad = combine(dot(normed_two, grad_gate_up, CONTRACT_FIRST).astype(LOW))
-    grad_normed_two = dot(grad_gate_up, gate_low, CONTRACT_LAST).astype(LOW)
-    grad_resid, grad_attended = back_layer(
-        grad_normed_two.reshape(team, count, width), resid, cot
-    )
-    grad_attended = grad_attended.reshape(all_tokens, width)
-    grad_mixed = dot(grad_attended, out_low).astype(LOW)
-    out_grad = dot(grad_attended, mixed, CONTRACT_FIRST)
-    grad_mixed = grad_mixed.reshape(team * units, length, heads, depth)
-    grad_prob = ein("uqhd,ukhd->uhqk", grad_mixed, values)
-    grad_values = ein("uhqk,uqhd->ukhd", prob_low, grad_mixed)
-    grad_scores = prob * (grad_prob - jnp.sum(grad_prob * prob, axis=-1, keepdims=True))
-    grad_scores = grad_scores.astype(LOW)
-    grad_query = rotate_back(ein("uhqk,ukhd->uqhd", grad_scores, keys) * scale, cosine, sine)
-    grad_keys = rotate_back(ein("uhqk,uqhd->ukhd", grad_scores, query) * scale, cosine, sine)
-    grad_projected = jnp.stack([grad_query, grad_keys, grad_values], axis=2).astype(LOW)
-    grad_projected = grad_projected.reshape(all_tokens, 3 * att_share)
-    qkv_grad = dot(normed_one, grad_projected, CONTRACT_FIRST)
-    att_grad = combine(jnp.concatenate([qkv_grad, out_grad], axis=1).astype(LOW))
-    grad_normed_one = dot(grad_projected, qkv_low, CONTRACT_LAST).astype(LOW)
-    grad_normed_one = sum_layer(grad_normed_one.reshape(team, count, width), 3)
-    grad_tokens = (grad_resid + normalize_back(flat, grad_normed_one)).reshape(units, length, width)
-    fed = dot(hidden, down_low, CONTRACT_LAST).astype(LOW)
-    fed = sum_layer(fed.reshape(team, count, width), 3)
-    out_tokens = (resid + fed).astype(LOW).reshape(units, length, width)
-
-    mlp_state, mlp_out = None, None
-    for grads, bases in ((down_grad, [2 * team]), (gate_grad, [0, team])):
-        *mlp_state, diff = adam_chunk(
-            trade(grads, 4 if len(bases) == 1 else 5),
-            mlp_master, mlp_first, mlp_second, bases, hid_share, mlp_state,
-        )
-        mlp_out = outer_chunk(
-            reps, diff, swap(diff), mlp_master, mlp_outer, bases, hid_share, mlp_out
-        )
-    bases = [0, team, 2 * team, 3 * team]
-    *att_state, diff = adam_chunk(
-        trade(att_grad, 4), att_master, att_first, att_second, bases, att_share, None
-    )
-    att_out = outer_chunk(reps, diff, swap(diff), att_master, att_outer, bases, att_share, None)
-    return (
+    (
         out_tokens,
         grad_tokens,
-        *(att_out[1], *att_state, att_out[0], att_out[2]),
-        *(mlp_out[1], *mlp_state, mlp_out[0], mlp_out[2]),
+        got_att,
+        got_gate,
+        got_down,
+        att_diff,
+        att_other,
+        mlp_diff,
+        mlp_other,
+        *_,
+    ) = backward_layer(
+        ranks,
+        (flat_low, resid, cot),
+        (att_master, att_first, att_second),
+        (mlp_master, mlp_first, mlp_second),
+        wide_cosine,
+        wide_sine,
+        bias,
+        grad_fed.reshape(all_tokens, width),
+        hidden.reshape(all_tokens, hid_share),
+        gate_value.reshape(all_tokens, hid_share),
+        up_value.reshape(all_tokens, hid_share),
+        normed_two.reshape(all_tokens, width),
+        normed_one.reshape(all_tokens, width),
+        projected,
+        mixed.reshape(all_tokens, att_share),
+        att_low,
+        gate_low,
+        down_low,
+    )
+    mlp = (mlp_master, mlp_first, mlp_second, mlp_outer, mlp_diff, mlp_other)
+    mlp_out = finish_chunk(reps, got_down, *mlp, [2], None)
+    mlp_out = finish_chunk(reps, got_gate, *mlp, [0, 1], mlp_out)
+    att_out = finish_chunk(
+        reps, got_att, att_master, att_first, att_second, att_outer, att_diff, att_other,
+        [0, 1, 2, 3], None,
+    )
+    return (
+        out_tokens.reshape(units, length, width),
+        grad_tokens.reshape(units, length, width),
+        *(att_out[3], att_out[0], att_out[1], att_out[2], att_out[4]),
+        *(mlp_out[3], mlp_out[0], mlp_out[1], mlp_out[2], mlp_out[4]),
     )
 
 

time: 1320 us -> 968 us (0.73)
  waiting for transfers between devices: 181 us -> 3.34 us
  matrix products: 124 us -> 0 us
  Pallas kernels: 872 us -> 933 us
  local copies, waits for them, and re-layouts: 55.9 us -> 3.8 us
  other arithmetic: 56.7 us -> 13.2 us
    ppermute x10 -> x7, waiting for transfers between devices: 181 us -> 3.34 us  [hop(): return lax.ppermute(values, ('rep', 'dp'), pairs)]
    dot_general x14 -> x0, matrix products: 124 us -> none  [the longest x9 120 us: dot(): return lax.dot_general(left, right, dims, preferred_element_type=FULL)]
    pallas_call x12 -> x4, Pallas kernels: 512 us -> 573 us  [the longest x1 508 us: backward_layer(): pl.pallas_call(functools.partial(backward_kernel, ranks), out_shape=[shap...]
    convert_element_type x7 -> x0, other arithmetic: 26.5 us -> none  [the longest x3 14 us: combine(): return kept.astype(LOW).reshape(team, rows, grad.shape[1])]
    convert_element_type x4 -> x0, local copies, waits for them, and re-layouts: 24.1 us -> none  [the longest x1 9.13 us: on_device(): gate_value = gate_value.reshape(all_tokens, hid_share).astype(FULL)]
  transfers between devices with their start and end apart: 13 -> 7, of which waited for: 3 -> 2; matrix products, arithmetic and copies ran while one was open for 8% -> 1% of each run, Pallas kernels for 31% -> 1%
where the time goes in v1:
time: 968 us; the launch traced here: 962 us
  Pallas kernels  933 us (96%)
  other arithmetic  13.2 us (1%)
    pallas_call x1, Pallas kernels, backward_layer(): pl.pallas_call(functools.partial(backward_kernel, ranks), out_shape=[shap...  508 us
    pallas_call x1, Pallas kernels, forward_layer(): pl.pallas_call(functools.partial(forward_kernel, ranks), out_shape=[shape...  353 us
    pallas_call x3, Pallas kernels, finish_chunk(): pl.pallas_call(functools.partial(finish_kernel, reps, share), grid=(parts...  65.7 us
  transfers between devices with their start and end apart: 7, of which 2 were waited for; matrix products, arithmetic and copies ran while one was open for 1% of the time, Pallas kernels for 1%

profile of v1, /device:TPU:0, one launch (start us, length us, event | category | flops | bytes accessed | tf_op | source)
XLA Modules:
  0.0 961.7 jit_solution(17656546430900409799)
XLA Ops:
  0.6 0.5 collective-permute-start
  1.2 2.6 collective-permute-start.1
  3.8 0.1 collective-permute-start.2
  3.8 1.8 collective-permute-start.3
  5.6 0.0 collective-permute-start.4
  5.7 0.8 copy.39
  6.5 1.4 convert_reduce_fusion
  7.9 1.6 fusion.2
  9.6 2.5 fusion.3.normed_own
  12.1 0.0 copy-start.2
  12.1 6.1 pack_shares.1.att_pack
  18.2 0.2 compare_and_fusion
  18.4 0.0 collective-permute-done
  18.4 0.0 copy-done.2
  18.4 2.7 collective-permute-start.5
  21.1 0.1 copy.40
  21.2 0.0 collective-permute-done.1
  21.2 0.1 collective-permute-start.6
  21.3 0.1 copy.41
  21.4 0.0 collective-permute-done.2
  21.4 0.1 copy.42
  21.5 0.0 collective-permute-done.3
  21.5 0.1 copy.43
  21.6 0.0 collective-permute-done.4
  21.6 0.1 copy.44
  21.7 1.3 collective-permute-done.5
  22.9 0.1 copy.45
  23.0 2.1 collective-permute-done.6
  25.1 0.1 copy.46
  25.2 0.1 stack.35
  25.3 0.1 select_reduce_fusion
  25.4 3.7 fusion.7
  29.1 1.6 fusion.6.bias
  30.7 1.9 maximum_bitcast_fusion
  32.6 353.3 %forward_layer.1 = (bf16[8,256,2048]{2,1,0:T(8,128)(2,1)}, bf16[8,256,2048]{2,1,0:T(8,128)(2,1)}, bf16[2048,1024]{1,0:T(8,128)(2,1)}, bf16[2048,2048]{1,0:T(8,12...) custom-call(bf16[256,2048]{1,0:T(8,128)(2,1)} %bitcast.30, ...), custom_call_target="tpu_custom_call" | custom-call | tf_op jit(solution)/shard_map/forward_layer/pallas_call | solution.py:623
  385.9 507.7 %backward_layer.1 = (bf16[256,2048]{1,0:T(8,128)(2,1)}, f32[256,2048]{1,0:T(8,128)}, bf16[16,128,1024]{2,1,0:T(8,128)(2,1)}, bf16[16,128,2048]{2,1,0:T(8,128)(2,...) custom-call(bf16[256,2048]{1,0:T(8,128)(2,1)} %bitcast.31, ...), custom_call_target="tpu_custom_call" | custom-call | tf_op jit(solution)/shard_map/backward_layer/pallas_call | solution.py:1264
  893.6 16.3 %finish_chunk.4 = (f32[1,128,24576]{2,1,0:T(8,128)}, f32[1,128,24576]{2,1,0:T(8,128)}, f32[128,24576]{1,0:T(8,128)}, f32[128,24576]{1,0:T(8,128)}, f32[128,24576]{1,0:T(8,128)}) custom-call(bf16[2,8,128,1024]{3,2,1,0:T(8,128)(2,1)} %bitcast.38, f32[128,24576]{1,0:T(8,128)} %master.5, f32[1,128,24576]{2,1,0:T(8,128)} %first.5, f32[1,128,24576]{2,1,0:T(8,128)} %second.5, ...), custom_call_target="tpu_custom_call" | custom-call | tf_op jit(solution)/shard_map/finish_chunk/pallas_call | solution.py:1346
  910.0 16.4 %finish_chunk.3 = (f32[1,128,8192]{2,1,0:T(8,128)}, f32[1,128,8192]{2,1,0:T(8,128)}, f32[128,8192]{1,0:T(8,128)}, f32[128,8192]{1,0:T(8,128)}, f32[128,8192]{1,0:T(8,128)}) custom-call(bf16[2,8,128,1024]{3,2,1,0:T(8,128)(2,1)} %bitcast.42, f32[128,8192]{1,0:T(8,128)} %master.3, f32[1,128,8192]{2,1,0:T(8,128)} %first.3, f32[1,128,8192]{2,1,0:T(8,128)} %second.3, ...), custom_call_target="tpu_custom_call" | custom-call | tf_op jit(solution)/shard_map/finish_chunk/pallas_call | solution.py:1346
  926.4 0.0 copy-start.1
  926.4 0.0 copy-start
  926.4 33.0 %finish_chunk.5 = (f32[1,128,24576]{2,1,0:T(8,128)}, f32[1,128,24576]{2,1,0:T(8,128)}, f32[128,24576]{1,0:T(8,128)}, f32[128,24576]{1,0:T(8,128)}, f32[128,24576]{1,0:T(8,128)}) custom-call(bf16[2,8,128,2048]{3,2,1,0:T(8,128)(2,1)} %bitcast.35, f32[128,24576]{1,0:T(8,128)} %master.5, ...), custom_call_target="tpu_custom_call", output_to_operand_aliasing={{0}: (7, {}), {1}: (8, {}), {2}: (9, {}), {3}: (10, {}), {4... | custom-call | tf_op jit(solution)/shard_map/finish_chunk/pallas_call | solution.py:1346
  959.4 0.0 copy-done.1
  959.4 1.0 copy.54
  960.3 0.0 copy-done
  960.3 1.3 copy.55
  (9 shorter events, 0.1 us)
Async XLA Ops:
  0.6 17.8 %collective-permute-start = (s32[1,2]{1,0:T(1,128)}, s32[1,2]{1,0:T(1,128)S(1)}, u32[]{:S(2)}, u32[]{:S(2)}) collective-permute-start(s32[1,2]{1,0:T(1,128)} %param.13), channel_id=1, source_target_pairs={{0,1},{1,0},{2,3},{3,2},{4,5},{5,4},{6,7},{7,6},{8,9},{9,8},{10,11... | collective-permute-start | bytes 32 | tf_op jit(solution)/shard_map/ppermute | solution.py:1392
  1.2 20.1 %collective-permute-start.1 = (s32[1,2]{1,0:T(1,128)}, s32[1,2]{1,0:T(1,128)S(1)}, u32[]{:S(2)}, u32[]{:S(2)}) collective-permute-start(s32[1,2]{1,0:T(1,128)} %param.13), channel_id=1, source_target_pairs={{0,2},{1,3},{2,0},{3,1},{4,6},{5,7},{6,4},{7,5},{8,10},{9,11},{10,... | collective-permute-start | bytes 32 | tf_op jit(solution)/shard_map/ppermute | solution.py:1392
  3.8 17.6 %collective-permute-start.2 = (s32[1,2]{1,0:T(1,128)}, s32[1,2]{1,0:T(1,128)S(1)}, u32[]{:S(2)}, u32[]{:S(2)}) collective-permute-start(s32[1,2]{1,0:T(1,128)} %param.13), channel_id=1, source_target_pairs={{0,3},{1,2},{2,1},{3,0},{4,7},{5,6},{6,5},{7,4},{8,11},{9,10},{10,... | collective-permute-start | bytes 32 | tf_op jit(solution)/shard_map/ppermute | solution.py:1392
  3.8 17.7 %collective-permute-start.3 = (s32[1,2]{1,0:T(1,128)}, s32[1,2]{1,0:T(1,128)S(1)}, u32[]{:S(2)}, u32[]{:S(2)}) collective-permute-start(s32[1,2]{1,0:T(1,128)} %param.13), channel_id=1, source_target_pairs={{0,4},{1,5},{2,6},{3,7},{4,0},{5,1},{6,2},{7,3},{8,12},{9,13},{10,... | collective-permute-start | bytes 32 | tf_op jit(solution)/shard_map/ppermute | solution.py:1392
  5.6 16.0 %collective-permute-start.4 = (s32[1,2]{1,0:T(1,128)}, s32[1,2]{1,0:T(1,128)S(1)}, u32[]{:S(2)}, u32[]{:S(2)}) collective-permute-start(s32[1,2]{1,0:T(1,128)} %param.13), channel_id=1, source_target_pairs={{0,5},{1,4},{2,7},{3,6},{4,1},{5,0},{6,3},{7,2},{8,13},{9,12},{10,... | collective-permute-start | bytes 32 | tf_op jit(solution)/shard_map/ppermute | solution.py:1392
  12.1 6.3 copy-start.2
  18.4 4.5 collective-permute-start.5
  21.2 3.9 collective-permute-start.6
  926.4 33.0 %copy-start.1 = (bf16[256,2048]{1,0:T(8,128)(2,1)S(1)}, bf16[256,2048]{1,0:T(8,128)(2,1)}, u32[]{:S(2)}) copy-start(bf16[256,2048]{1,0:T(8,128)(2,1)} %get-tuple-element.60) | copy-start | bytes 3145732
  926.4 34.0 %copy-start = (f32[256,2048]{1,0:T(8,128)S(1)}, f32[256,2048]{1,0:T(8,128)}, u32[]{:S(2)}) copy-start(f32[256,2048]{1,0:T(8,128)} %get-tuple-element.61) | copy-start | bytes 6291460

commit v2 on v1

--- a/solution.py
+++ b/solution.py
@@ -104,9 +104,11 @@
 ANYWHERE = pl.BlockSpec(memory_space=pl.ANY)
 BITS = (1, 2, 4)
 PIECES = 4
+FEED_EARLY = 6
+SPLIT_TOKENS, SPLIT_ATTENDED, SPLIT_NORMED, SPLIT_COT, SPLIT_BACK = 3, 3, 3, 3, 3
 STRIP = 16
 GATHER_COPIES = 6 * PIECES + 1
-VMEM_BYTES = 56 * 1024 * 1024
+VMEM_BYTES = 60 * 1024 * 1024
 
 
 def flip(me, bit):
@@ -153,14 +155,15 @@
 
 
 class TeamGather:
-    def __init__(self, me, own, out, send):
-        self.out, self.send = out, send
+    def __init__(self, me, own, out, send, split):
+        self.out, self.send, self.split = out, send, split
         self.piece = own.shape[0] // PIECES
         self.core, self.second, self.third = ({"dp": flip(me, bit)} for bit in BITS)
-        self.late = list(range(PIECES // 2, PIECES)) + list(range(PIECES // 2))
+        self.late = list(range(split, PIECES)) + list(range(split))
         self.early = list(range(PIECES))
         self.own = own
-        self.over_second, self.over_third, self.rest = {}, {}, []
+        self.over_second, self.over_third, self.corner = {}, {}, {}
+        self.rest, self.settled = [], []
 
     def cut(self, ref, p):
         return ref.at[pl.ds(p * self.piece, self.piece)]
@@ -172,28 +175,33 @@
             self.over_third[b] = self.send(cut(own, b), cut(out.at[4], b), self.third)
         self.rest.append(self.send(own, out.at[1], self.core))
 
-    def finish(self, middle=None):
+    def turn(self):
         out, cut, send = self.out, self.cut, self.send
-        half = PIECES // 2
-        corner = {}
         for a, b in zip(self.late, self.early):
             self.over_second[a].wait_recv()
-            if a >= half:
-                corner[a] = send(cut(out.at[2], a), cut(out.at[6], a), self.third)
+            if a >= self.split:
+                self.corner[a] = send(cut(out.at[2], a), cut(out.at[6], a), self.third)
             self.rest.append(send(cut(out.at[2], a), cut(out.at[3], a), self.core))
             self.over_third[b].wait_recv()
-            if b < half:
-                corner[b] = send(cut(out.at[4], b), cut(out.at[6], b), self.second)
+            if b < self.split:
+                self.corner[b] = send(cut(out.at[4], b), cut(out.at[6], b), self.second)
             self.rest.append(send(cut(out.at[4], b), cut(out.at[5], b), self.core))
-        if middle is not None:
-            middle()
-        for p in range(half):
-            for q in (p, p + half):
-                corner[q].wait_recv()
-                self.rest.append(send(cut(out.at[6], q), cut(out.at[7], q), self.core))
-        for group in (self.over_second, self.over_third, corner):
+
+    def settle(self):
+        for copy in self.rest:
+            copy.wait_recv()
+        self.settled, self.rest = self.rest, []
+
+    def finish(self):
+        for p, copy in self.corner.items():
+            copy.wait_recv()
+            at = self.cut(self.out.at[6], p), self.cut(self.out.at[7], p)
+            self.rest.append(self.send(*at, self.core))
+        for group in (self.over_second, self.over_third, self.corner):
             for copy in group.values():
                 copy.wait_send()
+        for copy in self.settled:
+            copy.wait_send()
         for copy in self.rest:
             copy.wait()
 
@@ -209,7 +217,7 @@
     ]
 
 
-def team_sum(me, parts, own, got, edge, send, loads, total, between=None, after=None):
+def team_sum(me, parts, own, got, edge, send, loads, total, split):
     core = {"dp": flip(me, 1)}
     loading = [pltpu.make_async_copy(parts.at[2 * j], own.at[j], loads.at[j]) for j in range(4)]
     first = {}
@@ -218,65 +226,68 @@
         first[j] = send(parts.at[2 * j + 1], got.at[j], core)
     for copy in loading:
         copy.wait()
-    sum_steps(me, own, got, edge, first, send, total, between, after)
-
-
-def sum_steps(me, own, got, edge, first, send, total, between=None, after=None):
+    yield from sum_steps(me, own, got, edge, first, send, total, split)
+
+
+def sum_steps(me, own, got, edge, first, send, total, split):
     count = own.shape[1]
-    half = count // 2
     _, second, third = ({"dp": flip(me, bit)} for bit in BITS)
-
-    def cut(ref, h):
-        return ref.at[pl.ds(h * half, half)]
+    spans = [pl.ds(0, split), pl.ds(split, count - split)]
 
     def add(j, h, extra=None):
-        @pl.loop(0, half // STRIP)
+        span = spans[h]
+
+        @pl.loop(0, span.size // STRIP)
         def _(step):
-            at = pl.ds(h * half + step * STRIP, STRIP)
+            at = pl.ds(span.start + step * STRIP, STRIP)
             value = own[j, at].astype(FULL) + got[j, at].astype(FULL)
             if extra is not None:
                 value = value + extra[at].astype(FULL)
             own[j, at] = value.astype(LOW)
 
+    def go(j, h, slot, where):
+        return send(own.at[j].at[spans[h]], edge.at[slot].at[spans[h]], where)
+
+    both = split < count
+    sends = []
     first[3].wait_recv()
     add(3, 0)
-    corner_second = send(cut(own.at[3], 0), cut(edge.at[0], 0), second)
-    add(3, 1)
-    corner_third = send(cut(own.at[3], 1), cut(edge.at[0], 1), third)
-    first[2].wait_recv()
-    add(2, 1)
-    third_late = send(cut(own.at[2], 1), cut(edge.at[2], 1), third)
+    corner_second = go(3, 0, 0, second)
+    if both:
+        add(3, 1)
+        corner_third = go(3, 1, 0, third)
+        sends.append(corner_third)
+        first[2].wait_recv()
+        add(2, 1)
+        sends.append(go(2, 1, 2, third))
     first[1].wait_recv()
     add(1, 0)
-    second_early = send(cut(own.at[1], 0), cut(edge.at[1], 0), second)
-    if between is not None:
-        between()
+    sends.append(go(1, 0, 1, second))
+    yield
+    if not both:
+        first[2].wait_recv()
     corner_second.wait_recv()
     add(2, 0, edge.at[0])
-    third_early = send(cut(own.at[2], 0), cut(edge.at[2], 0), third)
-    corner_third.wait_recv()
-    add(1, 1, edge.at[0])
-    second_late = send(cut(own.at[1], 1), cut(edge.at[1], 1), second)
-    if after is not None:
-        after()
+    sends.append(go(2, 0, 2, third))
+    if both:
+        corner_third.wait_recv()
+        add(1, 1, edge.at[0])
+        sends.append(go(1, 1, 1, second))
+    yield
     first[0].wait_recv()
-    for h, waits in ((0, (second_early, third_early)), (1, (third_late, second_late))):
-        for copy in waits:
+    for copy in sends:
+        if not both or copy is not corner_third:
             copy.wait_recv()
 
-        @pl.loop(0, half // STRIP)
-        def _(step, h=h):
-            start = h * half + step * STRIP
-            at = pl.ds(start, STRIP)
-            value = own[0, at].astype(FULL) + got[0, at].astype(FULL)
-            total(start, value + edge[1, at].astype(FULL) + edge[2, at].astype(FULL))
-
-    for copy in (
-        corner_second, corner_third, third_late, second_early, third_early, second_late
-    ):
+    @pl.loop(0, count // STRIP)
+    def _(step):
+        start = step * STRIP
+        at = pl.ds(start, STRIP)
+        value = own[0, at].astype(FULL) + got[0, at].astype(FULL)
+        total(start, value + edge[1, at].astype(FULL) + edge[2, at].astype(FULL))
+
+    for copy in sends + [corner_second] + [first[j] for j in range(4)]:
         copy.wait_send()
-    for j in range(4):
-        first[j].wait_send()
 
 
 def params(collective_id):
@@ -290,6 +301,56 @@
     centre = value - jnp.sum(value, axis=1, keepdims=True) * (1.0 / width)
     factor = lax.rsqrt(jnp.sum(centre * centre, axis=1, keepdims=True) * (1.0 / width) + LN_EPS)
     return (centre * factor, factor)
+
+
+UNIT = 256
+
+
+def unit_of(step):
+    return 2 * (TEAM // 2 - 1 - step % (TEAM // 2)) + jnp.where(step < TEAM // 2, 1, 0)
+
+
+def stream(steps, loads, body, arrive=None):
+    if arrive is not None:
+        arrive(0)
+    for copy in loads(0, 0):
+        copy.start()
+
+    @pl.loop(0, steps)
+    def _(step):
+        slot = step % 2
+
+        @pl.when(step + 1 < steps)
+        def _():
+            if arrive is not None:
+                arrive(step + 1)
+            for copy in loads(step + 1, 1 - slot):
+                copy.start()
+
+        for copy in loads(step, slot):
+            copy.wait()
+        body(step, slot)
+
+
+def stream_out(steps, loads, stores, body):
+    def whole(step, slot):
+        @pl.when(step >= 2)
+        def _():
+            for copy in stores(step - 2, slot):
+                copy.wait()
+
+        body(step, slot)
+        for copy in stores(step, slot):
+            copy.start()
+
+    stream(steps, loads, whole)
+    for step in (steps - 2, steps - 1):
+        for copy in stores(step, step % 2):
+            copy.wait()
+
+
+def rows_at(step, size):
+    return pl.ds(pl.multiple_of(step * size, size), size)
 
 
 class RowGather:
@@ -299,30 +360,36 @@
         self.rows = weights.shape[0] // ranks
         self.half = self.rows // 2
         self.order = list(range(TEAM, ranks)) + list(range(1, TEAM))
+        self.ways, self.swaps = {}, []
+        near = [other for other in self.order if other < 4]
+        self.turns = near + [other for other in self.order if other >= 4]
 
     def place(self, device):
         return self.weights.at[pl.ds(device * self.rows + self.rep * self.half, self.half)]
 
-    def begin(self, pack):
+    def begin(self, pack, number=None):
         me, rep = self.me, self.rep
-        at = self.weights.at[pl.ds(me * self.rows, self.rows)]
-        self.own = pltpu.make_async_copy(pack.at[me % TEAM], at, self.local)
-        self.own.start()
-        self.ways = []
-        for other in self.order:
+        if not self.ways:
+            at = self.weights.at[pl.ds(me * self.rows, self.rows)]
+            self.own = pltpu.make_async_copy(pack.at[me % TEAM], at, self.local)
+            self.own.start()
+        started = len(self.ways)
+        number = len(self.order) - started if number is None else number
+        for other in self.order[started : started + number]:
             where = across(me, other)
             source = pack.at[where % TEAM, pl.ds(rep * self.half, self.half)]
-            self.ways.append(self.send(source, self.place(me), {"dp": where}))
-
-    def forward(self):
-        self.swaps = []
-        for other, copy in zip(self.order, self.ways):
-            copy.wait_recv()
+            self.ways[other] = self.send(source, self.place(me), {"dp": where})
+
+    def forward(self, number=None):
+        done = len(self.swaps)
+        number = len(self.order) - done if number is None else number
+        for other in self.turns[done : done + number]:
+            self.ways[other].wait_recv()
             at = self.place(across(self.me, other))
             self.swaps.append(self.send_x(at, at, {"rep": 1 - self.rep}))
 
     def finish(self):
-        for copy in self.ways:
+        for copy in self.ways.values():
             copy.wait_send()
         for copy in self.swaps + [self.own]:
             copy.wait()
@@ -394,7 +461,7 @@
     send = Sender(sent_team, came_team)
     send_rows = Sender(sent_rows, came_rows)
     send_x = Sender(sent_x, came_x)
-    tokens = TeamGather(me, normed_own, normed_all, send)
+    tokens = TeamGather(me, normed_own, normed_all, send, SPLIT_TOKENS)
     tokens.begin()
     gathers = [
         RowGather(ranks, me, rep, weights, send_rows, send_x, local.at[i])
@@ -410,55 +477,43 @@
         def loads(t, slot):
             return [
                 pltpu.make_async_copy(
-                    mlp_master.at[:, pl.ds((p * TEAM + t) * hid, hid)],
+                    mlp_master.at[:, rows_at(p * TEAM + t, hid)],
                     wide.at[slot, p],
                     local.at[5 + 3 * slot + p],
                 )
                 for p in range(3)
             ]
 
-        for copy in loads(0, 0):
-            copy.start()
-
-        @pl.loop(0, TEAM)
-        def _(t):
-            slot = t % 2
-
-            @pl.when(t + 1 < TEAM)
-            def _():
-                for copy in loads(t + 1, 1 - slot):
-                    copy.start()
-
-            for copy in loads(t, slot):
-                copy.wait()
-            low[:, : 2 * hid] = jnp.concatenate(
-                [wide[slot, 0].astype(LOW), wide[slot, 1].astype(LOW)], axis=1
-            )
-            low[:, 2 * hid :] = wide[slot, 2].astype(LOW)
-            out_copies = [
-                pltpu.make_async_copy(low.at[:, pl.ds(0, 2 * hid)], gate_pack.at[t], local.at[11]),
-                pltpu.make_async_copy(low.at[:, pl.ds(2 * hid, hid)], down_pack.at[t], local.at[12]),
+        def stores(t, slot):
+            near = low.at[slot]
+            return [
+                pltpu.make_async_copy(
+                    near.at[:, pl.ds(0, 2 * hid)], gate_pack.at[t], local.at[11 + slot]
+                ),
+                pltpu.make_async_copy(
+                    near.at[:, pl.ds(2 * hid, hid)], down_pack.at[t], local.at[13 + slot]
+                ),
             ]
-            for copy in out_copies:
-                copy.start()
-            for copy in out_copies:
-                copy.wait()
+
+        def body(t, slot):
+            for p in range(3):
+                low[slot, :, p * hid : (p + 1) * hid] = wide[slot, p].astype(LOW)
+
+        stream_out(TEAM, loads, stores, body)
 
     pl.run_scoped(
-        pack, pltpu.VMEM((2, 3, rows, hid), FULL), pltpu.VMEM((rows, 3 * hid), LOW)
-    )
-    tokens.finish()
+        pack, pltpu.VMEM((2, 3, rows, hid), FULL), pltpu.VMEM((2, rows, 3 * hid), LOW)
+    )
+    tokens.turn()
     gathers[1].begin(gate_pack)
     gathers[0].forward()
+    tokens.finish()
     gathers[0].finish()
     for copy in keep:
         copy.wait()
     load = pltpu.make_async_copy(att_weights, att, local.at[0])
     load.start()
     load.wait()
-
-    def unit_of(step):
-        return 2 * (TEAM // 2 - 1 - step % (TEAM // 2)) + jnp.where(step < TEAM // 2, 1, 0)
 
     def fetch(step, slot):
         return pltpu.make_async_copy(
@@ -518,56 +573,48 @@
         resid[at] = value
         normed[at] = strip_normalize(value)[0].astype(LOW)
 
-    sum_steps(me, own, got, edge, first, send, total, gathers[1].forward)
-    tokens = TeamGather(me, normed, normed_two_all, send)
+    steps = sum_steps(me, own, got, edge, first, send, total, SPLIT_ATTENDED * UNIT // PIECES)
+    next(steps)
+    early = len(gathers[2].order) // 2
+    gathers[2].begin(down_pack, early)
+    gathers[1].forward()
+    next(steps)
+    for _ in steps:
+        pass
+    tokens = TeamGather(me, normed, normed_two_all, send, SPLIT_NORMED)
     tokens.begin()
+    gathers[2].begin(down_pack)
+    cots = TeamGather(me, cot, cot_all, send, SPLIT_COT)
+    cots.begin()
     keep = pltpu.make_async_copy(normed, normed_two_all.at[0], local.at[3])
     keep.start()
-    tokens.finish()
-    cots = TeamGather(me, cot, cot_all, send)
-    cots.begin()
-    gathers[2].begin(down_pack)
+    gathers[2].forward(early)
+    tokens.turn()
     keep.wait()
     gathers[1].finish()
+    tokens.settle()
     load = pltpu.make_async_copy(gate_weights, gate, local.at[1])
     load.start()
     load.wait()
 
-    def feed(low):
-        def fetch(unit, slot):
-            return pltpu.make_async_copy(
-                normed_two_all.at[unit], block.at[slot], local.at[5 + slot]
-            )
-
-        def stores(unit, slot):
+    def feed(base, low):
+        def loads(step, slot):
+            source = normed_two_all.at[base + step]
+            return [pltpu.make_async_copy(source, block.at[slot], local.at[5 + slot])]
+
+        def stores(step, slot):
             return [
-                pltpu.make_async_copy(low.at[slot, i], out.at[unit], local.at[7 + 3 * slot + i])
+                pltpu.make_async_copy(
+                    low.at[slot, i], out.at[base + step], local.at[7 + 3 * slot + i]
+                )
                 for i, out in enumerate((gate_all, up_all, hidden_all))
             ]
 
-        fetch(0, 0).start()
-
-        @pl.loop(0, TEAM)
-        def _(unit):
-            slot = unit % 2
-
-            @pl.when(unit + 1 < TEAM)
-            def _():
-                fetch(unit + 1, 1 - slot).start()
-
-            fetch(unit, slot).wait()
-
-            @pl.when(unit >= 2)
-            def _():
-                for copy in stores(unit - 2, slot):
-                    copy.wait()
-
-            tile = 256
-
-            @pl.loop(0, hid // tile)
+        def body(step, slot):
+            @pl.loop(0, hid // UNIT)
             def _(column):
-                at = pl.ds(pl.multiple_of(column * tile, tile), tile)
-                later = pl.ds(pl.multiple_of(hid + column * tile, tile), tile)
+                at = rows_at(column, UNIT)
+                later = pl.ds(pl.multiple_of(hid + column * UNIT, UNIT), UNIT)
                 gate_value = dot(block[slot], gate[:, at])
                 up_value = dot(block[slot], gate[:, later])
                 low[slot, 0, :, at] = gate_value.astype(LOW)
@@ -575,16 +622,15 @@
                 hidden = gate_value * jax.nn.sigmoid(gate_value) * up_value
                 low[slot, 2, :, at] = hidden.astype(LOW)
 
-            for copy in stores(unit, slot):
-                copy.start()
-
-        for unit in (TEAM - 2, TEAM - 1):
-            for copy in stores(unit, unit % 2):
-                copy.wait()
-
-    pl.run_scoped(feed, pltpu.VMEM((2, 3, normed.shape[0], hid), LOW))
+        stream_out(FEED_EARLY if base == 0 else TEAM - FEED_EARLY, loads, stores, body)
+
+    fed = pltpu.VMEM((2, 3, normed.shape[0], hid), LOW)
+    pl.run_scoped(functools.partial(feed, 0), fed)
+    tokens.finish()
+    cots.turn()
+    gathers[2].forward()
+    pl.run_scoped(functools.partial(feed, FEED_EARLY), fed)
     cots.finish()
-    gathers[2].forward()
     gathers[2].finish()
 
 
@@ -619,7 +665,7 @@
         (hidden, ANYWHERE),
     ]
     team_copies = 3 * GATHER_COPIES + SUM_COPIES
-    pairs = [team_copies] * 2 + [3 * (ranks - 1)] * 4 + [TEAM // 2] * 2 + [13]
+    pairs = [team_copies] * 2 + [3 * (ranks - 1)] * 4 + [TEAM // 2] * 2 + [15]
     return pl.pallas_call(
         functools.partial(forward_kernel, ranks),
         out_shape=[shape for shape, _ in out],
@@ -666,13 +712,6 @@
     return jnp.concatenate(grads[0] + grads[1] + grads[2], axis=1)
 
 
-UNIT = 256
-
-
-def unit_of(step):
-    return 2 * (TEAM // 2 - 1 - step % (TEAM // 2)) + jnp.where(step < TEAM // 2, 1, 0)
-
-
 class Terms:
     def __init__(self, me, odd, own, got, sent, came):
         self.odd, self.own, self.got, self.sent, self.came = odd, own, got, sent, came
@@ -704,43 +743,7 @@
         return [self.copy(j) for j in range(TEAM // 2)]
 
 
-def stream(steps, loads, body):
-    for copy in loads(0, 0):
-        copy.start()
-
-    @pl.loop(0, steps)
-    def _(step):
-        slot = step % 2
-
-        @pl.when(step + 1 < steps)
-        def _():
-            for copy in loads(step + 1, 1 - slot):
-                copy.start()
-
-        for copy in loads(step, slot):
-            copy.wait()
-        body(step, slot)
-
-
-def stream_out(steps, loads, stores, body):
-    def whole(step, slot):
-        @pl.when(step >= 2)
-        def _():
-            for copy in stores(step - 2, slot):
-                copy.wait()
-
-        body(step, slot)
-        for copy in stores(step, slot):
-            copy.start()
-
-    stream(steps, loads, whole)
-    for step in (steps - 2, steps - 1):
-        for copy in stores(step, step % 2):
-            copy.wait()
-
-
-def rows_at(step, size):
-    return pl.ds(pl.multiple_of(step * size, size), size)
+LOWS = (0, 4, 2, 6, 1, 5, 3, 7)
 
 
 def backward_kernel(
@@ -762,9 +765,6 @@
     att_weights,
     gate_weights,
     down_weights,
-    att_master,
-    att_first,
-    att_second,
     mlp_master,
     mlp_first,
     mlp_second,
@@ -773,8 +773,6 @@
     got_att,
     got_gate,
     got_down,
-    att_diff,
-    att_other,
     mlp_diff,
     mlp_other,
     grad_all,
@@ -792,6 +790,7 @@
     grad_low,
     grad_resid,
     stage,
+    wide,
     sent,
     came,
     sent_rows,
@@ -815,7 +814,7 @@
     greet(me, range(1, ranks), True)
     send = Sender(sent, came)
     order = []
-    for low_bits in range(TEAM):
+    for low_bits in LOWS:
         order += [top * TEAM + low_bits for top in range(1, tops)]
         order += [low_bits] if low_bits else []
 
@@ -869,6 +868,111 @@
         block_copy(0, other).start()
     own_copies = [keep_own(down_grad, got_down, 0)]
 
+    gate_order = list(order)
+
+    def more(number):
+        for _ in range(min(number, len(gate_order))):
+            block_copy(1, gate_order.pop(0)).start()
+
+    terms = Terms(me, odd, own, got, sent_first.at[0], came_first.at[0])
+
+    grad_gate = wide.at[pl.ds(0, tokens), pl.ds(0, 2 * hid)]
+
+    def hidden_phase(down, block, gate, up):
+        whole = pltpu.make_async_copy(down_weights, down, local.at[1])
+        whole.start()
+
+        def loads(step, slot):
+            at = rows_at(step, count)
+            return [
+                pltpu.make_async_copy(cot_all.at[at], block.at[slot], local.at[2 + slot]),
+                pltpu.make_async_copy(gate_all.at[at], gate.at[slot], local.at[4 + slot]),
+                pltpu.make_async_copy(up_all.at[at], up.at[slot], local.at[6 + slot]),
+            ]
+
+        def body(step, slot):
+            at = rows_at(step, count)
+
+            @pl.loop(0, hid // UNIT)
+            def _(column):
+                place = rows_at(column, UNIT)
+                later = pl.ds(pl.multiple_of(hid + column * UNIT, UNIT), UNIT)
+                grad = dot(block[slot], down[:, place])
+                value = gate[slot, :, place].astype(FULL)
+                sigmoid = jax.nn.sigmoid(value)
+                slope = sigmoid * (1.0 + value * (1.0 - sigmoid))
+                up_value = up[slot, :, place].astype(FULL)
+                grad_gate[at, place] = (grad * up_value * slope).astype(LOW)
+                grad_gate[at, later] = (grad * value * sigmoid).astype(LOW)
+
+        whole.wait()
+        stream(TEAM, loads, body)
+
+    pl.run_scoped(
+        hidden_phase,
+        pltpu.VMEM((width, hid), LOW),
+        pltpu.VMEM((2, count, width), LOW),
+        pltpu.VMEM((2, count, hid), LOW),
+        pltpu.VMEM((2, count, hid), LOW),
+    )
+
+    def back_phase(gate):
+        whole = pltpu.make_async_copy(gate_weights, gate, local.at[0])
+        whole.start()
+        whole.wait()
+
+        @pl.loop(0, TEAM)
+        def _(step):
+            at = rows_at(unit_of(step), count)
+            terms.put(step, dot(grad_gate[at, :], gate[...], CONTRACT_LAST).astype(LOW))
+
+    pl.run_scoped(back_phase, pltpu.VMEM((width, 2 * hid), LOW))
+
+    def weight_phase(tile, low):
+        def loads(step, slot):
+            at = rows_at(step, UNIT)
+            return [
+                pltpu.make_async_copy(
+                    normed_two_all.at[:, at], tile.at[slot], local.at[2 + slot]
+                )
+            ]
+
+        def stores(step, slot):
+            at = rows_at(step, UNIT)
+            return [pltpu.make_async_copy(low.at[slot], gate_grad.at[at], local.at[4 + slot])]
+
+        def body(step, slot):
+            low[slot] = dot(tile[slot], grad_gate[...], CONTRACT_FIRST).astype(LOW)
+
+        stream_out(tiles, loads, stores, body)
+
+
+    def resid_total(start, value):
+        at = pl.ds(start, STRIP)
+        normed, factor = strip_normalize(resid[at])
+        along = jnp.sum(value * normed, axis=1, keepdims=True) * (1.0 / width)
+        middle = jnp.sum(value, axis=1, keepdims=True) * (1.0 / width)
+        value = cot[at].astype(FULL) + factor * (value - middle - normed * along)
+        grad_resid[at] = value
+        grad_low[at] = value.astype(LOW)
+
+    split = SPLIT_BACK * UNIT // PIECES
+    steps = sum_steps(me, own, got, edge, terms.first(), send, resid_total, split)
+    next(steps)
+    pl.run_scoped(
+        weight_phase, pltpu.VMEM((2, tokens, UNIT), LOW), pltpu.VMEM((2, UNIT, 2 * hid), LOW)
+    )
+    own_copies.append(keep_own(gate_grad, got_gate, 1))
+    more(GATE_FIRST)
+    next(steps)
+    more(GATE_LATE)
+    for _ in steps:
+        pass
+    gather = TeamGather(me, grad_low, grad_all, send, SPLIT_BACK)
+    gather.begin()
+    more(GATE_GATHER)
+    keep = pltpu.make_async_copy(grad_low, grad_all.at[0], local.at[8])
+    keep.start()
     def fed_phase(hidden, down, term):
         whole = [
             pltpu.make_async_copy(hidden_all, hidden, local.at[0]),
@@ -893,117 +997,17 @@
         pltpu.VMEM((width, hid), LOW),
         pltpu.VMEM((2, count, width), LOW),
     )
-    gate_order = list(order)
-
-    def more(number):
-        def some():
-            for _ in range(min(number, len(gate_order))):
-                block_copy(1, gate_order.pop(0)).start()
-
-        return some
-
-    terms = Terms(me, odd, own, got, sent_first.at[0], came_first.at[0])
-
-    def gate_phase(grad_gate):
-        def hidden_phase(down, block, gate, up):
-            whole = pltpu.make_async_copy(down_weights, down, local.at[1])
-            whole.start()
-
-            def loads(step, slot):
-                at = rows_at(step, count)
-                return [
-                    pltpu.make_async_copy(cot_all.at[at], block.at[slot], local.at[2 + slot]),
-                    pltpu.make_async_copy(gate_all.at[at], gate.at[slot], local.at[4 + slot]),
-                    pltpu.make_async_copy(up_all.at[at], up.at[slot], local.at[6 + slot]),
-                ]
-
-            def body(step, slot):
-                at = rows_at(step, count)
-
-                @pl.loop(0, hid // UNIT)
-                def _(column):
-                    place = rows_at(column, UNIT)
-                    later = pl.ds(pl.multiple_of(hid + column * UNIT, UNIT), UNIT)
-                    grad = dot(block[slot], down[:, place])
-                    value = gate[slot, :, place].astype(FULL)
-                    sigmoid = jax.nn.sigmoid(value)
-                    slope = sigmoid * (1.0 + value * (1.0 - sigmoid))
-                    up_value = up[slot, :, place].astype(FULL)
-                    grad_gate[at, place] = (grad * up_value * slope).astype(LOW)
-                    grad_gate[at, later] = (grad * value * sigmoid).astype(LOW)
-
-            whole.wait()
-            stream(TEAM, loads, body)
-
-        pl.run_scoped(
-            hidden_phase,
-            pltpu.VMEM((width, hid), LOW),
-            pltpu.VMEM((2, count, width), LOW),
-            pltpu.VMEM((2, count, hid), LOW),
-            pltpu.VMEM((2, count, hid), LOW),
-        )
-
-        def weight_phase(tile, low):
-            def loads(step, slot):
-                at = rows_at(step, UNIT)
-                return [
-                    pltpu.make_async_copy(
-                        normed_two_all.at[:, at], tile.at[slot], local.at[2 + slot]
-                    )
-                ]
-
-            def stores(step, slot):
-                at = rows_at(step, UNIT)
-                return [pltpu.make_async_copy(low.at[slot], gate_grad.at[at], local.at[4 + slot])]
-
-            def body(step, slot):
-                low[slot] = dot(tile[slot], grad_gate[...], CONTRACT_FIRST).astype(LOW)
-
-            stream_out(tiles, loads, stores, body)
-
-        pl.run_scoped(
-            weight_phase, pltpu.VMEM((2, tokens, UNIT), LOW), pltpu.VMEM((2, UNIT, 2 * hid), LOW)
-        )
-        more(GATE_FIRST)()
-
-        def back_phase(gate):
-            whole = pltpu.make_async_copy(gate_weights, gate, local.at[0])
-            whole.start()
-            whole.wait()
-
-            @pl.loop(0, TEAM)
-            def _(step):
-                at = rows_at(unit_of(step), count)
-                terms.put(step, dot(grad_gate[at], gate[...], CONTRACT_LAST).astype(LOW))
-
-        pl.run_scoped(back_phase, pltpu.VMEM((width, 2 * hid), LOW))
-
-    pl.run_scoped(gate_phase, pltpu.VMEM((tokens, 2 * hid), LOW))
-    own_copies.append(keep_own(gate_grad, got_gate, 1))
-
-    def resid_total(start, value):
-        at = pl.ds(start, STRIP)
-        normed, factor = strip_normalize(resid[at])
-        along = jnp.sum(value * normed, axis=1, keepdims=True) * (1.0 / width)
-        middle = jnp.sum(value, axis=1, keepdims=True) * (1.0 / width)
-        value = cot[at].astype(FULL) + factor * (value - middle - normed * along)
-        grad_resid[at] = value
-        grad_low[at] = value.astype(LOW)
-
-    sum_steps(
-        me, own, got, edge, terms.first(), send, resid_total, more(GATE_EARLY), more(GATE_LATE)
-    )
-    gather = TeamGather(me, grad_low, grad_all, send)
-    gather.begin()
-    more(GATE_GATHER)()
-    keep = pltpu.make_async_copy(grad_low, grad_all.at[0], local.at[0])
-    keep.start()
-    gather.finish(more(len(gate_order)))
+    gather.turn()
+    more(len(gate_order))
+    gather.finish()
     keep.wait()
 
     terms = Terms(me, odd, own, got, sent_first.at[1], came_first.at[1])
 
-    def att_phase(att, grad_projected):
+    def att_phase():
+        att = wide.at[pl.ds(0, width), pl.ds(0, 4 * share)]
+        grad_projected = wide.at[pl.ds(0, tokens), pl.ds(4 * share, 3 * share)]
+
         def unit_phase(block, projected, tables, mask):
             def loads(step, slot):
                 unit = unit_of(step)
@@ -1022,7 +1026,7 @@
                 grads = attend_unit_back(
                     projected[slot], given, tables[slot, 0], tables[slot, 1], mask[slot], share
                 )
-                grad_projected[rows_at(unit_of(step), count)] = grads
+                grad_projected[rows_at(unit_of(step), count), :] = grads
                 terms.put(step, dot(grads, att[:, : 3 * share], CONTRACT_LAST).astype(LOW))
 
             whole = pltpu.make_async_copy(att_weights, att, local.at[10])
@@ -1073,133 +1077,120 @@
             pltpu.VMEM((2, UNIT, 4 * share), LOW),
         )
 
-    pl.run_scoped(
-        att_phase, pltpu.VMEM((width, 4 * share), LOW), pltpu.VMEM((tokens, 3 * share), LOW)
-    )
+    att_phase()
     for other in order:
         block_copy(2, other).start()
     own_copies.append(keep_own(att_grad, got_att, 2))
 
-    def differ(chunk, pieces, states, diff, other, column, mates):
-        master, first, second = states
-        each = hid // mates
-
-        def near(block):
+    def mate_at(low):
+        mate = 0
+        for bit in BITS:
+            mine, its = (me // bit) % 2, (low // bit) % 2
+            mate = mate + bit * (mine + its - 2 * mine * its)
+        return mate
+
+    def differ(chunk, parts, first_part, base):
+        source = chunks[chunk][1]
+
+        def low_at(step):
+            turn = step // parts
+            return 4 * (turn % 2) + 2 * ((turn // 2) % 2) + turn // 4
+
+        def column(step):
+            return rows_at((first_part + step % parts) * TEAM + mate_at(low_at(step)), hid)
+
+        def near(step):
+            at = column(step)
             return pltpu.make_async_copy(
-                stage.at[block], diff.at[:, column(block)], kept.at[3 + block]
+                stage.at[step % 2], mlp_diff.at[:, at], kept.at[3 + step % 2]
             )
 
-        def far(block):
-            index = chunk * TEAM + block
+        def far(step):
+            at = column(step)
             return pltpu.make_async_remote_copy(
-                src_ref=stage.at[block],
-                dst_ref=other.at[:, column(block)],
-                send_sem=sent_x.at[index],
-                recv_sem=came_x.at[index],
+                src_ref=mlp_diff.at[:, at],
+                dst_ref=mlp_other.at[:, at],
+                send_sem=sent_x.at[base + step],
+                recv_sem=came_x.at[base + step],
                 device_id={"rep": 1 - rep},
                 device_id_type=MESH,
             )
 
-        def run(wide, low):
-            def loads(block, slot):
-                at = column(block)
+        def arrive(step):
+            low = low_at(step)
+
+            @pl.when(step % parts == 0)
+            def _():
+                for top in range(tops):
+                    index = chunk * (ranks - 1) + top * TEAM + low - 1
+
+                    def wait():
+                        pltpu.make_async_remote_copy(
+                            src_ref=source.at[me],
+                            dst_ref=source.at[me],
+                            send_sem=sent_rows.at[index],
+                            recv_sem=came_rows.at[index],
+                            device_id={"dp": flip(me, 1)},
+                            device_id_type=MESH,
+                        ).wait_recv()
+
+                    if top:
+                        wait()
+                    else:
+                        pl.when(low > 0)(wait)
+                        pl.when(low == 0)(own_copies[chunk].wait)
+
+        def run(big, low):
+            def loads(step, slot):
+                at = column(step)
+                mate = mate_at(low_at(step))
+                part = rows_at(step % parts, hid)
                 return [
-                    pltpu.make_async_copy(master.at[:, at], wide.at[slot, 0], local.at[slot]),
-                    pltpu.make_async_copy(first.at[0, :, at], wide.at[slot, 1], local.at[2 + slot]),
-                    pltpu.make_async_copy(second.at[0, :, at], wide.at[slot, 2], local.at[4 + slot]),
+                    pltpu.make_async_copy(mlp_master.at[:, at], big.at[slot, 0], local.at[slot]),
+                    pltpu.make_async_copy(mlp_first.at[0, :, at], big.at[slot, 1], local.at[2 + slot]),
+                    pltpu.make_async_copy(mlp_second.at[0, :, at], big.at[slot, 2], local.at[4 + slot]),
                 ] + [
                     pltpu.make_async_copy(
-                        pieces(block, top, i),
-                        low.at[slot, top, i],
-                        local.at[6 + slot + 2 * (top * mates + i)],
+                        source.at[top * TEAM + mate, :, part],
+                        low.at[slot, top],
+                        local.at[6 + slot + 2 * top],
                     )
                     for top in range(tops)
-                    for i in range(mates)
                 ]
 
-            def body(block, slot):
+            def body(step, slot):
                 @pl.loop(0, rows // STRIP)
-                def _(step):
-                    at = pl.ds(step * STRIP, STRIP)
-                    for i in range(mates):
-                        span = slice(i * each, (i + 1) * each)
-                        grad = low[slot, 0, i, at].astype(FULL)
-                        for top in range(1, tops):
-                            grad = grad + low[slot, top, i, at].astype(FULL)
-                        value = wide[slot, 0, at, span]
-                        inner, _, _ = adam_step(
-                            value, grad, wide[slot, 1, at, span], wide[slot, 2, at, span]
-                        )
-                        stage[block, at, span] = (value - inner).astype(LOW)
-
-                near(block).start()
-                far(block).start()
-
-            stream(TEAM, loads, body)
-
-            @pl.loop(0, TEAM)
-            def _(block):
-                near(block).wait()
-                far(block).wait_send()
+                def _(strip):
+                    at = pl.ds(strip * STRIP, STRIP)
+                    grad = low[slot, 0, at].astype(FULL)
+                    for top in range(1, tops):
+                        grad = grad + low[slot, top, at].astype(FULL)
+                    value = big[slot, 0, at]
+                    inner, _, _ = adam_step(value, grad, big[slot, 1, at], big[slot, 2, at])
+                    stage[slot, at] = (value - inner).astype(LOW)
+
+                near(step).start()
+
+                @pl.when(step > 0)
+                def _():
+                    near(step - 1).wait()
+                    far(step - 1).start()
+
+            steps = parts * TEAM
+            stream(steps, loads, body, arrive)
+            near(steps - 1).wait()
+            far(steps - 1).start()
 
         pl.run_scoped(
-            run,
-            pltpu.VMEM((2, 3, rows, hid), FULL),
-            pltpu.VMEM((2, tops, mates, rows, each), LOW),
+            run, pltpu.VMEM((2, 3, rows, hid), FULL), pltpu.VMEM((2, tops, rows, hid), LOW)
         )
 
         def finish():
-            @pl.loop(0, TEAM)
-            def _(block):
-                far(block).wait_recv()
+            @pl.loop(0, parts * TEAM)
+            def _(step):
+                far(step).wait()
 
         return finish
-
-    def mlp_chunk(chunk, part, source, offset):
-        return differ(
-            chunk,
-            lambda block, top, i: source.at[top * TEAM + block, :, pl.ds(offset, hid)],
-            (mlp_master, mlp_first, mlp_second),
-            mlp_diff,
-            mlp_other,
-            lambda block: pl.ds(pl.multiple_of((part * TEAM + block) * hid, hid), hid),
-            1,
-        )
-
-    def att_chunk(chunk):
-        mates = hid // share
-        steps = TEAM // mates
-
-        def piece(block, top, i):
-            part = block // steps
-            mate = (block % steps) * mates + i
-            at = pl.ds(pl.multiple_of(part * share, share), share)
-            return got_att.at[top * TEAM + mate, :, at]
-
-        return differ(
-            chunk,
-            piece,
-            (att_master, att_first, att_second),
-            att_diff,
-            att_other,
-            lambda block: pl.ds(pl.multiple_of(block * hid, hid), hid),
-            mates,
-        )
-
-    waits = []
-
-    def down_changes():
-        own_copies[0].wait()
-        for other in order:
-            block_copy(0, other).wait_recv()
-        waits.append(mlp_chunk(0, 2, got_down, 0))
-
-    def gate_changes():
-        own_copies[1].wait()
-        for other in order:
-            block_copy(1, other).wait_recv()
-        waits.append(mlp_chunk(1, 0, got_gate, 0))
-        waits.append(mlp_chunk(2, 1, got_gate, hid))
 
     def tokens_total(start, value):
         at = pl.ds(start, STRIP)
@@ -1212,17 +1203,20 @@
         at = pl.ds(start, STRIP)
         out_tokens[at] = (resid[at] + value).astype(LOW)
 
-    def fed_sum():
-        team_sum(
-            me, fed_all, own_two, got_two, edge_two, send, local, out_total, gate_changes
-        )
-
-    down_changes()
-    sum_steps(me, own, got, edge, terms.first(), send, tokens_total, fed_sum)
+    waits = [differ(0, 1, 2, 0)]
+    one = sum_steps(me, own, got, edge, terms.first(), send, tokens_total, split)
+    two = team_sum(
+        me, fed_all, own_two, got_two, edge_two, send, local, out_total, split
+    )
+    next(one)
+    next(two)
+    waits.append(differ(1, 2, 0, TEAM))
+    for _ in range(2):
+        for steps in (one, two):
+            next(steps, None)
     own_copies[2].wait()
     for other in order:
         block_copy(2, other).wait_recv()
-    waits.append(att_chunk(3))
     for chunk in range(3):
         for other in order:
             block_copy(chunk, other).wait_send()
@@ -1230,10 +1224,10 @@
         wait()
 
 
-GATE_FIRST, GATE_EARLY, GATE_LATE, GATE_GATHER = 2, 2, 2, 2
-
-
-def backward_layer(ranks, tokens, att, mlp, *rest):
+GATE_FIRST, GATE_LATE, GATE_GATHER = 0, 1, 2
+
+
+def backward_layer(ranks, tokens, mlp, *rest):
     flat, resid, cot = tokens
     hidden_all, projected_all, gate_weights = rest[4], rest[9], rest[12]
     count, width = flat.shape
@@ -1248,8 +1242,6 @@
         (low((ranks, rows, 4 * share)), ANYWHERE),
         (low((ranks, rows, 2 * hid)), ANYWHERE),
         (low((ranks, rows, hid)), ANYWHERE),
-        (low(att[0].shape), ANYWHERE),
-        (low(att[0].shape), ANYWHERE),
         (low(mlp[0].shape), ANYWHERE),
         (low(mlp[0].shape), ANYWHERE),
         (low((TEAM, count, width)), ANYWHERE),
@@ -1264,7 +1256,7 @@
     return pl.pallas_call(
         functools.partial(backward_kernel, ranks),
         out_shape=[shape for shape, _ in out],
-        in_specs=[vmem] * 3 + [ANYWHERE] * (len(rest) + 6),
+        in_specs=[vmem] * 3 + [ANYWHERE] * (len(rest) + 3),
         out_specs=[spec for _, spec in out],
         scratch_shapes=sum_scratch(count, width)
         + [pltpu.VMEM((TEAM // 2, count, width), LOW)]
@@ -1272,18 +1264,19 @@
         + [
             pltpu.VMEM((count, width), LOW),
             pltpu.VMEM((count, width), FULL),
-            pltpu.VMEM((TEAM, rows, hid), LOW),
+            pltpu.VMEM((2, rows, hid), LOW),
+            pltpu.VMEM((max(width, all_tokens), max(2 * hid, 7 * share)), LOW),
         ]
         + [pltpu.SemaphoreType.DMA((number,)) for number in sems]
         + [pltpu.SemaphoreType.DMA((2, TEAM // 2))] * 2
-        + [pltpu.SemaphoreType.DMA((4 * TEAM,))] * 2
+        + [pltpu.SemaphoreType.DMA((3 * TEAM,))] * 2
         + [
             pltpu.SemaphoreType.DMA((3 + TEAM,)),
             pltpu.SemaphoreType.DMA((max(locals_needed, 12),)),
         ],
         compiler_params=params(2),
         name="backward_layer",
-    )(flat, resid, cot, *rest, *att, *mlp)
+    )(flat, resid, cot, *rest, *mlp)
 
 
 def pack_kernel(*refs):
@@ -1356,6 +1349,82 @@
         grads.reshape(ranks // TEAM, TEAM, rows, columns),
         master, first, second, outer, diff, other, *extra,
     )
+
+
+def adam_kernel(share, grad, master, first, second, *refs):
+    first_new, second_new, diff = refs[-3:]
+    for t in range(grad.shape[1]):
+        at = slice(t * share, (t + 1) * share)
+        gradient = grad[0, t].astype(FULL)
+        for top in range(1, grad.shape[0]):
+            gradient = gradient + grad[top, t].astype(FULL)
+        inner, first_new[0, :, at], second_new[0, :, at] = adam_step(
+            master[:, at], gradient, first[0, :, at], second[0, :, at]
+        )
+        diff[:, at] = (master[:, at] - inner).astype(LOW)
+
+
+def chunk_specs(tops, rows, bases, share, lanes):
+    per = lanes // share
+    steps = TEAM // per
+    parts = len(bases)
+
+    def column(p, t):
+        place = bases[0]
+        for q in range(1, parts):
+            place = place + jnp.where(p >= q, bases[q] - bases[q - 1], 0)
+        return place * steps + t
+
+    return (
+        (parts, steps),
+        pl.BlockSpec((tops, per, rows, share), lambda p, t: (0, t, 0, p)),
+        pl.BlockSpec((1, rows, lanes), lambda p, t: (0, 0, column(p, t))),
+        pl.BlockSpec((rows, lanes), lambda p, t: (0, column(p, t))),
+        pl.BlockSpec((rows, lanes), lambda p, t: (0, p * steps + t)),
+    )
+
+
+def adam_chunk(grads, master, first, second, bases):
+    ranks, rows, columns = grads.shape
+    share = columns // len(bases)
+    tops = ranks // TEAM
+    grid, grad, wide, flat, packed = chunk_specs(tops, rows, bases, share, max(LANES, share))
+    state = jax.ShapeDtypeStruct(first.shape, FULL)
+    return pl.pallas_call(
+        functools.partial(adam_kernel, share),
+        grid=grid,
+        out_shape=[
+            state,
+            state,
+            jax.ShapeDtypeStruct((rows, TEAM * len(bases) * share), LOW),
+        ],
+        in_specs=[grad, flat, wide, wide],
+        out_specs=[wide, wide, packed],
+        compiler_params=pltpu.CompilerParams(vmem_limit_bytes=VMEM_BYTES),
+        name="adam_chunk",
+    )(grads.reshape(tops, TEAM, rows, columns), master, first, second)
+
+
+def outer_kernel(reps, diff, other, master, momentum, *refs):
+    mean_out, new, momentum_new = refs[-3:]
+    mean = (diff[...].astype(FULL) + other[...].astype(FULL)) / reps
+    mean_out[...] = mean
+    new[...], momentum_new[...] = outer_step(master[...], mean, momentum[...])
+
+
+def outer_chunk(reps, diff, other, master, momentum, bases):
+    rows = master.shape[0]
+    share = diff.shape[1] // (TEAM * len(bases))
+    grid, _, _, flat, packed = chunk_specs(1, rows, bases, share, max(LANES, share))
+    return pl.pallas_call(
+        functools.partial(outer_kernel, reps),
+        grid=grid,
+        out_shape=[jax.ShapeDtypeStruct(master.shape, FULL)] * 3,
+        in_specs=[packed, packed, flat, flat],
+        out_specs=[flat] * 3,
+        compiler_params=pltpu.CompilerParams(vmem_limit_bytes=VMEM_BYTES),
+        name="outer_chunk",
+    )(diff, other, master, momentum)
 
 
 def on_device(
@@ -1389,6 +1458,10 @@
 
     def hop(values, other):
         pairs = [(r * ranks + i, r * ranks + (i ^ other)) for r in range(reps) for i in range(ranks)]
+        return lax.ppermute(values, ("rep", "dp"), pairs)
+
+    def swap(values):
+        pairs = [(r * ranks + i, (1 - r) * ranks + i) for r in range(reps) for i in range(ranks)]
         return lax.ppermute(values, ("rep", "dp"), pairs)
 
     flat_low = tokens.reshape(count, width)
@@ -1434,15 +1507,12 @@
         got_att,
         got_gate,
         got_down,
-        att_diff,
-        att_other,
         mlp_diff,
         mlp_other,
         *_,
     ) = backward_layer(
         ranks,
         (flat_low, resid, cot),
-        (att_master, att_first, att_second),
         (mlp_master, mlp_first, mlp_second),
         wide_cosine,
         wide_sine,
@@ -1460,16 +1530,15 @@
         down_low,
     )
     mlp = (mlp_master, mlp_first, mlp_second, mlp_outer, mlp_diff, mlp_other)
+    bases = [0, 1, 2, 3]
+    *att_state, att_diff = adam_chunk(got_att, att_master, att_first, att_second, bases)
     mlp_out = finish_chunk(reps, got_down, *mlp, [2], None)
     mlp_out = finish_chunk(reps, got_gate, *mlp, [0, 1], mlp_out)
-    att_out = finish_chunk(
-        reps, got_att, att_master, att_first, att_second, att_outer, att_diff, att_other,
-        [0, 1, 2, 3], None,
-    )
+    att_new = outer_chunk(reps, att_diff, swap(att_diff), att_master, att_outer, bases)
     return (
         out_tokens.reshape(units, length, width),
         grad_tokens.reshape(units, length, width),
-        *(att_out[3], att_out[0], att_out[1], att_out[2], att_out[4]),
+        *(att_new[1], *att_state, att_new[0], att_new[2]),
         *(mlp_out[3], mlp_out[0], mlp_out[1], mlp_out[2], mlp_out[4]),
     )
 

time: 968 us -> 829 us (0.86)
  Pallas kernels: 933 us -> 798 us
    pallas_call x1, Pallas kernels: 508 us -> 419 us  [backward_layer(): pl.pallas_call(functools.partial(backward_kernel, ranks), out_shape=[shap...]
    pallas_call x1, Pallas kernels: 353 us -> 300 us  [forward_layer(): pl.pallas_call(functools.partial(forward_kernel, ranks), out_shape=[shape...]
    pallas_call x0 -> x2, Pallas kernels: none -> 24 us  [the longest x1 12.2 us: adam_chunk(): pl.pallas_call(functools.partial(adam_kernel, share), grid=grid, out_shap...]
    pallas_call x3 -> x2, Pallas kernels: 65.7 us -> 48.5 us  [finish_chunk(): pl.pallas_call(functools.partial(finish_kernel, reps, share), grid=(parts...]
  transfers between devices with their start and end apart: 7 -> 8, of which waited for: 2 -> 2; matrix products, arithmetic and copies ran while one was open for 1% -> 1% of each run, Pallas kernels for 1% -> 7%
where the time goes in v2:
time: 829 us; the launch traced here: 827 us
  Pallas kernels  798 us (96%)
  other arithmetic  13.2 us (2%)
    pallas_call x1, Pallas kernels, backward_layer(): pl.pallas_call(functools.partial(backward_kernel, ranks), out_shape=[shap...  419 us
    pallas_call x1, Pallas kernels, forward_layer(): pl.pallas_call(functools.partial(forward_kernel, ranks), out_shape=[shape...  300 us
    pallas_call x2, Pallas kernels, finish_chunk(): pl.pallas_call(functools.partial(finish_kernel, reps, share), grid=(parts...  48.5 us
  transfers between devices with their start and end apart: 8, of which 2 were waited for; matrix products, arithmetic and copies ran while one was open for 1% of the time, Pallas kernels for 7%

profile of v2, /device:TPU:0, one launch (start us, length us, event | category | flops | bytes accessed | tf_op | source)
XLA Modules:
  0.0 826.9 jit_solution(8424235573250800311)
XLA Ops:
  0.6 0.5 collective-permute-start
  1.2 2.6 collective-permute-start.1
  3.8 0.1 collective-permute-start.2
  3.8 1.8 collective-permute-start.3
  5.6 0.0 collective-permute-start.4
  5.7 0.8 copy.39
  6.5 1.4 convert_reduce_fusion
  7.9 1.6 fusion.2
  9.6 2.5 fusion.3.normed_own
  12.1 0.0 copy-start.2
  12.1 6.1 pack_shares.1.att_pack
  18.2 0.2 compare_and_fusion
  18.4 0.0 collective-permute-done
  18.4 0.0 copy-done.2
  18.4 2.7 collective-permute-start.5
  21.1 0.1 copy.40
  21.2 0.0 collective-permute-done.1
  21.2 0.1 collective-permute-start.6
  21.3 0.1 copy.41
  21.4 0.0 collective-permute-done.2
  21.4 0.1 copy.42
  21.5 0.0 collective-permute-done.3
  21.5 0.1 copy.43
  21.6 0.0 collective-permute-done.4
  21.6 0.1 copy.44
  21.7 1.3 collective-permute-done.5
  22.9 0.1 copy.45
  23.0 2.1 collective-permute-done.6
  25.1 0.1 copy.46
  25.2 0.1 stack.35
  25.3 0.1 select_reduce_fusion
  25.4 3.7 fusion.7
  29.1 1.6 fusion.6.bias
  30.7 1.9 maximum_bitcast_fusion
  32.6 299.8 %forward_layer.1 = (bf16[8,256,2048]{2,1,0:T(8,128)(2,1)}, bf16[8,256,2048]{2,1,0:T(8,128)(2,1)}, bf16[2048,1024]{1,0:T(8,128)(2,1)}, bf16[2048,2048]{1,0:T(8,12...) custom-call(bf16[256,2048]{1,0:T(8,128)(2,1)} %bitcast.30, ...), custom_call_target="tpu_custom_call" | custom-call | tf_op jit(solution)/shard_map/forward_layer/pallas_call | solution.py:669
  332.4 419.3 %backward_layer.1 = (bf16[256,2048]{1,0:T(8,128)(2,1)}, f32[256,2048]{1,0:T(8,128)}, bf16[16,128,1024]{2,1,0:T(8,128)(2,1)}, bf16[16,128,2048]{2,1,0:T(8,128)(2,...) custom-call(bf16[256,2048]{1,0:T(8,128)(2,1)} %bitcast.31, ...), custom_call_target="tpu_custom_call" | custom-call | tf_op jit(solution)/shard_map/backward_layer/pallas_call | solution.py:1256
  751.7 12.2 %adam_chunk.1 = (f32[1,128,8192]{2,1,0:T(8,128)}, f32[1,128,8192]{2,1,0:T(8,128)}, bf16[128,8192]{1,0:T(8,128)(2,1)}) custom-call(bf16[2,8,128,1024]{3,2,1,0:T(8,128)(2,1)} %bitcast.42, f32[128,8192]{1,0:T(8,128)} %master.5, f32[1,128,8192]{2,1,0:T(8,128)} %first.3, f32[1,128,8192]{2,1,0:T(8,128)} %second.3), custom_call_target="tpu_custom_call" | custom-call | tf_op jit(solution)/shard_map/adam_chunk/pallas_call | solution.py:1393
  763.9 0.3 collective-permute-start.7
  764.2 16.3 %finish_chunk.2 = (f32[1,128,24576]{2,1,0:T(8,128)}, f32[1,128,24576]{2,1,0:T(8,128)}, f32[128,24576]{1,0:T(8,128)}, f32[128,24576]{1,0:T(8,128)}, f32[128,24576]{1,0:T(8,128)}) custom-call(bf16[2,8,128,1024]{3,2,1,0:T(8,128)(2,1)} %bitcast.38, f32[128,24576]{1,0:T(8,128)} %master.7, f32[1,128,24576]{2,1,0:T(8,128)} %first.5, f32[1,128,24576]{2,1,0:T(8,128)} %second.5, ...), custom_call_target="tpu_custom_call" | custom-call | tf_op jit(solution)/shard_map/finish_chunk/pallas_call | solution.py:1339
  780.6 32.2 %finish_chunk.3 = (f32[1,128,24576]{2,1,0:T(8,128)}, f32[1,128,24576]{2,1,0:T(8,128)}, f32[128,24576]{1,0:T(8,128)}, f32[128,24576]{1,0:T(8,128)}, f32[128,24576]{1,0:T(8,128)}) custom-call(bf16[2,8,128,2048]{3,2,1,0:T(8,128)(2,1)} %bitcast.32, f32[128,24576]{1,0:T(8,128)} %master.7, ...), custom_call_target="tpu_custom_call", output_to_operand_aliasing={{0}: (7, {}), {1}: (8, {}), {2}: (9, {}), {3}: (10, {}), {4... | custom-call | tf_op jit(solution)/shard_map/finish_chunk/pallas_call | solution.py:1339
  812.8 0.0 copy-start.1
  812.8 0.0 copy-start
  812.8 0.0 collective-permute-done.7.other
  812.8 11.8 %outer_chunk.1 = (f32[128,8192]{1,0:T(8,128)}, f32[128,8192]{1,0:T(8,128)}, f32[128,8192]{1,0:T(8,128)}) custom-call(bf16[128,8192]{1,0:T(8,128)(2,1)} %get-tuple-element.62.diff, bf16[128,8192]{1,0:T(8,128)(2,1)} %collective-permute-done.7.other, f32[128,8192]{1,0:T(8,128)} %master.5, f32[128,8192]{1,0:T(8,128)} %momentum.1), custom_call_target="tpu_custom_call" | custom-call | tf_op jit(solution)/shard_map/outer_chunk/pallas_call | solution.py:1419
  824.6 0.0 copy-done.1
  824.6 1.0 copy.54
  825.6 0.0 copy-done
  825.6 1.3 copy.55
  (9 shorter events, 0.1 us)
Async XLA Ops:
  0.6 17.8 %collective-permute-start = (s32[1,2]{1,0:T(1,128)}, s32[1,2]{1,0:T(1,128)S(1)}, u32[]{:S(2)}, u32[]{:S(2)}) collective-permute-start(s32[1,2]{1,0:T(1,128)} %param.13), channel_id=1, source_target_pairs={{0,1},{1,0},{2,3},{3,2},{4,5},{5,4},{6,7},{7,6},{8,9},{9,8},{10,11... | collective-permute-start | bytes 32 | tf_op jit(solution)/shard_map/ppermute | solution.py:1461
  1.2 20.1 %collective-permute-start.1 = (s32[1,2]{1,0:T(1,128)}, s32[1,2]{1,0:T(1,128)S(1)}, u32[]{:S(2)}, u32[]{:S(2)}) collective-permute-start(s32[1,2]{1,0:T(1,128)} %param.13), channel_id=1, source_target_pairs={{0,2},{1,3},{2,0},{3,1},{4,6},{5,7},{6,4},{7,5},{8,10},{9,11},{10,... | collective-permute-start | bytes 32 | tf_op jit(solution)/shard_map/ppermute | solution.py:1461
  3.8 17.6 %collective-permute-start.2 = (s32[1,2]{1,0:T(1,128)}, s32[1,2]{1,0:T(1,128)S(1)}, u32[]{:S(2)}, u32[]{:S(2)}) collective-permute-start(s32[1,2]{1,0:T(1,128)} %param.13), channel_id=1, source_target_pairs={{0,3},{1,2},{2,1},{3,0},{4,7},{5,6},{6,5},{7,4},{8,11},{9,10},{10,... | collective-permute-start | bytes 32 | tf_op jit(solution)/shard_map/ppermute | solution.py:1461
  3.8 17.7 %collective-permute-start.3 = (s32[1,2]{1,0:T(1,128)}, s32[1,2]{1,0:T(1,128)S(1)}, u32[]{:S(2)}, u32[]{:S(2)}) collective-permute-start(s32[1,2]{1,0:T(1,128)} %param.13), channel_id=1, source_target_pairs={{0,4},{1,5},{2,6},{3,7},{4,0},{5,1},{6,2},{7,3},{8,12},{9,13},{10,... | collective-permute-start | bytes 32 | tf_op jit(solution)/shard_map/ppermute | solution.py:1461
  5.6 16.0 %collective-permute-start.4 = (s32[1,2]{1,0:T(1,128)}, s32[1,2]{1,0:T(1,128)S(1)}, u32[]{:S(2)}, u32[]{:S(2)}) collective-permute-start(s32[1,2]{1,0:T(1,128)} %param.13), channel_id=1, source_target_pairs={{0,5},{1,4},{2,7},{3,6},{4,1},{5,0},{6,3},{7,2},{8,13},{9,12},{10,... | collective-permute-start | bytes 32 | tf_op jit(solution)/shard_map/ppermute | solution.py:1461
  12.1 6.3 copy-start.2
  18.4 4.5 collective-permute-start.5
  21.2 3.9 collective-permute-start.6
  763.9 48.9 %collective-permute-start.7 = (bf16[128,8192]{1,0:T(8,128)(2,1)}, bf16[128,8192]{1,0:T(8,128)(2,1)}, u32[]{:S(2)}, u32[]{:S(2)}) collective-permute-start(bf16[128,8192]{1,0:T(8,128)(2,1)} %get-tuple-element.62.diff), channel_id=1, source_target_pairs={{0,16},{1,17},{2,18},{3,19},{4,20},{5,21},{6,22},{7,23},{8,24},{9,... | collective-permute-start | bytes 6291464 | tf_op jit(solution)/shard_map/ppermute | solution.py:1465
  812.8 11.9 %copy-start.1 = (bf16[256,2048]{1,0:T(8,128)(2,1)S(1)}, bf16[256,2048]{1,0:T(8,128)(2,1)}, u32[]{:S(2)}) copy-start(bf16[256,2048]{1,0:T(8,128)(2,1)} %get-tuple-element.59) | copy-start | bytes 3145732
  812.8 12.8 %copy-start = (f32[256,2048]{1,0:T(8,128)S(1)}, f32[256,2048]{1,0:T(8,128)}, u32[]{:S(2)}) copy-start(f32[256,2048]{1,0:T(8,128)} %get-tuple-element.60) | copy-start | bytes 6291460

commit v3 on v2

--- a/solution.py
+++ b/solution.py
@@ -104,8 +104,10 @@
 ANYWHERE = pl.BlockSpec(memory_space=pl.ANY)
 BITS = (1, 2, 4)
 PIECES = 4
+GATE_AHEAD, GATE_MIDDLE = 7, 3
+DOWN_EARLY = 15
 FEED_EARLY = 6
-SPLIT_TOKENS, SPLIT_ATTENDED, SPLIT_NORMED, SPLIT_COT, SPLIT_BACK = 3, 3, 3, 3, 3
+SPLIT_TOKENS, SPLIT_ATTENDED, SPLIT_NORMED, SPLIT_COT, SPLIT_BACK = 3, 3, 3, 2, 3
 STRIP = 16
 GATHER_COPIES = 6 * PIECES + 1
 VMEM_BYTES = 60 * 1024 * 1024
@@ -217,7 +219,41 @@
     ]
 
 
-def team_sum(me, parts, own, got, edge, send, loads, total, split):
+def fold_steps(me, own, got, edge, first, send, split):
+    count = own.shape[1]
+    _, second, third = ({"dp": flip(me, bit)} for bit in BITS)
+    spans = [pl.ds(0, split), pl.ds(split, count - split)]
+
+    def add(j, span, extra=None):
+        @pl.loop(0, span.size // STRIP)
+        def _(step):
+            at = pl.ds(span.start + step * STRIP, STRIP)
+            value = own[j, at].astype(FULL)
+            if extra is None:
+                value = value + got[j, at].astype(FULL)
+            else:
+                value = value + extra[at].astype(FULL)
+            own[j, at] = value.astype(LOW)
+
+    whole = pl.ds(0, count)
+    first[3].wait_recv()
+    add(3, whole)
+    corners = [
+        send(own.at[3].at[span], edge.at[0].at[span], where)
+        for span, where in zip(spans, (second, third))
+    ]
+    for j in (2, 1, 0):
+        first[j].wait_recv()
+        add(j, whole)
+    yield
+    for j, span, copy in zip((2, 1), spans, corners):
+        copy.wait_recv()
+        add(j, span, edge.at[0])
+    for copy in corners + [first[j] for j in range(4)]:
+        copy.wait_send()
+
+
+def fold_parts(me, parts, own, got, edge, send, loads, split):
     core = {"dp": flip(me, 1)}
     loading = [pltpu.make_async_copy(parts.at[2 * j], own.at[j], loads.at[j]) for j in range(4)]
     first = {}
@@ -226,7 +262,7 @@
         first[j] = send(parts.at[2 * j + 1], got.at[j], core)
     for copy in loading:
         copy.wait()
-    yield from sum_steps(me, own, got, edge, first, send, total, split)
+    yield from fold_steps(me, own, got, edge, first, send, split)
 
 
 def sum_steps(me, own, got, edge, first, send, total, split):
@@ -359,10 +395,8 @@
         self.send, self.send_x = send, send_x
         self.rows = weights.shape[0] // ranks
         self.half = self.rows // 2
-        self.order = list(range(TEAM, ranks)) + list(range(1, TEAM))
+        self.order = list(range(1, ranks))
         self.ways, self.swaps = {}, []
-        near = [other for other in self.order if other < 4]
-        self.turns = near + [other for other in self.order if other >= 4]
 
     def place(self, device):
         return self.weights.at[pl.ds(device * self.rows + self.rep * self.half, self.half)]
@@ -383,7 +417,7 @@
     def forward(self, number=None):
         done = len(self.swaps)
         number = len(self.order) - done if number is None else number
-        for other in self.turns[done : done + number]:
+        for other in self.order[done : done + number]:
             self.ways[other].wait_recv()
             at = self.place(across(self.me, other))
             self.swaps.append(self.send_x(at, at, {"rep": 1 - self.rep}))
@@ -515,6 +549,8 @@
     load.start()
     load.wait()
 
+    gathers[1].forward(GATE_AHEAD)
+
     def fetch(step, slot):
         return pltpu.make_async_copy(
             normed_all.at[unit_of(step)], block.at[slot], local.at[5 + slot]
@@ -575,9 +611,9 @@
 
     steps = sum_steps(me, own, got, edge, first, send, total, SPLIT_ATTENDED * UNIT // PIECES)
     next(steps)
-    early = len(gathers[2].order) // 2
+    early = DOWN_EARLY * (ranks - 1) // 15
     gathers[2].begin(down_pack, early)
-    gathers[1].forward()
+    gathers[1].forward(GATE_MIDDLE * (ranks - TEAM) // TEAM)
     next(steps)
     for _ in steps:
         pass
@@ -588,6 +624,7 @@
     cots.begin()
     keep = pltpu.make_async_copy(normed, normed_two_all.at[0], local.at[3])
     keep.start()
+    gathers[1].forward()
     gathers[2].forward(early)
     tokens.turn()
     keep.wait()
@@ -748,7 +785,6 @@
 
 def backward_kernel(
     ranks,
-    flat,
     resid,
     cot,
     cosine,
@@ -768,8 +804,9 @@
     mlp_master,
     mlp_first,
     mlp_second,
-    out_tokens,
-    grad_tokens,
+    grad_resid,
+    one_folded,
+    two_folded,
     got_att,
     got_gate,
     got_down,
@@ -788,7 +825,6 @@
     got_two,
     edge_two,
     grad_low,
-    grad_resid,
     stage,
     wide,
     sent,
@@ -1192,28 +1228,26 @@
 
         return finish
 
-    def tokens_total(start, value):
-        at = pl.ds(start, STRIP)
-        normed, factor = strip_normalize(flat[at].astype(FULL))
-        along = jnp.sum(value * normed, axis=1, keepdims=True) * (1.0 / width)
-        middle = jnp.sum(value, axis=1, keepdims=True) * (1.0 / width)
-        grad_tokens[at] = grad_resid[at] + factor * (value - middle - normed * along)
-
-    def out_total(start, value):
-        at = pl.ds(start, STRIP)
-        out_tokens[at] = (resid[at] + value).astype(LOW)
-
     waits = [differ(0, 1, 2, 0)]
-    one = sum_steps(me, own, got, edge, terms.first(), send, tokens_total, split)
-    two = team_sum(
-        me, fed_all, own_two, got_two, edge_two, send, local, out_total, split
-    )
-    next(one)
-    next(two)
+    folds = [
+        fold_steps(me, own, got, edge, terms.first(), send, split),
+        fold_parts(me, fed_all, own_two, got_two, edge_two, send, local, split),
+    ]
+    for steps in folds:
+        next(steps)
     waits.append(differ(1, 2, 0, TEAM))
-    for _ in range(2):
-        for steps in (one, two):
-            next(steps, None)
+    outs = []
+    for steps, terms_now, folded in zip(folds, (own, own_two), (one_folded, two_folded)):
+        for _ in steps:
+            pass
+        outs.append(
+            pltpu.make_async_copy(
+                terms_now.at[pl.ds(0, 3)], folded, local.at[len(outs)]
+            )
+        )
+        outs[-1].start()
+    for copy in outs:
+        copy.wait()
     own_copies[2].wait()
     for other in order:
         block_copy(2, other).wait_recv()
@@ -1228,17 +1262,18 @@
 
 
 def backward_layer(ranks, tokens, mlp, *rest):
-    flat, resid, cot = tokens
+    resid, cot = tokens
     hidden_all, projected_all, gate_weights = rest[4], rest[9], rest[12]
-    count, width = flat.shape
+    count, width = resid.shape
     all_tokens, hid = hidden_all.shape
     share = projected_all.shape[2] // 3
     rows = width // ranks
     vmem = pl.BlockSpec(memory_space=pltpu.VMEM)
     low = functools.partial(jax.ShapeDtypeStruct, dtype=LOW)
     out = [
-        (low((count, width)), vmem),
         (jax.ShapeDtypeStruct((count, width), FULL), vmem),
+        (low((3, count, width)), ANYWHERE),
+        (low((3, count, width)), ANYWHERE),
         (low((ranks, rows, 4 * share)), ANYWHERE),
         (low((ranks, rows, 2 * hid)), ANYWHERE),
         (low((ranks, rows, hid)), ANYWHERE),
@@ -1256,14 +1291,13 @@
     return pl.pallas_call(
         functools.partial(backward_kernel, ranks),
         out_shape=[shape for shape, _ in out],
-        in_specs=[vmem] * 3 + [ANYWHERE] * (len(rest) + 3),
+        in_specs=[vmem] * 2 + [ANYWHERE] * (len(rest) + 3),
         out_specs=[spec for _, spec in out],
         scratch_shapes=sum_scratch(count, width)
         + [pltpu.VMEM((TEAM // 2, count, width), LOW)]
         + sum_scratch(count, width)
         + [
             pltpu.VMEM((count, width), LOW),
-            pltpu.VMEM((count, width), FULL),
             pltpu.VMEM((2, rows, hid), LOW),
             pltpu.VMEM((max(width, all_tokens), max(2 * hid, 7 * share)), LOW),
         ]
@@ -1276,7 +1310,7 @@
         ],
         compiler_params=params(2),
         name="backward_layer",
-    )(flat, resid, cot, *rest, *mlp)
+    )(resid, cot, *rest, *mlp)
 
 
 def pack_kernel(*refs):
@@ -1502,8 +1536,9 @@
         bias,
     )
     (
-        out_tokens,
-        grad_tokens,
+        grad_resid,
+        one_folded,
+        two_folded,
         got_att,
         got_gate,
         got_down,
@@ -1512,7 +1547,7 @@
         *_,
     ) = backward_layer(
         ranks,
-        (flat_low, resid, cot),
+        (resid, cot),
         (mlp_master, mlp_first, mlp_second),
         wide_cosine,
         wide_sine,
@@ -1529,6 +1564,13 @@
         gate_low,
         down_low,
     )
+    def unfold(folded):
+        terms = (folded[0], hop(folded[1], 2), hop(folded[2], 4))
+        return sum(term.astype(FULL) for term in terms)
+
+    grad_normed_one, fed = unfold(one_folded), unfold(two_folded)
+    grad_tokens = grad_resid + normalize_back(flat, grad_normed_one)
+    out_tokens = (resid + fed).astype(LOW)
     mlp = (mlp_master, mlp_first, mlp_second, mlp_outer, mlp_diff, mlp_other)
     bases = [0, 1, 2, 3]
     *att_state, att_diff = adam_chunk(got_att, att_master, att_first, att_second, bases)

time: 829 us -> 817 us (0.986)
  Pallas kernels: 798 us -> 768 us
    pallas_call x1, Pallas kernels: 419 us -> 399 us  [backward_layer(): pl.pallas_call(functools.partial(backward_kernel, ranks), out_shape=[shap...]
    pallas_call x1, Pallas kernels: 300 us -> 291 us  [forward_layer(): pl.pallas_call(functools.partial(forward_kernel, ranks), out_shape=[shape...]
  transfers between devices with their start and end apart: 8 -> 12, of which waited for: 2 -> 2; matrix products, arithmetic and copies ran while one was open for 1% -> 2% of each run, Pallas kernels for 7% -> 8%
where the time goes in v3:
time: 817 us; the launch traced here: 814 us
  Pallas kernels  768 us (94%)
  other arithmetic  21.4 us (3%)
  starting transfers between devices  14.3 us (2%)
    pallas_call x1, Pallas kernels, backward_layer(): pl.pallas_call(functools.partial(backward_kernel, ranks), out_shape=[shap...  399 us
    pallas_call x1, Pallas kernels, forward_layer(): pl.pallas_call(functools.partial(forward_kernel, ranks), out_shape=[shape...  291 us
    pallas_call x2, Pallas kernels, finish_chunk(): pl.pallas_call(functools.partial(finish_kernel, reps, share), grid=(parts...  48.7 us
  transfers between devices with their start and end apart: 12, of which 2 were waited for; matrix products, arithmetic and copies ran while one was open for 2% of the time, Pallas kernels for 8%

profile of v3, /device:TPU:0, one launch (start us, length us, event | category | flops | bytes accessed | tf_op | source)
XLA Modules:
  0.0 814.5 jit_solution(5652488280293019923)
XLA Ops:
  0.6 0.0 copy-start
  0.7 0.5 collective-permute-start
  1.2 2.6 collective-permute-start.1
  3.8 0.1 collective-permute-start.2
  3.8 1.8 collective-permute-start.3
  5.6 0.0 collective-permute-start.4
  5.7 0.8 copy.39
  6.5 1.4 convert_reduce_fusion
  7.9 1.6 fusion.10
  9.6 0.0 copy-done
  9.6 1.3 fusion.4.normed_own
  10.9 6.1 pack_shares.1.att_pack
  17.0 0.2 compare_and_fusion
  17.2 0.0 collective-permute-done
  17.2 0.0 copy-done.5
  17.2 2.7 collective-permute-start.5
  19.9 0.1 copy.40
  20.0 0.0 collective-permute-done.1
  20.0 0.1 collective-permute-start.6
  20.1 0.1 copy.41
  20.2 0.0 collective-permute-done.2
  20.2 0.1 copy.42
  20.3 0.0 collective-permute-done.3
  20.3 0.1 copy.43
  20.4 0.0 collective-permute-done.4
  20.4 0.1 copy.44
  20.5 1.3 collective-permute-done.5
  21.7 0.1 copy.45
  21.8 2.1 collective-permute-done.6
  23.9 0.1 copy.46
  24.0 0.1 stack.35
  24.1 0.1 select_reduce_fusion
  24.2 3.7 fusion.19
  27.9 1.6 fusion.17.bias
  29.5 1.9 maximum_bitcast_fusion
  31.4 291.3 %forward_layer.1 = (bf16[8,256,2048]{2,1,0:T(8,128)(2,1)}, bf16[8,256,2048]{2,1,0:T(8,128)(2,1)}, bf16[2048,1024]{1,0:T(8,128)(2,1)}, bf16[2048,2048]{1,0:T(8,12...) custom-call(bf16[256,2048]{1,0:T(8,128)(2,1)} %bitcast.54, ...), custom_call_target="tpu_custom_call" | custom-call | tf_op jit(solution)/shard_map/forward_layer/pallas_call | solution.py:706
  322.7 398.6 %backward_layer.1 = (f32[256,2048]{1,0:T(8,128)}, bf16[3,256,2048]{2,1,0:T(8,128)(2,1)}, bf16[3,256,2048]{2,1,0:T(8,128)(2,1)}, bf16[16,128,1024]{2,1,0:T(8,128)...) custom-call(f32[256,2048]{1,0:T(8,128)} %get-tuple-element.48.resid,, ...), custom_call_target="tpu_custom_call" | custom-call | tf_op jit(solution)/shard_map/backward_layer/pallas_call | solution.py:1291
  721.3 0.0 copy-start.3
  721.3 3.3 slice_bitcast_fusion.1
  724.6 1.1 collective-permute-start.10
  725.6 2.6 collective-permute-start.9
  728.2 0.0 copy-done.3
  728.2 1.5 slice_bitcast_fusion.3
  729.7 0.0 collective-permute-start.7
  729.7 2.0 collective-permute-start.8
  731.7 12.2 %adam_chunk.1 = (f32[1,128,8192]{2,1,0:T(8,128)}, f32[1,128,8192]{2,1,0:T(8,128)}, bf16[128,8192]{1,0:T(8,128)(2,1)}) custom-call(bf16[2,8,128,1024]{3,2,1,0:T(8,128)(2,1)} %bitcast.65, f32[128,8192]{1,0:T(8,128)} %master.5, f32[1,128,8192]{2,1,0:T(8,128)} %first.3, f32[1,128,8192]{2,1,0:T(8,128)} %second.3), custom_call_target="tpu_custom_call" | custom-call | tf_op jit(solution)/shard_map/adam_chunk/pallas_call | solution.py:1427
  743.9 0.8 collective-permute-start.11
  744.7 16.3 %finish_chunk.2 = (f32[1,128,24576]{2,1,0:T(8,128)}, f32[1,128,24576]{2,1,0:T(8,128)}, f32[128,24576]{1,0:T(8,128)}, f32[128,24576]{1,0:T(8,128)}, f32[128,24576]{1,0:T(8,128)}) custom-call(bf16[2,8,128,1024]{3,2,1,0:T(8,128)(2,1)} %bitcast.61, f32[128,24576]{1,0:T(8,128)} %master.7, f32[1,128,24576]{2,1,0:T(8,128)} %first.5, f32[1,128,24576]{2,1,0:T(8,128)} %second.5, ...), custom_call_target="tpu_custom_call" | custom-call | tf_op jit(solution)/shard_map/finish_chunk/pallas_call | solution.py:1373
  761.0 0.0 copy-start.1
  761.0 32.4 %finish_chunk.3 = (f32[1,128,24576]{2,1,0:T(8,128)}, f32[1,128,24576]{2,1,0:T(8,128)}, f32[128,24576]{1,0:T(8,128)}, f32[128,24576]{1,0:T(8,128)}, f32[128,24576]{1,0:T(8,128)}) custom-call(bf16[2,8,128,2048]{3,2,1,0:T(8,128)(2,1)} %bitcast.55, f32[128,24576]{1,0:T(8,128)} %master.7, ...), custom_call_target="tpu_custom_call", output_to_operand_aliasing={{0}: (7, {}), {1}: (8, {}), {2}: (9, {}), {3}: (10, {}), {4... | custom-call | tf_op jit(solution)/shard_map/finish_chunk/pallas_call | solution.py:1373
  793.4 0.0 copy-start.2
  793.4 0.0 collective-permute-done.10
  793.4 0.0 collective-permute-done.9
  793.4 0.0 copy-done.1
  793.4 2.2 fusion.20
  795.6 0.0 copy-start.4
  795.6 0.0 collective-permute-done.7
  795.7 0.0 collective-permute-done.8
  795.7 0.0 copy-done.2
  795.7 3.7 fusion.18
  799.3 0.0 copy-done.4
  799.3 3.5 fusion.9
  802.9 0.0 collective-permute-done.11.other
  802.9 11.6 %outer_chunk.1 = (f32[128,8192]{1,0:T(8,128)}, f32[128,8192]{1,0:T(8,128)}, f32[128,8192]{1,0:T(8,128)}) custom-call(bf16[128,8192]{1,0:T(8,128)(2,1)} %get-tuple-element.64.diff, bf16[128,8192]{1,0:T(8,128)(2,1)} %collective-permute-done.11.other, f32[128,8192]{1,0:T(8,128)} %master.5, f32[128,8192]{1,0:T(8,128)} %momentum.1), custom_call_target="tpu_custom_call" | custom-call | tf_op jit(solution)/shard_map/outer_chunk/pallas_call | solution.py:1453
  (12 shorter events, 0.1 us)
Async XLA Ops:
  0.6 8.9 %copy-start = (bf16[1,256,2048]{2,1,0:T(8,128)(2,1)S(1)}, bf16[1,256,2048]{2,1,0:T(8,128)(2,1)}, u32[]{:S(2)}) copy-start(bf16[1,256,2048]{2,1,0:T(8,128)(2,1)} %param.11) | copy-start | bytes 3145732
  0.7 16.6 %collective-permute-start = (s32[1,2]{1,0:T(1,128)}, s32[1,2]{1,0:T(1,128)S(1)}, u32[]{:S(2)}, u32[]{:S(2)}) collective-permute-start(s32[1,2]{1,0:T(1,128)} %param.13), channel_id=1, source_target_pairs={{0,1},{1,0},{2,3},{3,2},{4,5},{5,4},{6,7},{7,6},{8,9},{9,8},{10,11... | collective-permute-start | bytes 32 | tf_op jit(solution)/shard_map/ppermute | solution.py:1495
  1.2 18.8 %collective-permute-start.1 = (s32[1,2]{1,0:T(1,128)}, s32[1,2]{1,0:T(1,128)S(1)}, u32[]{:S(2)}, u32[]{:S(2)}) collective-permute-start(s32[1,2]{1,0:T(1,128)} %param.13), channel_id=1, source_target_pairs={{0,2},{1,3},{2,0},{3,1},{4,6},{5,7},{6,4},{7,5},{8,10},{9,11},{10,... | collective-permute-start | bytes 32 | tf_op jit(solution)/shard_map/ppermute | solution.py:1495
  3.8 16.4 %collective-permute-start.2 = (s32[1,2]{1,0:T(1,128)}, s32[1,2]{1,0:T(1,128)S(1)}, u32[]{:S(2)}, u32[]{:S(2)}) collective-permute-start(s32[1,2]{1,0:T(1,128)} %param.13), channel_id=1, source_target_pairs={{0,3},{1,2},{2,1},{3,0},{4,7},{5,6},{6,5},{7,4},{8,11},{9,10},{10,... | collective-permute-start | bytes 32 | tf_op jit(solution)/shard_map/ppermute | solution.py:1495
  3.8 16.4 %collective-permute-start.3 = (s32[1,2]{1,0:T(1,128)}, s32[1,2]{1,0:T(1,128)S(1)}, u32[]{:S(2)}, u32[]{:S(2)}) collective-permute-start(s32[1,2]{1,0:T(1,128)} %param.13), channel_id=1, source_target_pairs={{0,4},{1,5},{2,6},{3,7},{4,0},{5,1},{6,2},{7,3},{8,12},{9,13},{10,... | collective-permute-start | bytes 32 | tf_op jit(solution)/shard_map/ppermute | solution.py:1495
  5.6 14.7 %collective-permute-start.4 = (s32[1,2]{1,0:T(1,128)}, s32[1,2]{1,0:T(1,128)S(1)}, u32[]{:S(2)}, u32[]{:S(2)}) collective-permute-start(s32[1,2]{1,0:T(1,128)} %param.13), channel_id=1, source_target_pairs={{0,5},{1,4},{2,7},{3,6},{4,1},{5,0},{6,3},{7,2},{8,13},{9,12},{10,... | collective-permute-start | bytes 32 | tf_op jit(solution)/shard_map/ppermute | solution.py:1495
  10.9 6.3 copy-start.5
  17.2 4.5 collective-permute-start.5
  20.0 3.9 collective-permute-start.6
  721.3 7.0 copy-start.3
  724.6 68.8 %collective-permute-start.10 = (bf16[256,2048]{1,0:T(8,128)(2,1)}, bf16[256,2048]{1,0:T(8,128)(2,1)S(1)}, u32[]{:S(2)}, u32[]{:S(2)}) collective-permute-start(bf16[256,2048]{1,0:T(8,128)(2,1)} %get-tuple-element.87), channel_id=1, source_target_pairs={{0,4},{1,5},{2,6},{3,7},{4,0},{5,1},{6,2},{7,3},{8,12},{9,13},{10,... | collective-permute-start | bytes 3145736 | tf_op jit(solution)/shard_map/ppermute | solution.py:1495
  725.6 67.8 %collective-permute-start.9 = (bf16[256,2048]{1,0:T(8,128)(2,1)}, bf16[256,2048]{1,0:T(8,128)(2,1)S(1)}, u32[]{:S(2)}, u32[]{:S(2)}) collective-permute-start(bf16[256,2048]{1,0:T(8,128)(2,1)} %get-tuple-element.86), channel_id=1, source_target_pairs={{0,2},{1,3},{2,0},{3,1},{4,6},{5,7},{6,4},{7,5},{8,10},{9,11},{10,... | collective-permute-start | bytes 3145736 | tf_op jit(solution)/shard_map/ppermute | solution.py:1495
  729.7 66.0 %collective-permute-start.7 = (bf16[256,2048]{1,0:T(8,128)(2,1)}, bf16[256,2048]{1,0:T(8,128)(2,1)}, u32[]{:S(2)}, u32[]{:S(2)}) collective-permute-start(bf16[256,2048]{1,0:T(8,128)(2,1)} %get-tuple-element.88), channel_id=1, source_target_pairs={{0,2},{1,3},{2,0},{3,1},{4,6},{5,7},{6,4},{7,5},{8,10},{9,11},{10,... | collective-permute-start | bytes 3145736 | tf_op jit(solution)/shard_map/ppermute | solution.py:1495
  729.7 66.0 %collective-permute-start.8 = (bf16[256,2048]{1,0:T(8,128)(2,1)}, bf16[256,2048]{1,0:T(8,128)(2,1)}, u32[]{:S(2)}, u32[]{:S(2)}) collective-permute-start(bf16[256,2048]{1,0:T(8,128)(2,1)} %get-tuple-element.89), channel_id=1, source_target_pairs={{0,4},{1,5},{2,6},{3,7},{4,0},{5,1},{6,2},{7,3},{8,12},{9,13},{10,... | collective-permute-start | bytes 3145736 | tf_op jit(solution)/shard_map/ppermute | solution.py:1495
  743.9 59.0 %collective-permute-start.11 = (bf16[128,8192]{1,0:T(8,128)(2,1)}, bf16[128,8192]{1,0:T(8,128)(2,1)}, u32[]{:S(2)}, u32[]{:S(2)}) collective-permute-start(bf16[128,8192]{1,0:T(8,128)(2,1)} %get-tuple-element.64.diff), channel_id=1, source_target_pairs={{0,16},{1,17},{2,18},{3,19},{4,20},{5,21},{6,22},{7,23},{8,24},{9,... | collective-permute-start | bytes 6291464 | tf_op jit(solution)/shard_map/ppermute | solution.py:1499
  761.0 32.4 %copy-start.1 = (bf16[1,256,2048]{2,1,0:T(8,128)(2,1)S(1)}, bf16[1,256,2048]{2,1,0:T(8,128)(2,1)}, u32[]{:S(2)}) copy-start(bf16[1,256,2048]{2,1,0:T(8,128)(2,1)} %param.11) | copy-start | bytes 3145732
  793.4 2.3 copy-start.2
  795.6 3.7 copy-start.4

commit v4 on v3

--- a/solution.py
+++ b/solution.py
@@ -107,7 +107,7 @@
 GATE_AHEAD, GATE_MIDDLE = 7, 3
 DOWN_EARLY = 15
 FEED_EARLY = 6
-SPLIT_TOKENS, SPLIT_ATTENDED, SPLIT_NORMED, SPLIT_COT, SPLIT_BACK = 3, 3, 3, 2, 3
+SPLIT_TOKENS, SPLIT_ATTENDED, SPLIT_NORMED, SPLIT_COT, SPLIT_BACK = 3, 3, 2, 2, 3
 STRIP = 16
 GATHER_COPIES = 6 * PIECES + 1
 VMEM_BYTES = 60 * 1024 * 1024

time: 817 us -> 812 us (level)
  no operation moved by 1% of the time
where the time goes in v4:
time: 812 us; the launch traced here: 810 us
  Pallas kernels  763 us (94%)
  other arithmetic  21.4 us (3%)
  starting transfers between devices  15 us (2%)
    pallas_call x1, Pallas kernels, backward_layer(): pl.pallas_call(functools.partial(backward_kernel, ranks), out_shape=[shap...  399 us
    pallas_call x1, Pallas kernels, forward_layer(): pl.pallas_call(functools.partial(forward_kernel, ranks), out_shape=[shape...  286 us
    pallas_call x2, Pallas kernels, finish_chunk(): pl.pallas_call(functools.partial(finish_kernel, reps, share), grid=(parts...  48.7 us
  transfers between devices with their start and end apart: 12, of which 2 were waited for; matrix products, arithmetic and copies ran while one was open for 2% of the time, Pallas kernels for 8%

profile of v4, /device:TPU:0, one launch (start us, length us, event | category | flops | bytes accessed | tf_op | source)
XLA Modules:
  0.0 810.1 jit_solution(2720270369509571106)
XLA Ops:
  0.6 0.0 copy-start
  0.7 0.5 collective-permute-start
  1.2 2.6 collective-permute-start.1
  3.8 0.1 collective-permute-start.2
  3.8 1.8 collective-permute-start.3
  5.6 0.0 collective-permute-start.4
  5.7 0.8 copy.39
  6.5 1.4 convert_reduce_fusion
  7.9 1.6 fusion.10
  9.6 0.0 copy-done
  9.6 1.3 fusion.4.normed_own
  10.9 6.1 pack_shares.1.att_pack
  17.0 0.2 compare_and_fusion
  17.2 0.0 collective-permute-done
  17.2 0.0 copy-done.5
  17.2 2.7 collective-permute-start.5
  19.9 0.1 copy.40
  20.0 0.0 collective-permute-done.1
  20.0 0.1 collective-permute-start.6
  20.1 0.1 copy.41
  20.2 0.0 collective-permute-done.2
  20.2 0.1 copy.42
  20.3 0.0 collective-permute-done.3
  20.3 0.1 copy.43
  20.4 0.0 collective-permute-done.4
  20.4 0.1 copy.44
  20.5 1.3 collective-permute-done.5
  21.7 0.1 copy.45
  21.8 2.1 collective-permute-done.6
  23.9 0.1 copy.46
  24.0 0.1 stack.35
  24.1 0.1 select_reduce_fusion
  24.2 3.7 fusion.19
  27.9 1.6 fusion.17.bias
  29.5 1.9 maximum_bitcast_fusion
  31.4 285.7 %forward_layer.1 = (bf16[8,256,2048]{2,1,0:T(8,128)(2,1)}, bf16[8,256,2048]{2,1,0:T(8,128)(2,1)}, bf16[2048,1024]{1,0:T(8,128)(2,1)}, bf16[2048,2048]{1,0:T(8,12...) custom-call(bf16[256,2048]{1,0:T(8,128)(2,1)} %bitcast.54, ...), custom_call_target="tpu_custom_call" | custom-call | tf_op jit(solution)/shard_map/forward_layer/pallas_call | solution.py:706
  317.1 399.1 %backward_layer.1 = (f32[256,2048]{1,0:T(8,128)}, bf16[3,256,2048]{2,1,0:T(8,128)(2,1)}, bf16[3,256,2048]{2,1,0:T(8,128)(2,1)}, bf16[16,128,1024]{2,1,0:T(8,128)...) custom-call(f32[256,2048]{1,0:T(8,128)} %get-tuple-element.48.resid,, ...), custom_call_target="tpu_custom_call" | custom-call | tf_op jit(solution)/shard_map/backward_layer/pallas_call | solution.py:1291
  716.2 0.0 copy-start.3
  716.2 3.3 slice_bitcast_fusion.1
  719.4 3.1 collective-permute-start.10
  722.5 2.5 collective-permute-start.9
  725.0 0.0 copy-done.3
  725.0 1.5 slice_bitcast_fusion.3
  726.5 0.0 collective-permute-start.7
  726.5 0.0 collective-permute-start.8
  726.5 12.2 %adam_chunk.1 = (f32[1,128,8192]{2,1,0:T(8,128)}, f32[1,128,8192]{2,1,0:T(8,128)}, bf16[128,8192]{1,0:T(8,128)(2,1)}) custom-call(bf16[2,8,128,1024]{3,2,1,0:T(8,128)(2,1)} %bitcast.65, f32[128,8192]{1,0:T(8,128)} %master.5, f32[1,128,8192]{2,1,0:T(8,128)} %first.3, f32[1,128,8192]{2,1,0:T(8,128)} %second.3), custom_call_target="tpu_custom_call" | custom-call | tf_op jit(solution)/shard_map/adam_chunk/pallas_call | solution.py:1427
  738.7 1.7 collective-permute-start.11
  740.4 16.3 %finish_chunk.2 = (f32[1,128,24576]{2,1,0:T(8,128)}, f32[1,128,24576]{2,1,0:T(8,128)}, f32[128,24576]{1,0:T(8,128)}, f32[128,24576]{1,0:T(8,128)}, f32[128,24576]{1,0:T(8,128)}) custom-call(bf16[2,8,128,1024]{3,2,1,0:T(8,128)(2,1)} %bitcast.61, f32[128,24576]{1,0:T(8,128)} %master.7, f32[1,128,24576]{2,1,0:T(8,128)} %first.5, f32[1,128,24576]{2,1,0:T(8,128)} %second.5, ...), custom_call_target="tpu_custom_call" | custom-call | tf_op jit(solution)/shard_map/finish_chunk/pallas_call | solution.py:1373
  756.7 0.0 copy-start.1
  756.7 32.4 %finish_chunk.3 = (f32[1,128,24576]{2,1,0:T(8,128)}, f32[1,128,24576]{2,1,0:T(8,128)}, f32[128,24576]{1,0:T(8,128)}, f32[128,24576]{1,0:T(8,128)}, f32[128,24576]{1,0:T(8,128)}) custom-call(bf16[2,8,128,2048]{3,2,1,0:T(8,128)(2,1)} %bitcast.55, f32[128,24576]{1,0:T(8,128)} %master.7, ...), custom_call_target="tpu_custom_call", output_to_operand_aliasing={{0}: (7, {}), {1}: (8, {}), {2}: (9, {}), {3}: (10, {}), {4... | custom-call | tf_op jit(solution)/shard_map/finish_chunk/pallas_call | solution.py:1373
  789.0 0.0 copy-start.2
  789.1 0.0 collective-permute-done.10
  789.1 0.0 collective-permute-done.9
  789.1 0.0 copy-done.1
  789.1 2.2 fusion.20
  791.3 0.0 copy-start.4
  791.3 0.0 collective-permute-done.7
  791.3 0.0 collective-permute-done.8
  791.3 0.0 copy-done.2
  791.3 3.7 fusion.18
  795.0 0.0 copy-done.4
  795.0 3.5 fusion.9
  798.6 0.0 collective-permute-done.11.other
  798.6 11.6 %outer_chunk.1 = (f32[128,8192]{1,0:T(8,128)}, f32[128,8192]{1,0:T(8,128)}, f32[128,8192]{1,0:T(8,128)}) custom-call(bf16[128,8192]{1,0:T(8,128)(2,1)} %get-tuple-element.64.diff, bf16[128,8192]{1,0:T(8,128)(2,1)} %collective-permute-done.11.other, f32[128,8192]{1,0:T(8,128)} %master.5, f32[128,8192]{1,0:T(8,128)} %momentum.1), custom_call_target="tpu_custom_call" | custom-call | tf_op jit(solution)/shard_map/outer_chunk/pallas_call | solution.py:1453
  (12 shorter events, 0.1 us)
Async XLA Ops:
  0.6 8.9 %copy-start = (bf16[1,256,2048]{2,1,0:T(8,128)(2,1)S(1)}, bf16[1,256,2048]{2,1,0:T(8,128)(2,1)}, u32[]{:S(2)}) copy-start(bf16[1,256,2048]{2,1,0:T(8,128)(2,1)} %param.11) | copy-start | bytes 3145732
  0.7 16.6 %collective-permute-start = (s32[1,2]{1,0:T(1,128)}, s32[1,2]{1,0:T(1,128)S(1)}, u32[]{:S(2)}, u32[]{:S(2)}) collective-permute-start(s32[1,2]{1,0:T(1,128)} %param.13), channel_id=1, source_target_pairs={{0,1},{1,0},{2,3},{3,2},{4,5},{5,4},{6,7},{7,6},{8,9},{9,8},{10,11... | collective-permute-start | bytes 32 | tf_op jit(solution)/shard_map/ppermute | solution.py:1495
  1.2 18.8 %collective-permute-start.1 = (s32[1,2]{1,0:T(1,128)}, s32[1,2]{1,0:T(1,128)S(1)}, u32[]{:S(2)}, u32[]{:S(2)}) collective-permute-start(s32[1,2]{1,0:T(1,128)} %param.13), channel_id=1, source_target_pairs={{0,2},{1,3},{2,0},{3,1},{4,6},{5,7},{6,4},{7,5},{8,10},{9,11},{10,... | collective-permute-start | bytes 32 | tf_op jit(solution)/shard_map/ppermute | solution.py:1495
  3.8 16.4 %collective-permute-start.2 = (s32[1,2]{1,0:T(1,128)}, s32[1,2]{1,0:T(1,128)S(1)}, u32[]{:S(2)}, u32[]{:S(2)}) collective-permute-start(s32[1,2]{1,0:T(1,128)} %param.13), channel_id=1, source_target_pairs={{0,3},{1,2},{2,1},{3,0},{4,7},{5,6},{6,5},{7,4},{8,11},{9,10},{10,... | collective-permute-start | bytes 32 | tf_op jit(solution)/shard_map/ppermute | solution.py:1495
  3.8 16.4 %collective-permute-start.3 = (s32[1,2]{1,0:T(1,128)}, s32[1,2]{1,0:T(1,128)S(1)}, u32[]{:S(2)}, u32[]{:S(2)}) collective-permute-start(s32[1,2]{1,0:T(1,128)} %param.13), channel_id=1, source_target_pairs={{0,4},{1,5},{2,6},{3,7},{4,0},{5,1},{6,2},{7,3},{8,12},{9,13},{10,... | collective-permute-start | bytes 32 | tf_op jit(solution)/shard_map/ppermute | solution.py:1495
  5.6 14.7 %collective-permute-start.4 = (s32[1,2]{1,0:T(1,128)}, s32[1,2]{1,0:T(1,128)S(1)}, u32[]{:S(2)}, u32[]{:S(2)}) collective-permute-start(s32[1,2]{1,0:T(1,128)} %param.13), channel_id=1, source_target_pairs={{0,5},{1,4},{2,7},{3,6},{4,1},{5,0},{6,3},{7,2},{8,13},{9,12},{10,... | collective-permute-start | bytes 32 | tf_op jit(solution)/shard_map/ppermute | solution.py:1495
  10.9 6.3 copy-start.5
  17.2 4.5 collective-permute-start.5
  20.0 3.9 collective-permute-start.6
  716.2 8.8 %copy-start.3 = (bf16[3,256,2048]{2,1,0:T(8,128)(2,1)S(1)}, bf16[3,256,2048]{2,1,0:T(8,128)(2,1)}, u32[]{:S(2)}) copy-start(bf16[3,256,2048]{2,1,0:T(8,128)(2,1)} %get-tuple-element.60) | copy-start | bytes 9437188
  719.4 69.6 %collective-permute-start.10 = (bf16[256,2048]{1,0:T(8,128)(2,1)}, bf16[256,2048]{1,0:T(8,128)(2,1)S(1)}, u32[]{:S(2)}, u32[]{:S(2)}) collective-permute-start(bf16[256,2048]{1,0:T(8,128)(2,1)} %get-tuple-element.87), channel_id=1, source_target_pairs={{0,4},{1,5},{2,6},{3,7},{4,0},{5,1},{6,2},{7,3},{8,12},{9,13},{10,... | collective-permute-start | bytes 3145736 | tf_op jit(solution)/shard_map/ppermute | solution.py:1495
  722.5 66.5 %collective-permute-start.9 = (bf16[256,2048]{1,0:T(8,128)(2,1)}, bf16[256,2048]{1,0:T(8,128)(2,1)S(1)}, u32[]{:S(2)}, u32[]{:S(2)}) collective-permute-start(bf16[256,2048]{1,0:T(8,128)(2,1)} %get-tuple-element.86), channel_id=1, source_target_pairs={{0,2},{1,3},{2,0},{3,1},{4,6},{5,7},{6,4},{7,5},{8,10},{9,11},{10,... | collective-permute-start | bytes 3145736 | tf_op jit(solution)/shard_map/ppermute | solution.py:1495
  726.5 64.8 %collective-permute-start.7 = (bf16[256,2048]{1,0:T(8,128)(2,1)}, bf16[256,2048]{1,0:T(8,128)(2,1)}, u32[]{:S(2)}, u32[]{:S(2)}) collective-permute-start(bf16[256,2048]{1,0:T(8,128)(2,1)} %get-tuple-element.88), channel_id=1, source_target_pairs={{0,2},{1,3},{2,0},{3,1},{4,6},{5,7},{6,4},{7,5},{8,10},{9,11},{10,... | collective-permute-start | bytes 3145736 | tf_op jit(solution)/shard_map/ppermute | solution.py:1495
  726.5 64.9 %collective-permute-start.8 = (bf16[256,2048]{1,0:T(8,128)(2,1)}, bf16[256,2048]{1,0:T(8,128)(2,1)}, u32[]{:S(2)}, u32[]{:S(2)}) collective-permute-start(bf16[256,2048]{1,0:T(8,128)(2,1)} %get-tuple-element.89), channel_id=1, source_target_pairs={{0,4},{1,5},{2,6},{3,7},{4,0},{5,1},{6,2},{7,3},{8,12},{9,13},{10,... | collective-permute-start | bytes 3145736 | tf_op jit(solution)/shard_map/ppermute | solution.py:1495
  738.7 59.9 %collective-permute-start.11 = (bf16[128,8192]{1,0:T(8,128)(2,1)}, bf16[128,8192]{1,0:T(8,128)(2,1)}, u32[]{:S(2)}, u32[]{:S(2)}) collective-permute-start(bf16[128,8192]{1,0:T(8,128)(2,1)} %get-tuple-element.64.diff), channel_id=1, source_target_pairs={{0,16},{1,17},{2,18},{3,19},{4,20},{5,21},{6,22},{7,23},{8,24},{9,... | collective-permute-start | bytes 6291464 | tf_op jit(solution)/shard_map/ppermute | solution.py:1499
  756.7 32.4 %copy-start.1 = (bf16[1,256,2048]{2,1,0:T(8,128)(2,1)S(1)}, bf16[1,256,2048]{2,1,0:T(8,128)(2,1)}, u32[]{:S(2)}) copy-start(bf16[1,256,2048]{2,1,0:T(8,128)(2,1)} %param.11) | copy-start | bytes 3145732
  789.0 2.3 copy-start.2
  791.3 3.7 copy-start.4
